TPU v7x, 32 devices: a whole 2x2x4 slice. The times are simulated.
32 devices in a mesh: fsdp: 16 (over z, y, x), tp: 2 (over core).
Axes of the slice: x: 2, y: 2, z: 4, core: 2. Of those that a mesh axis runs over, the one named last changes fastest.
Arguments:
- tokens_in: bfloat16 [4096, 2560], P(('fsdp', 'tp')), may hold values from -6 to 6
- cotangent: bfloat16 [4096, 2560], P(('fsdp', 'tp')), may hold values from -6 to 6
- doc_ids: int32 [4096], P('fsdp'), may hold values from 0 to 2, as said below
- routes: int32 [4096, 6], P('fsdp'), may hold values from 0 to 15, all different within a row; in each aligned block of 256 rows (0 to 255, 256 to 511, ...) at most 128 rows name the same one
- gain_attn: bfloat16 [2560], P('fsdp'), may hold values from 0.5 to 1.5
- w_query: bfloat16 [2560, 2560], P('fsdp', 'tp'), may hold values from -0.125 to 0.125
- w_key: bfloat16 [2560, 512], P('fsdp', 'tp'), may hold values from -0.125 to 0.125
- w_value: bfloat16 [2560, 512], P('fsdp', 'tp'), may hold values from -0.125 to 0.125
- w_out: bfloat16 [2560, 2560], P('tp', 'fsdp'), may hold values from -0.625 to 0.625
- gain_ffn: bfloat16 [2560], P('fsdp'), may hold values from 0.5 to 1.5
- w_router: bfloat16 [2560, 16], P('fsdp'), may hold values from -0.0625 to 0.0625
- w_shared_gate: bfloat16 [2560, 3072], P('fsdp', 'tp'), may hold values from -0.125 to 0.125
- w_shared_up: bfloat16 [2560, 3072], P('fsdp', 'tp'), may hold values from -0.125 to 0.125
- w_shared_down: bfloat16 [3072, 2560], P('tp', 'fsdp'), may hold values from -0.109375 to 0.109375
- w_expert_gate: bfloat16 [16, 2560, 1536], P('fsdp', None, 'tp'), may hold values from -0.125 to 0.125
- w_expert_up: bfloat16 [16, 2560, 1536], P('fsdp', None, 'tp'), may hold values from -0.125 to 0.125
- w_expert_down: bfloat16 [16, 1536, 2560], P('fsdp', 'tp'), may hold values from -0.3125 to 0.3125
Outputs:
- block_out: bfloat16 [4096, 2560], P(('fsdp', 'tp'))
- grad_tokens: float32 [4096, 2560], P(('fsdp', 'tp'))
- grad_gain_attn: float32 [2560], P('fsdp')
- grad_query: float32 [2560, 2560], P('fsdp', 'tp')
- grad_key: float32 [2560, 512], P('fsdp', 'tp')
- grad_value: float32 [2560, 512], P('fsdp', 'tp')
- grad_out: float32 [2560, 2560], P('tp', 'fsdp')
- grad_gain_ffn: float32 [2560], P('fsdp')
- grad_router: float32 [2560, 16], P('fsdp')
- grad_shared_gate: float32 [2560, 3072], P('fsdp', 'tp')
- grad_shared_up: float32 [2560, 3072], P('fsdp', 'tp')
- grad_shared_down: float32 [3072, 2560], P('tp', 'fsdp')
- grad_expert_gate: float32 [16, 2560, 1536], P('fsdp', None, 'tp')
- grad_expert_up: float32 [16, 2560, 1536], P('fsdp', None, 'tp')
- grad_expert_down: float32 [16, 1536, 2560], P('fsdp', 'tp')
Inputs may be any that keep to these rules, and one draw needn't show every extreme that they name: `doc_ids`: each sequence's tokens are numbered 0, 1, 2 by document, never falling; every number occurs. `routes`: among the 256 tokens of one sequence no expert is named more than 128 times, a bound that some block reaches.
All inputs are finite; a program needn't handle non-finite values.
Results may differ from a plain program's by a relative error of at most 0.017.
Values may be sent and summed in bfloat16 or wider, within the bound.
No kernel may reach another device: no remote copies, remote signals or barrier semaphores. Data moves between devices by JAX's collectives and lax.ppermute only.
A program may use at most 320 MiB of HBM per device.

v0:
```python
import jax
import jax.numpy as jnp
from jax import lax
from jax.sharding import PartitionSpec as P

QUERY_HEADS = 20
KEY_VALUE_HEADS = 4
HEAD_SIZE = 128
TOPK = 6


norm_eps = 1e-05
rope_base = 500000.0


def rotary_tables(length_total):
    half_width = HEAD_SIZE // 2
    inverse = 1.0 / rope_base ** (jnp.arange(half_width, dtype=jnp.float32) * (2.0 / HEAD_SIZE))
    angles = jnp.arange(length_total, dtype=jnp.float32)[:, None] * inverse[None, :]
    return (jnp.cos(angles), jnp.sin(angles))


def apply_rotary(values, rotary_cosine, rotary_sine):
    half_width = values.shape[-1] // 2
    first_half = values[..., :half_width]
    second_half = values[..., half_width:]
    cos_rows = rotary_cosine[:, None, :]
    sin_rows = rotary_sine[:, None, :]
    return jnp.concatenate(
        [
            first_half * cos_rows - second_half * sin_rows,
            second_half * cos_rows + first_half * sin_rows,
        ],
        axis=-1,
    )


def smooth_gate(values):
    return values / (1.0 + jnp.exp(-values))


def smooth_slope(values):
    sigmoid = 1.0 / (1.0 + jnp.exp(-values))
    return sigmoid * (1.0 + values * (1.0 - sigmoid))


def rms_scale(values):
    return lax.rsqrt(jnp.mean(values * values, axis=-1, keepdims=True) + norm_eps)


def norm_back(grad_in, normed, inv_rms, gain_vec):
    scaled = grad_in * gain_vec
    return inv_rms * (scaled - normed * jnp.mean(scaled * normed, axis=-1, keepdims=True))


def product(left_mat, right_mat):
    return jnp.dot(left_mat, right_mat, preferred_element_type=jnp.float32)


def times_transposed(left_mat, right_mat):
    return lax.dot_general(
        left_mat, right_mat, (((1,), (1,)), ((), ())), preferred_element_type=jnp.float32
    )


def transposed_times(left_mat, right_mat):
    return lax.dot_general(
        left_mat, right_mat, (((0,), (0,)), ((), ())), preferred_element_type=jnp.float32
    )


def attention_scores(query_rot, rotated_key, allowed):
    scores = jnp.einsum(
        "qgjd,kgd->gjqk", query_rot, rotated_key, preferred_element_type=jnp.float32
    ) * HEAD_SIZE ** (-0.5)
    return jnp.where(allowed, scores, -1e30)


def shards(
    tokens_in,
    cotangent,
    doc_ids,
    routes,
    gain_attn,
    w_query,
    w_key,
    w_value,
    w_out,
    gain_ffn,
    w_router,
    w_shared_gate,
    w_shared_up,
    w_shared_down,
    w_expert_gate,
    w_expert_up,
    w_expert_down,
):
    own_rows = tokens_in.shape[0]
    seq_rows = doc_ids.shape[0]
    model_width = tokens_in.shape[1]
    experts = w_router.shape[1]
    local_experts = w_expert_gate.shape[0]
    sources = experts // local_experts
    capacity = max(2, 4 * seq_rows * TOPK // (3 * experts))
    position = lax.axis_index("tp")
    gathered = (
        lax.all_gather(w_query, "fsdp", axis=0, tiled=True),
        lax.all_gather(w_key, "fsdp", axis=0, tiled=True),
        lax.all_gather(w_value, "fsdp", axis=0, tiled=True),
        lax.all_gather(w_out, "fsdp", axis=1, tiled=True),
        lax.all_gather(w_shared_gate, "fsdp", axis=0, tiled=True),
        lax.all_gather(w_shared_up, "fsdp", axis=0, tiled=True),
        lax.all_gather(w_shared_down, "fsdp", axis=1, tiled=True),
        lax.all_gather(w_router, "fsdp", axis=0, tiled=True),
        lax.all_gather(gain_attn, "fsdp", axis=0, tiled=True),
        lax.all_gather(gain_ffn, "fsdp", axis=0, tiled=True),
    )
    (
        full_query,
        full_key,
        full_value,
        full_out,
        full_sgate,
        full_sup,
        full_sdown,
        full_router,
        gain_one_low,
        gain_two_low,
    ) = gathered
    first_norm_gain = gain_one_low.astype(jnp.float32)
    second_norm_gain = gain_two_low.astype(jnp.float32)
    group_tokens, group_cot = (
        lax.all_gather(tokens_in, "tp", axis=0, tiled=True),
        lax.all_gather(cotangent, "tp", axis=0, tiled=True),
    )
    residual = group_tokens.astype(jnp.float32)
    upstream = group_cot.astype(jnp.float32)
    scale_one = rms_scale(residual)
    normed_one = residual * scale_one
    attn_input = (normed_one * first_norm_gain).astype(jnp.bfloat16)
    heads_local = full_query.shape[1] // HEAD_SIZE
    kv_local = full_key.shape[1] // HEAD_SIZE
    tokens_per_group = QUERY_HEADS // KEY_VALUE_HEADS
    rotary_cosine, rotary_sine = rotary_tables(seq_rows)
    query_rot = (
        apply_rotary(
            product(attn_input, full_query).reshape(seq_rows, heads_local, HEAD_SIZE),
            rotary_cosine,
            rotary_sine,
        )
        .astype(jnp.bfloat16)
        .reshape(seq_rows, kv_local, tokens_per_group, HEAD_SIZE)
    )
    rotated_key = apply_rotary(
        product(attn_input, full_key).reshape(seq_rows, kv_local, HEAD_SIZE),
        rotary_cosine,
        rotary_sine,
    ).astype(jnp.bfloat16)
    value_low = (
        product(attn_input, full_value).astype(jnp.bfloat16).reshape(seq_rows, kv_local, HEAD_SIZE)
    )
    order_ids = jnp.arange(seq_rows)
    allowed = (doc_ids[:, None] == doc_ids[None, :]) & (order_ids[:, None] >= order_ids[None, :])
    scores = attention_scores(query_rot, rotated_key, allowed)
    top_score = jnp.max(scores, axis=-1, keepdims=True)
    weights = jnp.exp(scores - top_score)
    weight_sum = jnp.sum(weights, axis=-1, keepdims=True)
    log_total = top_score + jnp.log(weight_sum)
    probs_low = (weights / weight_sum).astype(jnp.bfloat16)
    heads_out = (
        jnp.einsum("gjqk,kgd->qgjd", probs_low, value_low, preferred_element_type=jnp.float32)
        .astype(jnp.bfloat16)
        .reshape(seq_rows, heads_local * HEAD_SIZE)
    )
    attn_branch = lax.psum(product(heads_out, full_out), "tp")
    middle = residual + attn_branch
    scale_two = rms_scale(middle)
    normed_two = middle * scale_two
    ffn_input = (normed_two * second_norm_gain).astype(jnp.bfloat16)
    logits = product(ffn_input, full_router)
    chosen = routes[:, :, None] == jnp.arange(experts, dtype=jnp.int32)[None, None, :]
    picked = jnp.sum(jnp.where(chosen, logits[:, None, :], 0.0), axis=-1)
    top_pick = jnp.max(picked, axis=-1, keepdims=True)
    gate_exp = jnp.exp(picked - top_pick)
    gate_values = gate_exp / jnp.sum(gate_exp, axis=-1, keepdims=True)
    shared_gate = product(ffn_input, full_sgate)
    shared_up = product(ffn_input, full_sup)
    shared_act = smooth_gate(shared_gate)
    shared_hidden = (shared_act * shared_up).astype(jnp.bfloat16)
    ffn_part = product(shared_hidden, full_sdown)
    flat_routes = routes.reshape(-1)
    onehot = (flat_routes[:, None] == jnp.arange(experts, dtype=jnp.int32)[None, :]).astype(
        jnp.int32
    )
    earlier = jnp.cumsum(onehot, axis=0) - onehot
    target = flat_routes * capacity + jnp.sum(earlier * onehot, axis=1)
    source = (
        jnp.full((experts * capacity,), -1, jnp.int32)
        .at[target]
        .set(jnp.arange(seq_rows * TOPK, dtype=jnp.int32))
    )
    filled = (source >= 0)[:, None]
    safe_source = jnp.maximum(source, 0)
    zero_low = jnp.zeros((), jnp.bfloat16)
    send_rows = jnp.where(filled, ffn_input[safe_source // TOPK], zero_low).reshape(
        experts, capacity, model_width
    )
    gated_cot = (
        (gate_values[:, :, None] * upstream[:, None, :])
        .astype(jnp.bfloat16)
        .reshape(seq_rows * TOPK, model_width)
    )
    send_grads = jnp.where(filled, gated_cot[safe_source], zero_low).reshape(
        experts, capacity, model_width
    )
    arrived = lax.all_to_all(send_rows, "fsdp", split_axis=0, concat_axis=0, tiled=True)
    slot_count = arrived.shape[1]
    grouped = arrived.reshape(sources, local_experts, slot_count, model_width)
    gate_pre = jnp.einsum(
        "sjcd,jdf->sjcf", grouped, w_expert_gate, preferred_element_type=jnp.float32
    )
    up_pre = jnp.einsum("sjcd,jdf->sjcf", grouped, w_expert_up, preferred_element_type=jnp.float32)
    hidden = (smooth_gate(gate_pre) * up_pre).astype(jnp.bfloat16)
    result = jnp.einsum(
        "sjcf,jfd->sjcd", hidden, w_expert_down, preferred_element_type=jnp.float32
    ).astype(jnp.bfloat16)
    half_width = gate_pre.shape[-1]
    expert_out = result.reshape(experts, slot_count, model_width)
    gate_keep = gate_pre.reshape(experts, slot_count, half_width)
    up_keep = up_pre.reshape(experts, slot_count, half_width)
    returned = lax.all_to_all(expert_out, "fsdp", split_axis=0, concat_axis=0, tiled=True)
    picked_rows = (
        returned.reshape(experts * capacity, model_width)[target]
        .reshape(seq_rows, TOPK, model_width)
        .astype(jnp.float32)
    )
    ffn_part = ffn_part + jnp.sum(gate_values[:, :, None] * picked_rows, axis=1)
    ffn_sum = lax.psum_scatter(
        ffn_part.astype(jnp.bfloat16), "tp", scatter_dimension=0, tiled=True
    ).astype(jnp.float32)
    middle_own = lax.dynamic_slice_in_dim(middle, position * own_rows, own_rows, 0)
    block_out = (middle_own + ffn_sum).astype(jnp.bfloat16)
    gate_grad = lax.psum(jnp.sum(upstream[:, None, :] * picked_rows, axis=-1), "tp")
    arrived_grads = lax.all_to_all(send_grads, "fsdp", split_axis=0, concat_axis=0, tiled=True)
    half_width = gate_keep.shape[-1]
    grad_rows = arrived_grads.reshape(sources, local_experts, capacity, model_width)
    input_rows = arrived.reshape(sources, local_experts, capacity, model_width)
    gate_pre = gate_keep.reshape(sources, local_experts, capacity, half_width)
    up_pre = up_keep.reshape(sources, local_experts, capacity, half_width)
    expert_act = smooth_gate(gate_pre)
    expert_hidden = (expert_act * up_pre).astype(jnp.bfloat16)
    hidden_grad = jnp.einsum(
        "sjcd,jfd->sjcf", grad_rows, w_expert_down, preferred_element_type=jnp.float32
    )
    grad_expert_down = jnp.einsum(
        "sjcf,sjcd->jfd", expert_hidden, grad_rows, preferred_element_type=jnp.float32
    )
    gate_low = (hidden_grad * up_pre * smooth_slope(gate_pre)).astype(jnp.bfloat16)
    up_low = (hidden_grad * expert_act).astype(jnp.bfloat16)
    grad_expert_gate = jnp.einsum(
        "sjcd,sjcf->jdf", input_rows, gate_low, preferred_element_type=jnp.float32
    )
    grad_expert_up = jnp.einsum(
        "sjcd,sjcf->jdf", input_rows, up_low, preferred_element_type=jnp.float32
    )
    row_grads = jnp.einsum(
        "sjcf,jdf->sjcd", gate_low, w_expert_gate, preferred_element_type=jnp.float32
    ) + jnp.einsum("sjcf,jdf->sjcd", up_low, w_expert_up, preferred_element_type=jnp.float32)
    row_grads = row_grads.astype(jnp.bfloat16).reshape(experts, capacity, model_width)
    back_rows = lax.all_to_all(row_grads, "fsdp", split_axis=0, concat_axis=0, tiled=True)
    input_grad = jnp.sum(
        back_rows.reshape(experts * capacity, model_width)[target]
        .reshape(seq_rows, TOPK, model_width)
        .astype(jnp.float32),
        axis=1,
    )
    shared_hidden_grad = times_transposed(group_cot, full_sdown)
    grad_shared_down = transposed_times(shared_hidden, group_cot)
    sgate_low = (shared_hidden_grad * shared_up * smooth_slope(shared_gate)).astype(jnp.bfloat16)
    sup_low = (shared_hidden_grad * shared_act).astype(jnp.bfloat16)
    grad_shared_gate = transposed_times(ffn_input, sgate_low)
    grad_shared_up = transposed_times(ffn_input, sup_low)
    input_grad = (
        input_grad + times_transposed(sgate_low, full_sgate) + times_transposed(sup_low, full_sup)
    )
    input_grad = lax.psum(input_grad, "tp")
    pick_grad = gate_values * (gate_grad - jnp.sum(gate_values * gate_grad, axis=-1, keepdims=True))
    logit_low = jnp.sum(jnp.where(chosen, pick_grad[:, :, None], 0.0), axis=1).astype(jnp.bfloat16)
    grad_router = transposed_times(ffn_input, logit_low)
    input_grad = input_grad + times_transposed(logit_low, full_router)
    grad_gain_ffn = jnp.sum(input_grad * normed_two, axis=0)
    middle_grad = upstream + norm_back(input_grad, normed_two, scale_two, second_norm_gain)
    attn_grad_low = middle_grad.astype(jnp.bfloat16)
    grad_out = transposed_times(heads_out, attn_grad_low)
    heads_grad = (
        times_transposed(attn_grad_low, full_out)
        .astype(jnp.bfloat16)
        .reshape(seq_rows, kv_local, tokens_per_group, HEAD_SIZE)
    )
    again_scores = attention_scores(query_rot, rotated_key, allowed)
    attn_probs = jnp.exp(again_scores - log_total)
    probs_grad = jnp.einsum(
        "qgjd,kgd->gjqk", heads_grad, value_low, preferred_element_type=jnp.float32
    )
    value_grad = (
        jnp.einsum(
            "gjqk,qgjd->kgd",
            attn_probs.astype(jnp.bfloat16),
            heads_grad,
            preferred_element_type=jnp.float32,
        )
        .astype(jnp.bfloat16)
        .reshape(seq_rows, kv_local * HEAD_SIZE)
    )
    score_low = (
        attn_probs * (probs_grad - jnp.sum(attn_probs * probs_grad, axis=-1, keepdims=True))
    ).astype(jnp.bfloat16)
    query_grad = jnp.einsum(
        "gjqk,kgd->qgjd", score_low, rotated_key, preferred_element_type=jnp.float32
    ) * HEAD_SIZE ** (-0.5)
    key_grad = jnp.einsum(
        "gjqk,qgjd->kgd", score_low, query_rot, preferred_element_type=jnp.float32
    ) * HEAD_SIZE ** (-0.5)
    query_low = (
        apply_rotary(
            query_grad.reshape(seq_rows, heads_local, HEAD_SIZE), rotary_cosine, -rotary_sine
        )
        .astype(jnp.bfloat16)
        .reshape(seq_rows, heads_local * HEAD_SIZE)
    )
    key_low = (
        apply_rotary(key_grad, rotary_cosine, -rotary_sine)
        .astype(jnp.bfloat16)
        .reshape(seq_rows, kv_local * HEAD_SIZE)
    )
    grad_query = transposed_times(attn_input, query_low)
    grad_key = transposed_times(attn_input, key_low)
    grad_value = transposed_times(attn_input, value_grad)
    attn_in_grad = (
        times_transposed(query_low, full_query)
        + times_transposed(key_low, full_key)
        + times_transposed(value_grad, full_value)
    )
    attn_in_grad = lax.psum(attn_in_grad.astype(jnp.bfloat16), "tp").astype(jnp.float32)
    grad_gain_attn = jnp.sum(attn_in_grad * normed_one, axis=0)
    token_grad = middle_grad + norm_back(attn_in_grad, normed_one, scale_one, first_norm_gain)
    grad_tokens = lax.dynamic_slice_in_dim(token_grad, position * own_rows, own_rows, 0)
    everything = (
        lax.psum_scatter(grad_query, "fsdp", scatter_dimension=0, tiled=True),
        lax.psum_scatter(grad_key, "fsdp", scatter_dimension=0, tiled=True),
        lax.psum_scatter(grad_value, "fsdp", scatter_dimension=0, tiled=True),
        lax.psum_scatter(grad_out, "fsdp", scatter_dimension=1, tiled=True),
        lax.psum_scatter(grad_gain_attn, "fsdp", scatter_dimension=0, tiled=True),
        lax.psum_scatter(grad_shared_gate, "fsdp", scatter_dimension=0, tiled=True),
        lax.psum_scatter(grad_shared_up, "fsdp", scatter_dimension=0, tiled=True),
        lax.psum_scatter(grad_shared_down, "fsdp", scatter_dimension=1, tiled=True),
        lax.psum_scatter(grad_router, "fsdp", scatter_dimension=0, tiled=True),
        lax.psum_scatter(grad_gain_ffn, "fsdp", scatter_dimension=0, tiled=True),
    )
    attn_grads = everything[:5]
    ffn_grads = everything[5:]
    return (
        block_out,
        grad_tokens,
        attn_grads[4],
        attn_grads[0],
        attn_grads[1],
        attn_grads[2],
        attn_grads[3],
        ffn_grads[4],
        ffn_grads[3],
        ffn_grads[0],
        ffn_grads[1],
        ffn_grads[2],
        grad_expert_gate,
        grad_expert_up,
        grad_expert_down,
    )


def solution(mesh):
    return jax.shard_map(
        shards,
        mesh=mesh,
        in_specs=(
            P(("fsdp", "tp"), None),
            P(("fsdp", "tp"), None),
            P("fsdp"),
            P("fsdp", None),
            P("fsdp"),
            P("fsdp", "tp"),
            P("fsdp", "tp"),
            P("fsdp", "tp"),
            P("tp", "fsdp"),
            P("fsdp"),
            P("fsdp", None),
            P("fsdp", "tp"),
            P("fsdp", "tp"),
            P("tp", "fsdp"),
            P("fsdp", None, "tp"),
            P("fsdp", None, "tp"),
            P("fsdp", "tp", None),
        ),
        out_specs=(
            P(("fsdp", "tp"), None),
            P(("fsdp", "tp"), None),
            P("fsdp"),
            P("fsdp", "tp"),
            P("fsdp", "tp"),
            P("fsdp", "tp"),
            P("tp", "fsdp"),
            P("fsdp"),
            P("fsdp", None),
            P("fsdp", "tp"),
            P("fsdp", "tp"),
            P("tp", "fsdp"),
            P("fsdp", None, "tp"),
            P("fsdp", None, "tp"),
            P("fsdp", "tp", None),
        ),
        check_vma=False,
    )
```

profile of v0, /device:TPU:10, one launch (start us, length us, event | category | flops | bytes accessed | tf_op | source)
XLA Modules:
  0.0 3378.7 jit_solution(8281403758844581188)
XLA Ops:
  14.9 65.6 %all-reduce.5 = (bf16[2560]{0:T(1024)(128)(2,1)S(1)}, bf16[2560]{0:T(1024)(128)(2,1)S(1)}) all-reduce(bf16[2560]{0:T(1024)(128)(2,1)S(1)} %dynamic-update-slice, bf16[2560]{0:T(1024)(128)(2,1)S(1)} %dynamic-update-slice.1), channel_id=1, replica_groups=mesh['fsdp'=16,'tp'=2] {'fsdp'}, use_global_device_ids=true, to_apply=%add | all-reduce | flops 5120 | bytes 20480
  86.6 51.9 %all-gather.13.cloned.1.call-done = bf16[2560,256]{1,0:T(8,128)(2,1)} async-done(((bf16[160,256]{1,0:T(8,128)(2,1)}), bf16[2560,256]{1,0:T(8,128)(2,1)}) %all-gather.13.cloned.1.call-update) | async-done | bytes 1310736 | tf_op jit(solution)/shard_map/all_gather | solution.py:109
  140.6 96.6 %all-gather.17.cloned.1.call-done = bf16[2560,1280]{1,0:T(8,128)(2,1)} async-done(((bf16[160,1280]{1,0:T(8,128)(2,1)}), bf16[2560,1280]{1,0:T(8,128)(2,1)}) %all-gather.17.cloned.1.call-update) | async-done | bytes 6553616 | tf_op jit(solution)/shard_map/all_gather | solution.py:107
  246.8 87.8 %all-gather.19.cloned.1.call-done = bf16[1280,2560]{0,1:T(8,128)(2,1)} async-done(((bf16[1280,160]{0,1:T(8,128)(2,1)}), bf16[1280,2560]{0,1:T(8,128)(2,1)}) %all-gather.19.cloned.1.call-update) | async-done | bytes 6553616 | tf_op jit(solution)/shard_map/all_gather | solution.py:110
  342.1 31.4 all-gather
  394.7 18.4 mul.542
  438.0 23.8 gather_fusion.2
  474.4 232.4 %all_to_all.20 = bf16[16,128,2560]{2,1,0:T(8,128)(2,1)} all-to-all(bf16[16,128,2560]{2,1,0:T(8,128)(2,1)S(1)} %get-tuple-element.48), channel_id=1, replica_groups=mesh['fsdp'=16,'tp'=2] {'fsdp'}, dimensions={0} | all-to-all | bytes 20971520 | tf_op jit(solution)/shard_map/all_to_all | solution.py:216
  727.7 282.5 %all-to-all-done.2 = bf16[16,128,2560]{2,1,0:T(8,128)(2,1)} async-done(((bf16[16,128,2560]{2,1,0:T(8,128)(2,1)}), bf16[16,128,2560]{2,1,0:T(8,128)(2,1)}, u32[]{:S(2)}, u32[]{:S(2)}) %all-to-all-start.2) | async-done | bytes 10485792 | tf_op jit(solution)/shard_map/all_to_all | solution.py:244
  1024.2 17.2 fusion.22
  1041.4 15.6 fusion.15
  1057.0 16.8 add_convert_fusion
  1095.5 290.2 %all-to-all-done.3 = bf16[16,128,2560]{2,1,0:T(8,128)(2,1)} async-done(((bf16[16,128,2560]{2,1,0:T(8,128)(2,1)}), bf16[16,128,2560]{2,1,0:T(8,128)(2,1)}, u32[]{:S(2)}, u32[]{:S(2)}) %all-to-all-start.3) | async-done | bytes 10485792 | tf_op jit(solution)/shard_map/all_to_all | solution.py:270
  1407.6 259.5 %all-gather.25.cloned.1.call-done = bf16[1536,2560]{0,1:T(8,128)(2,1)} async-done(((bf16[1536,160]{0,1:T(8,128)(2,1)}), bf16[1536,2560]{0,1:T(8,128)(2,1)}) %all-gather.25.cloned.1.call-update) | async-done | bytes 7864336 | tf_op jit(solution)/shard_map/all_gather | solution.py:113
  1674.9 20.9 gather_fusion.3
  1739.9 20.6 gather_fusion.1
  1928.9 70.4 %all-reduce.4 = (f32[2560]{0:T(1024)S(1)}, f32[2560]{0:T(1024)S(1)}) all-reduce(f32[2560]{0:T(1024)S(1)} %get-tuple-element.19, f32[2560]{0:T(1024)S(1)} %copy-done.58), channel_id=3, replica_groups=mesh['fsdp'=16,'tp'=2] {'fsdp'}, use_global_device_ids=true, to_apply=%region_25.26.clone | all-reduce | flops 5120 | bytes 40960
  2003.8 153.2 %reduce-scatter.22.cloned.1.call-done = f32[160,1536]{1,0:T(8,128)} async-done(((f32[2560,1536]{1,0:T(8,128)}), f32[160,1536]{1,0:T(8,128)}) %reduce-scatter.22.cloned.1.call-update) | async-done | bytes 983056 | tf_op jit(solution)/shard_map/reduce_scatter | solution.py:354
  2157.0 245.3 %reduce-scatter.24.cloned.1.call-done = f32[160,1536]{1,0:T(8,128)} async-done(((f32[2560,1536]{1,0:T(8,128)}), f32[160,1536]{1,0:T(8,128)}) %reduce-scatter.24.cloned.1.call-update) | async-done | bytes 983056 | tf_op jit(solution)/shard_map/reduce_scatter | solution.py:355
  2402.3 244.3 %reduce-scatter.26.cloned.1.call-done = f32[1536,160]{0,1:T(8,128)} async-done(((f32[1536,2560]{0,1:T(8,128)}), f32[1536,160]{0,1:T(8,128)}) %reduce-scatter.26.cloned.1.call-update) | async-done | bytes 983056 | tf_op jit(solution)/shard_map/reduce_scatter | solution.py:356
  2646.6 76.6 %reduce-scatter.18.cloned.1.call-done = f32[160,256]{1,0:T(8,128)} async-done(((f32[2560,256]{1,0:T(8,128)}), f32[160,256]{1,0:T(8,128)}) %reduce-scatter.18.cloned.1.call-update) | async-done | bytes 163856 | tf_op jit(solution)/shard_map/reduce_scatter | solution.py:351
  2723.2 82.4 %reduce-scatter.16.cloned.1.call-done = f32[160,256]{1,0:T(8,128)} async-done(((f32[2560,256]{1,0:T(8,128)}), f32[160,256]{1,0:T(8,128)}) %reduce-scatter.16.cloned.1.call-update) | async-done | bytes 163856 | tf_op jit(solution)/shard_map/reduce_scatter | solution.py:350
  2805.6 285.5 %reduce-scatter.20.cloned.1.call-done = f32[1280,160]{0,1:T(8,128)} async-done(((f32[1280,2560]{0,1:T(8,128)}), f32[1280,160]{0,1:T(8,128)}) %reduce-scatter.20.cloned.1.call-update) | async-done | bytes 819216 | tf_op jit(solution)/shard_map/reduce_scatter | solution.py:352
  3091.1 280.5 %reduce-scatter.14.cloned.1.call-done = f32[160,1280]{1,0:T(8,128)} async-done(((f32[2560,1280]{1,0:T(8,128)}), f32[160,1280]{1,0:T(8,128)}) %reduce-scatter.14.cloned.1.call-update) | async-done | bytes 819216 | tf_op jit(solution)/shard_map/reduce_scatter | solution.py:349
  (344 shorter events, 392.0 us)
Async XLA Ops:
  7.2 74.7 %all-gather.11.cloned.1.call-start = ((), (), s32[]{:S(2)}) async-start(), calls=%async_computation.13 | async-start | bytes 1966080 | tf_op jit(solution)/shard_map/all_gather | solution.py:133
  7.9 75.6 %all-gather.15.cloned.1.call-start = ((), (), s32[]{:S(2)}) async-start(), calls=%async_computation.15 | async-start | bytes 1392640 | tf_op jit(solution)/shard_map/all_gather | solution.py:108
  8.7 129.8 %all-gather.13.cloned.1.call-start = ((), (), s32[]{:S(2)}) async-start(), calls=%async_computation.14 | async-start | bytes 1392640 | tf_op jit(solution)/shard_map/all_gather | solution.py:109
  9.4 227.7 %all-gather.17.cloned.1.call-start = ((), (), s32[]{:S(2)}) async-start(), calls=%async_computation.16 | async-start | bytes 6963200 | tf_op jit(solution)/shard_map/all_gather | solution.py:107
  10.0 324.7 %all-gather.19.cloned.1.call-start = ((), (), s32[]{:S(2)}) async-start(), calls=%async_computation.17 | async-start | bytes 6963200 | tf_op jit(solution)/shard_map/all_gather | solution.py:110
  10.6 375.1 %all-gather.27.cloned.1.call-start = ((), (), s32[]{:S(2)}) async-start(), calls=%async_computation.23 | async-start | bytes 1966080 | tf_op jit(solution)/shard_map/all_gather | solution.py:134
  11.1 402.0 %all-reduce.10.cloned.1.call-start = ((), (), s32[]{:S(2)}) async-start(), calls=%async_computation.18 | async-start | bytes 5242880 | tf_op jit(solution)/shard_map/psum | solution.py:175
  706.8 303.4 %all-to-all-start.2 = ((bf16[16,128,2560]{2,1,0:T(8,128)(2,1)}), bf16[16,128,2560]{2,1,0:T(8,128)(2,1)}, u32[]{:S(2)}, u32[]{:S(2)}) async-start(bf16[16,128,2560]{2,1,0:T(8,128)(2,1)} %get-tuple-element.47), calls=%async_computation.3 | async-start | bytes 20971520 | tf_op jit(solution)/shard_map/all_to_all | solution.py:244
  713.1 681.1 %all-gather.21.cloned.1.call-start = ((), (), s32[]{:S(2)}) async-start(), calls=%async_computation.19 | async-start | bytes 8355840 | tf_op jit(solution)/shard_map/all_gather | solution.py:111
  1073.9 311.8 %all-to-all-start.3 = ((bf16[16,128,2560]{2,1,0:T(8,128)(2,1)}), bf16[16,128,2560]{2,1,0:T(8,128)(2,1)}, u32[]{:S(2)}, u32[]{:S(2)}) async-start(bf16[16,128,2560]{2,1,0:T(8,128)(2,1)} %add_convert_fusion), calls=%async_computation.4 | async-start | bytes 20971520 | tf_op jit(solution)/shard_map/all_to_all | solution.py:270
  1081.8 319.0 %all-gather.23.cloned.1.call-start = ((), (), s32[]{:S(2)}) async-start(), calls=%async_computation.20 | async-start | bytes 8355840 | tf_op jit(solution)/shard_map/all_gather | solution.py:112
  1385.6 354.3 %all-to-all-start.1 = ((bf16[16,128,2560]{2,1,0:T(8,128)(2,1)}), bf16[16,128,2560]{2,1,0:T(8,128)(2,1)}, u32[]{:S(2)}, u32[]{:S(2)}) async-start(bf16[16,128,2560]{2,1,0:T(8,128)(2,1)} %convolution_convert_fusion), calls=%async_computation.1 | async-start | bytes 20971520 | tf_op jit(solution)/shard_map/all_to_all | solution.py:231
  1393.6 273.5 %all-gather.25.cloned.1.call-start = ((), (), s32[]{:S(2)}) async-start(), calls=%async_computation.21 | async-start | bytes 8355840 | tf_op jit(solution)/shard_map/all_gather | solution.py:113
  1394.2 409.9 %all-reduce.12.cloned.1.call-start = ((), (), s32[]{:S(2)}) async-start(), calls=%async_computation.24 | async-start | bytes 5242880 | tf_op jit(solution)/shard_map/psum | solution.py:286
  1736.0 184.0 %reduce-scatter.28.cloned.1.call-start = ((), (), s32[]{:S(2)}) async-start(), calls=%async_computation.33 | async-start | bytes 1392640
  1796.4 125.2 %reduce-scatter.12.cloned.1.call-start = ((), (), s32[]{:S(2)}) async-start(), calls=%async_computation.22 | async-start | bytes 1966080 | tf_op jit(solution)/shard_map/reduce_scatter | solution.py:238
  1803.8 119.8 %all-reduce.14.cloned.1.call-start = ((), (), s32[]{:S(2)}) async-start(), calls=%async_computation.25 | async-start | bytes 2621440 | tf_op jit(solution)/shard_map/psum | solution.py:344
  1833.2 323.8 %reduce-scatter.22.cloned.1.call-start = ((), (), s32[]{:S(2)}) async-start(), calls=%async_computation.30 | async-start | bytes 16711680 | tf_op jit(solution)/shard_map/reduce_scatter | solution.py:354
  1842.1 560.3 %reduce-scatter.24.cloned.1.call-start = ((), (), s32[]{:S(2)}) async-start(), calls=%async_computation.31 | async-start | bytes 16711680 | tf_op jit(solution)/shard_map/reduce_scatter | solution.py:355
  1851.5 795.1 %reduce-scatter.26.cloned.1.call-start = ((), (), s32[]{:S(2)}) async-start(), calls=%async_computation.32 | async-start | bytes 16711680 | tf_op jit(solution)/shard_map/reduce_scatter | solution.py:356
  1860.4 862.8 %reduce-scatter.18.cloned.1.call-start = ((), (), s32[]{:S(2)}) async-start(), calls=%async_computation.28 | async-start | bytes 2785280 | tf_op jit(solution)/shard_map/reduce_scatter | solution.py:351
  1864.1 941.5 %reduce-scatter.16.cloned.1.call-start = ((), (), s32[]{:S(2)}) async-start(), calls=%async_computation.27 | async-start | bytes 2785280 | tf_op jit(solution)/shard_map/reduce_scatter | solution.py:350
  1866.3 1224.8 %reduce-scatter.20.cloned.1.call-start = ((), (), s32[]{:S(2)}) async-start(), calls=%async_computation.29 | async-start | bytes 13926400 | tf_op jit(solution)/shard_map/reduce_scatter | solution.py:352
  1874.7 1496.9 %reduce-scatter.14.cloned.1.call-start = ((), (), s32[]{:S(2)}) async-start(), calls=%async_computation.26 | async-start | bytes 13926400 | tf_op jit(solution)/shard_map/reduce_scatter | solution.py:349
  (82 other events, 2752.6 us)
Sparse Core Ops, SparseCore 0:
  9.6 10.8 all-gather.10
  23.2 56.6 all-gather.14
  82.6 55.8 all-gather.12
  141.0 96.0 all-gather.16
  239.7 94.9 all-gather.18
  336.0 8.6 all-gather.26
  347.7 23.3 all-reduce.9
  717.1 266.3 all-gather.20
  1085.8 272.3 all-gather.22
  1397.3 269.7 all-gather.24
  1736.1 25.0 all-reduce.11
  1796.5 70.9 reduce-scatter.27
  1870.3 16.2 reduce-scatter.11
  1888.9 21.1 all-reduce.13
  1916.2 240.7 reduce-scatter.21
  2164.1 238.1 reduce-scatter.23
  2408.4 238.1 reduce-scatter.25
  2649.4 73.7 reduce-scatter.17
  2726.2 79.3 reduce-scatter.15
  2808.4 282.6 reduce-scatter.19
  3094.1 277.4 reduce-scatter.13
where the time goes:
time: 3390 us; the launch traced here: 3380 us
  waiting for transfers between devices  2440 us (72%)
  blocking collectives  402 us (12%)
  matrix products  254 us (7%)
  local copies, waits for them, and re-layouts  163 us (5%)
  other arithmetic  76.1 us (2%)
    all_to_all x1, waiting for transfers between devices, shards(): lax.all_to_all(row_grads, 'fsdp', split_axis=0, concat_axis=0, tiled=True)  290 us
    reduce_scatter x1, waiting for transfers between devices, shards(): lax.psum_scatter(grad_out, 'fsdp', scatter_dimension=1, tiled=True)  285 us
    all_to_all x1, waiting for transfers between devices, shards(): lax.all_to_all(send_grads, 'fsdp', split_axis=0, concat_axis=0, tiled=True)  283 us
    reduce_scatter x1, waiting for transfers between devices, shards(): lax.psum_scatter(grad_query, 'fsdp', scatter_dimension=0, tiled=True)  281 us
    all_gather x1, waiting for transfers between devices, shards(): lax.all_gather(w_shared_down, 'fsdp', axis=1, tiled=True)  260 us
    reduce_scatter x1, waiting for transfers between devices, shards(): lax.psum_scatter(grad_shared_up, 'fsdp', scatter_dimension=0, tiled=True)  245 us
    reduce_scatter x1, waiting for transfers between devices, shards(): lax.psum_scatter(grad_shared_down, 'fsdp', scatter_dimension=1, tiled=True)  244 us
    all_to_all x1, blocking collectives, shards(): lax.all_to_all(send_rows, 'fsdp', split_axis=0, concat_axis=0, tiled=True)  232 us
  transfers between devices with their start and end apart: 24, of which 13 were waited for; matrix products, arithmetic and copies ran while one was open for 13% of the time, Pallas kernels for 0%

commit v1 on v0

--- a/solution.py
+++ b/solution.py
@@ -1,6 +1,8 @@
 import jax
 import jax.numpy as jnp
 from jax import lax
+from jax.experimental import pallas as pl
+from jax.experimental.pallas import tpu as pltpu
 from jax.sharding import PartitionSpec as P
 
 QUERY_HEADS = 20
@@ -378,9 +380,571 @@
     )
 
 
+GROUP_IDS = ((0, 8), (4, 12), (2, 10), (5, 13), (1, 9), (6, 14), (3, 11), (7, 15))
+
+
+def hop(values, bit):
+    count = lax.axis_size("fsdp")
+    return lax.ppermute(values, "fsdp", [(i, i ^ bit) for i in range(count)])
+
+
+def swap(values):
+    return lax.ppermute(values, "tp", [(0, 1), (1, 0)])
+
+
+def join(*parts):
+    return jnp.concatenate(parts, axis=0)
+
+
+def spread(block):
+    far = hop(block, 8)
+    near = hop(block, 4)
+    cross = hop(block, 12)
+    even0, odd0 = join(block, far), join(near, cross)
+    even1, odd1 = hop(even0, 2), hop(odd0, 1)
+    even2, odd2 = hop(even0, 1), hop(odd0, 2)
+    even3, odd3 = hop(even1, 1), hop(odd1, 2)
+    return even0, odd0, even1, odd1, even2, odd2, even3, odd3
+
+
+def plus(left, right):
+    return (left.astype(jnp.float32) + right.astype(jnp.float32)).astype(jnp.bfloat16)
+
+
+def collect(groups):
+    even0, odd0, even1, odd1, even2, odd2, even3, odd3 = groups
+    even1 = plus(even1, hop(even3, 1))
+    odd1 = plus(odd1, hop(odd3, 2))
+    even0 = plus(even0, hop(even2, 1))
+    odd0 = plus(odd0, hop(odd2, 2))
+    even0 = plus(even0, hop(even1, 2))
+    odd0 = plus(odd0, hop(odd1, 1))
+    rows = even0.shape[0] // 2
+    far = hop(even0[rows:], 8)
+    near = hop(odd0[:rows], 4)
+    cross = hop(odd0[rows:], 12)
+    return (
+        even0[:rows].astype(jnp.float32)
+        + far.astype(jnp.float32)
+        + near.astype(jnp.float32)
+        + cross.astype(jnp.float32)
+    )
+
+
+def in_order(groups, me):
+    rows = groups[0].shape[0] // 2
+    whole = jnp.zeros((rows * 2 * len(groups), groups[0].shape[1]), groups[0].dtype)
+    for ids, group in zip(GROUP_IDS, groups, strict=True):
+        for place, index in enumerate(ids):
+            whole = lax.dynamic_update_slice_in_dim(
+                whole, group[place * rows : (place + 1) * rows], (me ^ index) * rows, 0
+            )
+    return whole
+
+
+def in_groups(whole, me):
+    rows = whole.shape[0] // (2 * len(GROUP_IDS))
+    return [
+        join(
+            *(
+                lax.dynamic_slice_in_dim(whole, (me ^ index) * rows, rows, 0).astype(jnp.bfloat16)
+                for index in ids
+            )
+        )
+        for ids in GROUP_IDS
+    ]
+
+
+def expert_kernel(
+    first,
+    own_ref,
+    other_ref,
+    cot_own_ref,
+    cot_other_ref,
+    place_ref,
+    gate_ref,
+    w_gate_ref,
+    w_up_ref,
+    w_down_ref,
+    shared_in_ref,
+    shared_out_ref,
+    *rest,
+):
+    if first:
+        outs = rest
+    else:
+        shared_sum_ref = rest[0]
+        outs = rest[6:]
+    (
+        shared_grad_ref,
+        rows_ref,
+        dy_ref,
+        hidden_ref,
+        dgate_ref,
+        dup_ref,
+        back_own_ref,
+        back_other_ref,
+        out_own_ref,
+        out_other_ref,
+        pick_ref,
+        cot_rows,
+        back_sum,
+        out_sum,
+        pick_sum,
+        gate_column,
+    ) = outs
+    step = pl.program_id(0)
+    slots = own_ref.shape[0]
+
+    def chooser(part):
+        numbers = lax.broadcasted_iota(jnp.int32, (slots, slots), 0).astype(jnp.float32)
+        return numbers == place_ref[0, part : part + 1, :]
+
+    @pl.when(step == 0)
+    def start():
+        chosen = [chooser(0), chooser(1)]
+        low = [c.astype(jnp.bfloat16) for c in chosen]
+        rows_ref[...] = (product(low[0], own_ref[...]) + product(low[1], other_ref[...])).astype(
+            jnp.bfloat16
+        )
+        cot = product(low[0], cot_own_ref[...]) + product(low[1], cot_other_ref[...])
+        cot_rows[...] = cot.astype(jnp.bfloat16)
+        gates = sum(
+            jnp.sum(
+                jnp.where(chosen[part], gate_ref[0, part : part + 1, :], 0.0),
+                axis=1,
+                keepdims=True,
+            )
+            for part in range(2)
+        )
+        gate_column[...] = gates
+        dy_ref[...] = (gates * cot).astype(jnp.bfloat16)
+        back_sum[...] = jnp.zeros_like(back_sum)
+        out_sum[...] = jnp.zeros_like(out_sum)
+        pick_sum[...] = jnp.zeros_like(pick_sum)
+
+    gates = gate_column[...]
+    gate_pre = product(rows_ref[...], w_gate_ref[0])
+    up_pre = product(rows_ref[...], w_up_ref[0])
+    cot_hidden = times_transposed(cot_rows[...], w_down_ref[0])
+    sigmoid = 1.0 / (1.0 + jnp.exp(-gate_pre))
+    act = gate_pre * sigmoid
+    hidden = (act * up_pre).astype(jnp.bfloat16)
+    hidden_grad = gates * cot_hidden
+    gate_low = (hidden_grad * up_pre * (sigmoid * (1.0 + gate_pre * (1.0 - sigmoid)))).astype(
+        jnp.bfloat16
+    )
+    up_low = (hidden_grad * act).astype(jnp.bfloat16)
+    hidden_ref[...] = hidden
+    dgate_ref[...] = gate_low
+    dup_ref[...] = up_low
+    pick_sum[...] += jnp.sum(hidden.astype(jnp.float32) * cot_hidden, axis=1, keepdims=True)
+    back_sum[...] += times_transposed(gate_low, w_gate_ref[0]) + times_transposed(
+        up_low, w_up_ref[0]
+    )
+    out_sum[...] += product(hidden, w_down_ref[0])
+
+    @pl.when(step == pl.num_programs(0) - 1)
+    def finish():
+        back_rows = back_sum[...].astype(jnp.bfloat16)
+        out_rows = (gates * out_sum[...]).astype(jnp.bfloat16)
+        picks = pick_sum[...]
+        total = None
+        half = shared_out_ref.shape[0]
+        for part, (tok_ref, cot_ref, back_ref, out_ref) in enumerate(
+            (
+                (own_ref, cot_own_ref, back_own_ref, out_own_ref),
+                (other_ref, cot_other_ref, back_other_ref, out_other_ref),
+            )
+        ):
+            chosen = chooser(part)
+            pick_ref[0, part : part + 1, :] = jnp.sum(
+                jnp.where(chosen, picks, 0.0), axis=0, keepdims=True
+            )
+            low = chosen.astype(jnp.bfloat16)
+            both = product(tok_ref[...], shared_in_ref[...])
+            pre, up = both[:, :half], both[:, half:]
+            hid_grad = times_transposed(cot_ref[...], shared_out_ref[...])
+            sig = 1.0 / (1.0 + jnp.exp(-pre))
+            sact = pre * sig
+            shid = (sact * up).astype(jnp.bfloat16)
+            sboth = jnp.concatenate(
+                [hid_grad * up * (sig * (1.0 + pre * (1.0 - sig))), hid_grad * sact], axis=1
+            ).astype(jnp.bfloat16)
+            back_ref[...] = (
+                transposed_times(low, back_rows) + times_transposed(sboth, shared_in_ref[...])
+            ).astype(jnp.bfloat16)
+            out_ref[...] = (
+                transposed_times(low, out_rows) + product(shid, shared_out_ref[...])
+            ).astype(jnp.bfloat16)
+            grads = jnp.concatenate(
+                [
+                    transposed_times(sboth, tok_ref[...]),
+                    transposed_times(shid, cot_ref[...]),
+                ],
+                axis=0,
+            )
+            total = grads if total is None else total + grads
+        if first:
+            shared_grad_ref[...] = total
+        else:
+            shared_grad_ref[...] = shared_sum_ref[...] + total
+
+
+def expert_call(number, tokens, cots, places, gates, weights, kept):
+    own, other = tokens
+    cot_own, cot_other = cots
+    w_gate, w_up, w_down, shared_in, shared_out = weights
+    slots, width = own.shape
+    hidden = w_gate.shape[2]
+    tile = 256
+    total = slots * len(GROUP_IDS)
+    first = kept is None
+
+    def whole(shape):
+        return pl.BlockSpec(shape, lambda h: (0,) * len(shape), pipeline_mode=pl.Buffered(1))
+
+    def rows_block(columns):
+        return pl.BlockSpec((slots, columns), lambda h: (number, 0))
+
+    def tile_block():
+        return pl.BlockSpec((slots, tile), lambda h: (number, h))
+
+    def fixed(shape):
+        return pl.BlockSpec(shape, lambda h: (0,) * len(shape))
+
+    shared_rows = shared_in.shape[1] + shared_out.shape[0]
+    in_specs = [
+        whole((slots, width)),
+        whole((slots, width)),
+        whole((slots, width)),
+        whole((slots, width)),
+        pl.BlockSpec((1, 2, slots), lambda h: (number, 0, 0)),
+        pl.BlockSpec((1, 2, slots), lambda h: (number, 0, 0)),
+        pl.BlockSpec((1, width, tile), lambda h: (0, 0, h)),
+        pl.BlockSpec((1, width, tile), lambda h: (0, 0, h)),
+        pl.BlockSpec((1, tile, width), lambda h: (0, h, 0)),
+        whole(shared_in.shape),
+        whole(shared_out.shape),
+    ]
+    operands = [own, other, cot_own, cot_other, places, gates, w_gate, w_up, w_down]
+    operands += [shared_in, shared_out]
+    aliases = {}
+    if not first:
+        in_specs += [whole((shared_rows, width))] + [pl.BlockSpec(memory_space=pl.ANY)] * 5
+        aliases = {len(operands) + i: i for i in range(6)}
+        operands += list(kept)
+    low = jnp.bfloat16
+    out_shape = [
+        jax.ShapeDtypeStruct((shared_rows, width), jnp.float32),
+        jax.ShapeDtypeStruct((total, width), low),
+        jax.ShapeDtypeStruct((total, width), low),
+        jax.ShapeDtypeStruct((total, hidden), low),
+        jax.ShapeDtypeStruct((total, hidden), low),
+        jax.ShapeDtypeStruct((total, hidden), low),
+        jax.ShapeDtypeStruct((slots, width), low),
+        jax.ShapeDtypeStruct((slots, width), low),
+        jax.ShapeDtypeStruct((slots, width), low),
+        jax.ShapeDtypeStruct((slots, width), low),
+        jax.ShapeDtypeStruct((1, 2, slots), jnp.float32),
+    ]
+    out_specs = [
+        fixed((shared_rows, width)),
+        rows_block(width),
+        rows_block(width),
+        tile_block(),
+        tile_block(),
+        tile_block(),
+        fixed((slots, width)),
+        fixed((slots, width)),
+        fixed((slots, width)),
+        fixed((slots, width)),
+        fixed((1, 2, slots)),
+    ]
+    results = pl.pallas_call(
+        lambda *refs: expert_kernel(first, *refs),
+        grid=(hidden // tile,),
+        in_specs=in_specs,
+        out_specs=out_specs,
+        out_shape=out_shape,
+        scratch_shapes=[
+            pltpu.VMEM((slots, width), low),
+            pltpu.VMEM((slots, width), jnp.float32),
+            pltpu.VMEM((slots, width), jnp.float32),
+            pltpu.VMEM((slots, 1), jnp.float32),
+            pltpu.VMEM((slots, 1), jnp.float32),
+        ],
+        input_output_aliases=aliases,
+        compiler_params=pltpu.CompilerParams(
+            dimension_semantics=("arbitrary",), vmem_limit_bytes=60 * 1024 * 1024
+        ),
+        cost_estimate=pl.CostEstimate(
+            flops=2 * slots * width * (6 * hidden + 2 * slots + 6 * slots),
+            bytes_accessed=24 * 1024 * 1024,
+            transcendentals=slots * hidden,
+        ),
+        name="expert_pass",
+    )(*operands)
+    return results[:6], results[6:8], results[8:10], results[10]
+
+
+def gathered_shards(
+    tokens_in,
+    cotangent,
+    doc_ids,
+    routes,
+    gain_attn,
+    w_query,
+    w_key,
+    w_value,
+    w_out,
+    gain_ffn,
+    w_router,
+    w_shared_gate,
+    w_shared_up,
+    w_shared_down,
+    w_expert_gate,
+    w_expert_up,
+    w_expert_down,
+):
+    low = jnp.bfloat16
+    own_rows, width = tokens_in.shape
+    seq_rows = doc_ids.shape[0]
+    experts = w_router.shape[1]
+    sources = lax.axis_size("fsdp")
+    capacity = max(2, 4 * seq_rows * TOPK // (3 * experts))
+    me = lax.axis_index("fsdp")
+    side = lax.axis_index("tp")
+    relative = jnp.arange(sources, dtype=jnp.int32) ^ me
+    query_width, kv_width = w_query.shape[1], w_key.shape[1]
+    heads_local, kv_local = query_width // HEAD_SIZE, kv_width // HEAD_SIZE
+    per_kv = QUERY_HEADS // KEY_VALUE_HEADS
+
+    small = jnp.concatenate([gain_attn[:, None], gain_ffn[:, None], w_router], axis=1)
+    small_width = small.shape[1]
+    small = jnp.pad(small, ((0, 0), (0, -small_width % 128)))
+    packed = jnp.concatenate([w_query, w_key, w_value, small], axis=1)
+    full_in = in_order(spread(packed), me)
+    qkv_width = query_width + 2 * kv_width
+    full_qkv = full_in[:, :qkv_width]
+    gain_one = full_in[:, qkv_width].astype(jnp.float32)
+    gain_two = full_in[:, qkv_width + 1].astype(jnp.float32)
+    full_router = full_in[:, qkv_width + 2 : qkv_width + small_width]
+    full_out = in_order(spread(w_out.T), me)
+
+    slice_width = w_shared_gate.shape[1] // sources
+    pad_width = -slice_width % 128
+    shards_in = jnp.concatenate(
+        [
+            jnp.pad(
+                part.reshape(part.shape[0], sources, slice_width), ((0, 0), (0, 0), (0, pad_width))
+            )
+            for part in (w_shared_gate, w_shared_up, w_shared_down.T)
+        ],
+        axis=2,
+    )
+    shared_all = lax.all_to_all(
+        shards_in.transpose(1, 0, 2), "fsdp", split_axis=0, concat_axis=0, tiled=True
+    ).reshape(width, 3 * (slice_width + pad_width))
+    wide = slice_width + pad_width
+    shared_in = shared_all[:, : 2 * wide]
+    shared_out = shared_all[:, 2 * wide :].T
+
+    cot_groups = spread(cotangent)
+    cot_pairs = [(group, swap(group)) for group in cot_groups]
+
+    tokens_all = join(tokens_in, swap(tokens_in))
+    residual = tokens_all.astype(jnp.float32)
+    scale_one = rms_scale(residual)
+    normed_one = residual * scale_one
+    attn_input = (normed_one * gain_one).astype(low)
+    turn = side * own_rows
+    rotary_cosine, rotary_sine = (jnp.roll(t, -turn, axis=0) for t in rotary_tables(seq_rows))
+    order_ids = jnp.roll(jnp.arange(seq_rows), -turn)
+    docs = jnp.roll(doc_ids, -turn)
+    projected = product(attn_input, full_qkv)
+    query_rot = (
+        apply_rotary(
+            projected[:, :query_width].reshape(seq_rows, heads_local, HEAD_SIZE),
+            rotary_cosine,
+            rotary_sine,
+        )
+        .astype(low)
+        .reshape(seq_rows, kv_local, per_kv, HEAD_SIZE)
+    )
+    rotated_key = apply_rotary(
+        projected[:, query_width : query_width + kv_width].reshape(seq_rows, kv_local, HEAD_SIZE),
+        rotary_cosine,
+        rotary_sine,
+    ).astype(low)
+    value_low = projected[:, query_width + kv_width :].astype(low)
+    value_low = value_low.reshape(seq_rows, kv_local, HEAD_SIZE)
+    allowed = (docs[:, None] == docs[None, :]) & (order_ids[:, None] >= order_ids[None, :])
+    scores = attention_scores(query_rot, rotated_key, allowed)
+    top_score = jnp.max(scores, axis=-1, keepdims=True)
+    weights = jnp.exp(scores - top_score)
+    attn_probs = weights / jnp.sum(weights, axis=-1, keepdims=True)
+    probs_low = attn_probs.astype(low)
+    heads_out = (
+        jnp.einsum("gjqk,kgd->qgjd", probs_low, value_low, preferred_element_type=jnp.float32)
+        .astype(low)
+        .reshape(seq_rows, heads_local * HEAD_SIZE)
+    )
+    branch = times_transposed(heads_out, full_out)
+    middle = tokens_in.astype(jnp.float32) + (branch[:own_rows] + swap(branch[own_rows:]))
+
+    scale_two = rms_scale(middle)
+    normed_two = middle * scale_two
+    ffn_input = (normed_two * gain_two).astype(low)
+    ffn_groups = spread(ffn_input)
+    ffn_pairs = [(group, swap(group)) for group in ffn_groups]
+    logits = product(ffn_input, full_router)
+    own_routes = lax.dynamic_slice_in_dim(routes, turn, own_rows, 0)
+    routed = jnp.any(
+        own_routes[:, :, None] == jnp.arange(experts, dtype=jnp.int32)[None, None, :], axis=1
+    )
+    top_pick = jnp.max(jnp.where(routed, logits, -jnp.inf), axis=-1, keepdims=True)
+    gate_exp = jnp.where(routed, jnp.exp(logits - top_pick), 0.0)
+    gate_values = gate_exp / jnp.sum(gate_exp, axis=-1, keepdims=True)
+    sent_gates = jnp.where(routed, gate_values, -1.0).T
+    got_gates = lax.all_to_all(sent_gates, "fsdp", split_axis=0, concat_axis=0, tiled=True)
+    got_gates = got_gates[relative]
+    both_gates = jnp.stack([got_gates, swap(got_gates)], axis=1)
+    flags = (both_gates >= 0.0).astype(low).reshape(sources, seq_rows)
+    before = (jnp.arange(seq_rows)[:, None] < jnp.arange(seq_rows)[None, :]).astype(low)
+    ranks = product(flags, before).reshape(both_gates.shape)
+    ids = jnp.asarray(GROUP_IDS)
+    offsets = jnp.arange(2, dtype=jnp.float32)[None, :, None, None] * capacity
+    places = jnp.where(both_gates[ids] >= 0.0, ranks[ids] + offsets, -1.0)
+    places = places.transpose(0, 2, 1, 3).reshape(len(GROUP_IDS), 2, 2 * own_rows)
+    gate_rows = both_gates[ids].transpose(0, 2, 1, 3).reshape(len(GROUP_IDS), 2, 2 * own_rows)
+
+    expert_weights = (w_expert_gate, w_expert_up, w_expert_down, shared_in, shared_out)
+    kept = None
+    back_pairs, out_pairs, picks = [], [], []
+    for number in range(len(GROUP_IDS)):
+        kept, back, out, pick = expert_call(
+            number,
+            ffn_pairs[number],
+            cot_pairs[number],
+            places,
+            gate_rows,
+            expert_weights,
+            kept,
+        )
+        back_pairs.append(back)
+        out_pairs.append(out)
+        picks.append(pick)
+    shared_grads, slot_rows, slot_dy, slot_hidden, slot_dgate, slot_dup = kept
+    input_grad = collect([plus(own, swap(other)) for own, other in back_pairs])
+    ffn_sum = collect([plus(own, swap(other)) for own, other in out_pairs])
+    block_out = (middle + ffn_sum).astype(low)
+
+    pick_groups = jnp.concatenate(picks, axis=0)
+    pick_groups = pick_groups.reshape(len(GROUP_IDS), 2, 2, own_rows)
+    pick_groups = pick_groups[:, 0] + swap(pick_groups[:, 1])
+    pick_blocks = jnp.zeros((sources, own_rows), jnp.float32)
+    pick_blocks = pick_blocks.at[ids.reshape(-1)].set(pick_groups.reshape(sources, own_rows))
+    gate_grad = lax.all_to_all(
+        pick_blocks[relative], "fsdp", split_axis=0, concat_axis=0, tiled=True
+    ).T
+
+    grad_expert_down = transposed_times(slot_hidden, slot_dy)[None]
+    grad_expert_gate = transposed_times(slot_rows, slot_dgate)[None]
+    grad_expert_up = transposed_times(slot_rows, slot_dup)[None]
+
+    shared_back = shared_grads.astype(low).T.reshape(sources, width // sources, 3 * wide)
+    shared_back = lax.all_to_all(shared_back, "fsdp", split_axis=0, concat_axis=0, tiled=True)
+    shared_back = shared_back.transpose(1, 0, 2).astype(jnp.float32)
+    grad_shared_gate, grad_shared_up, grad_shared_down = (
+        shared_back[:, :, i * wide : i * wide + slice_width].reshape(width // sources, -1)
+        for i in range(3)
+    )
+    grad_shared_down = grad_shared_down.T
+
+    pick_grad = gate_values * (gate_grad - jnp.sum(gate_values * gate_grad, axis=-1, keepdims=True))
+    logit_low = jnp.where(routed, pick_grad, 0.0).astype(low)
+    grad_router = transposed_times(ffn_input, logit_low)
+    input_grad = input_grad + times_transposed(logit_low, full_router)
+    grad_gain_ffn = jnp.sum(input_grad * normed_two, axis=0)
+    middle_grad = cotangent.astype(jnp.float32) + norm_back(
+        input_grad, normed_two, scale_two, gain_two
+    )
+    attn_grad_own = middle_grad.astype(low)
+    attn_grad_low = join(attn_grad_own, swap(attn_grad_own))
+
+    grad_out = transposed_times(attn_grad_low, heads_out)
+    heads_grad = (
+        product(attn_grad_low, full_out).astype(low).reshape(seq_rows, kv_local, per_kv, HEAD_SIZE)
+    )
+    probs_grad = jnp.einsum(
+        "qgjd,kgd->gjqk", heads_grad, value_low, preferred_element_type=jnp.float32
+    )
+    value_grad = (
+        jnp.einsum("gjqk,qgjd->kgd", probs_low, heads_grad, preferred_element_type=jnp.float32)
+        .astype(low)
+        .reshape(seq_rows, kv_width)
+    )
+    score_low = (
+        attn_probs * (probs_grad - jnp.sum(attn_probs * probs_grad, axis=-1, keepdims=True))
+    ).astype(low)
+    query_grad = jnp.einsum(
+        "gjqk,kgd->qgjd", score_low, rotated_key, preferred_element_type=jnp.float32
+    ) * HEAD_SIZE ** (-0.5)
+    key_grad = jnp.einsum(
+        "gjqk,qgjd->kgd", score_low, query_rot, preferred_element_type=jnp.float32
+    ) * HEAD_SIZE ** (-0.5)
+    query_low = (
+        apply_rotary(
+            query_grad.reshape(seq_rows, heads_local, HEAD_SIZE), rotary_cosine, -rotary_sine
+        )
+        .astype(low)
+        .reshape(seq_rows, query_width)
+    )
+    key_low = (
+        apply_rotary(key_grad, rotary_cosine, -rotary_sine).astype(low).reshape(seq_rows, kv_width)
+    )
+    qkv_low = jnp.concatenate([query_low, key_low, value_grad], axis=1)
+    grad_qkv = transposed_times(attn_input, qkv_low)
+    attn_in_grad = times_transposed(qkv_low, full_qkv).astype(low)
+    attn_in_grad = attn_in_grad[:own_rows].astype(jnp.float32) + swap(
+        attn_in_grad[own_rows:]
+    ).astype(jnp.float32)
+    normed_own, scale_own = normed_one[:own_rows], scale_one[:own_rows]
+    grad_gain_attn = jnp.sum(attn_in_grad * normed_own, axis=0)
+    grad_tokens = middle_grad + norm_back(attn_in_grad, normed_own, scale_own, gain_one)
+
+    small_grads = jnp.concatenate(
+        [grad_gain_attn[:, None], grad_gain_ffn[:, None], grad_router], axis=1
+    )
+    small_grads = small_grads + swap(small_grads)
+    small_grads = jnp.pad(small_grads, ((0, 0), (0, -small_width % 128)))
+    out_sum = collect(in_groups(grad_out, me))
+    in_sum = collect(in_groups(jnp.concatenate([grad_qkv, small_grads], axis=1), me))
+    small_sum = in_sum[:, qkv_width:]
+    return (
+        block_out,
+        grad_tokens,
+        small_sum[:, 0],
+        in_sum[:, :query_width],
+        in_sum[:, query_width : query_width + kv_width],
+        in_sum[:, query_width + kv_width : qkv_width],
+        out_sum.T,
+        small_sum[:, 1],
+        small_sum[:, 2:small_width],
+        grad_shared_gate,
+        grad_shared_up,
+        grad_shared_down,
+        grad_expert_gate,
+        grad_expert_up,
+        grad_expert_down,
+    )
+
+
 def solution(mesh):
+    wide = mesh.shape["fsdp"] == 16 and mesh.shape["tp"] == 2
     return jax.shard_map(
-        shards,
+        gathered_shards if wide else shards,
         mesh=mesh,
         in_specs=(
             P(("fsdp", "tp"), None),

time: 3390 us -> 1490 us (0.44)
  waiting for transfers between devices: 2440 us -> 623 us
  blocking collectives: 402 us -> 0 us
  Pallas kernels: 0 us -> 218 us
  local copies, waits for them, and re-layouts: 163 us -> 338 us
  matrix products: 254 us -> 81.9 us
  starting transfers between devices: 24.1 us -> 123 us
    reduce_scatter x8 -> x0, waiting for transfers between devices: 1370 us -> none  [the longest x1 285 us: shards(): lax.psum_scatter(grad_out, 'fsdp', scatter_dimension=1, tiled=True)]
    ppermute x0 -> x111, waiting for transfers between devices: none -> 587 us  [the longest x72 587 us: hop(): return lax.ppermute(values, 'fsdp', [(i, i ^ bit) for i in range(count)])]
    all_to_all x3 -> x4, waiting for transfers between devices: 573 us -> 36.5 us  [the longest x1 36.5 us: gathered_shards(): lax.all_to_all(sent_gates, 'fsdp', split_axis=0, concat_axis=0, tiled=True)]
    all_gather x9 -> x0, waiting for transfers between devices: 496 us -> none  [the longest x1 260 us: shards(): lax.all_gather(w_shared_down, 'fsdp', axis=1, tiled=True)]
    all_to_all x1 -> x0, blocking collectives: 232 us -> none  [shards(): lax.all_to_all(send_rows, 'fsdp', split_axis=0, concat_axis=0, tiled=True)]
    pallas_call x0 -> x8, Pallas kernels: none -> 218 us  [expert_call(): pl.pallas_call(lambda *refs: expert_kernel(first, *refs), grid=(hidden //...]
    dynamic_update_slice x0 -> x30, local copies, waits for them, and re-layouts: none -> 210 us  [in_order(): lax.dynamic_update_slice_in_dim(whole, group[place * rows:(place + 1) * r...]
    unnamed x2 -> x0, blocking collectives: 136 us -> none
  transfers between devices with their start and end apart: 24 -> 115, of which waited for: 13 -> 33; matrix products, arithmetic and copies ran while one was open for 13% -> 28% of each run, Pallas kernels for 0% -> 15%
where the time goes in v1:
time: 1490 us; the launch traced here: 1470 us
  waiting for transfers between devices  623 us (42%)
  local copies, waits for them, and re-layouts  338 us (23%)
  Pallas kernels  218 us (15%)
  starting transfers between devices  123 us (8%)
  matrix products  81.9 us (5%)
  other arithmetic  81.5 us (5%)
    ppermute x72, waiting for transfers between devices, hop(): return lax.ppermute(values, 'fsdp', [(i, i ^ bit) for i in range(count)])  587 us
    pallas_call x8, Pallas kernels, expert_call(): pl.pallas_call(lambda *refs: expert_kernel(first, *refs), grid=(hidden //...  218 us
    dynamic_update_slice x30, local copies, waits for them, and re-layouts, in_order(): lax.dynamic_update_slice_in_dim(whole, group[place * rows:(place + 1) * r...  210 us
    ppermute x72, starting transfers between devices, hop(): return lax.ppermute(values, 'fsdp', [(i, i ^ bit) for i in range(count)])  79.1 us
    dot_general x6, matrix products, transposed_times(): lax.dot_general(left_mat, right_mat, (((0,), (0,)), ((), ())), preferred_...  45.3 us
    convert_element_type x24, other arithmetic, plus(): (left.astype(jnp.float32) + right.astype(jnp.float32)).astype(jnp.bfloat16)  39.7 us
    all_to_all x1, waiting for transfers between devices, gathered_shards(): lax.all_to_all(sent_gates, 'fsdp', split_axis=0, concat_axis=0, tiled=True)  36.5 us
    slice x18, local copies, waits for them, and re-layouts, in_order(): group[place * rows:(place + 1) * rows]  33.9 us
  transfers between devices with their start and end apart: 115, of which 33 were waited for; matrix products, arithmetic and copies ran while one was open for 28% of the time, Pallas kernels for 15%

profile of v1, /device:TPU:10, one launch (start us, length us, event | category | flops | bytes accessed | tf_op | source)
XLA Modules:
  0.0 1469.5 jit_solution(18299927554174228851)
XLA Ops:
  36.2 41.6 %collective-permute-done.10 = bf16[160,1280]{1,0:T(8,128)(2,1)S(1)} collective-permute-done((bf16[160,1280]{1,0:T(8,128)(2,1)}, bf16[160,1280]{1,0:T(8,128)(2,1)S(1)}, u32[]{:S(2)}, u32[]{:S(2)}) %collective-permute-start.10) | collective-permute-done | bytes 409632 | tf_op jit(solution)/shard_map/ppermute | solution.py:388
  181.6 23.3 %collective-permute-done.5 = bf16[320,1920]{1,0:T(8,128)(2,1)} collective-permute-done((bf16[320,1920]{1,0:T(8,128)(2,1)}, bf16[320,1920]{1,0:T(8,128)(2,1)}, u32[]{:S(2)}, u32[]{:S(2)}) %collective-permute-start.5) | collective-permute-done | bytes 1228832 | tf_op jit(solution)/shard_map/ppermute | solution.py:388
  453.2 36.5 %all-to-all-done = f32[16,1,128]{2,1,0:T(1,128)S(1)} async-done(((f32[16,1,128]{2,1,0:T(1,128)}), f32[16,1,128]{2,1,0:T(1,128)S(1)}, u32[]{:S(2)}, u32[]{:S(2)}) %all-to-all-start) | async-done | bytes 8224 | tf_op jit(solution)/shard_map/all_to_all | solution.py:810
  510.1 35.5 %collective-permute-done.40.refs_2_ = bf16[256,2560]{1,0:T(8,128)(2,1)} collective-permute-done((bf16[256,2560]{1,0:T(8,128)(2,1)}, bf16[256,2560]{1,0:T(8,128)(2,1)}, u32[]{:S(2)}, u32[]{:S(2)}) %collective-permute-start.40) | collective-permute-done | bytes 1310752 | tf_op jit(solution)/shard_map/ppermute | solution.py:388
  546.9 32.1 %collective-permute-done.28.refs_2_ = bf16[256,2560]{1,0:T(8,128)(2,1)} collective-permute-done((bf16[256,2560]{1,0:T(8,128)(2,1)}, bf16[256,2560]{1,0:T(8,128)(2,1)}, u32[]{:S(2)}, u32[]{:S(2)}) %collective-permute-start.28) | collective-permute-done | bytes 1310752 | tf_op jit(solution)/shard_map/ppermute | solution.py:388
  605.5 23.2 %collective-permute-done.38.refs_0_ = bf16[256,2560]{1,0:T(8,128)(2,1)} collective-permute-done((bf16[256,2560]{1,0:T(8,128)(2,1)}, bf16[256,2560]{1,0:T(8,128)(2,1)}, u32[]{:S(2)}, u32[]{:S(2)}) %collective-permute-start.38) | collective-permute-done | bytes 1310752 | tf_op jit(solution)/shard_map/ppermute | solution.py:388
  628.7 25.6 %expert_pass.8 = (f32[384,2560]{1,0:T(8,128)}, bf16[2048,2560]{1,0:T(8,128)(2,1)}, bf16[2048,2560]{1,0:T(8,128)(2,1)}, bf16[2048,768]{1,0:T(8,128)(2,1)}, bf16[2...) custom-call(bf16[256,2560]{1,0:T(8,128)(2,1)} %pad_maximum_fusion.1., ...), custom_call_target="tpu_custom_call" | custom-call | flops 8724152320 | bytes 25165824 | tf_op jit(solution)/shard_map/expert_pass/pallas_call | solution.py:664
  655.6 27.5 %expert_pass.9 = (f32[384,2560]{1,0:T(8,128)}, bf16[2048,2560]{1,0:T(8,128)(2,1)}, bf16[2048,2560]{1,0:T(8,128)(2,1)}, bf16[2048,768]{1,0:T(8,128)(2,1)}, bf16[2...) custom-call(bf16[256,2560]{1,0:T(8,128)(2,1)} %copy-done.26, ...), custom_call_target="tpu_custom_call", output_to_operand_aliasing={{0}: (11, {}), {1}: (12, {}), {2}: (13, {}), {3}: (14, {}),... | custom-call | flops 8724152320 | bytes 25165824 | tf_op jit(solution)/shard_map/expert_pass/pallas_call | solution.py:664
  685.4 27.4 %expert_pass.10 = (f32[384,2560]{1,0:T(8,128)}, bf16[2048,2560]{1,0:T(8,128)(2,1)}, bf16[2048,2560]{1,0:T(8,128)(2,1)}, bf16[2048,768]{1,0:T(8,128)(2,1)}, bf16[...) custom-call(bf16[256,2560]{1,0:T(8,128)(2,1)} %collective-permute-do, ...), custom_call_target="tpu_custom_call", output_to_operand_aliasing={{0}: (11, {}), {1}: (12, {}), {2}: (13, {}), {3}: (14, {}),... | custom-call | flops 8724152320 | bytes 25165824 | tf_op jit(solution)/shard_map/expert_pass/pallas_call | solution.py:664
  715.0 27.7 %expert_pass.11 = (f32[384,2560]{1,0:T(8,128)}, bf16[2048,2560]{1,0:T(8,128)(2,1)}, bf16[2048,2560]{1,0:T(8,128)(2,1)}, bf16[2048,768]{1,0:T(8,128)(2,1)}, bf16[...) custom-call(bf16[256,2560]{1,0:T(8,128)(2,1)} %collective-permute-do, ...), custom_call_target="tpu_custom_call", output_to_operand_aliasing={{0}: (11, {}), {1}: (12, {}), {2}: (13, {}), {3}: (14, {}),... | custom-call | flops 8724152320 | bytes 25165824 | tf_op jit(solution)/shard_map/expert_pass/pallas_call | solution.py:664
  743.3 27.4 %expert_pass.12 = (f32[384,2560]{1,0:T(8,128)}, bf16[2048,2560]{1,0:T(8,128)(2,1)}, bf16[2048,2560]{1,0:T(8,128)(2,1)}, bf16[2048,768]{1,0:T(8,128)(2,1)}, bf16[...) custom-call(bf16[256,2560]{1,0:T(8,128)(2,1)} %collective-permute-do, ...), custom_call_target="tpu_custom_call", output_to_operand_aliasing={{0}: (11, {}), {1}: (12, {}), {2}: (13, {}), {3}: (14, {}),... | custom-call | flops 8724152320 | bytes 25165824 | tf_op jit(solution)/shard_map/expert_pass/pallas_call | solution.py:664
  772.3 27.6 %expert_pass.13 = (f32[384,2560]{1,0:T(8,128)}, bf16[2048,2560]{1,0:T(8,128)(2,1)}, bf16[2048,2560]{1,0:T(8,128)(2,1)}, bf16[2048,768]{1,0:T(8,128)(2,1)}, bf16[...) custom-call(bf16[256,2560]{1,0:T(8,128)(2,1)} %collective-permute-do, ...), custom_call_target="tpu_custom_call", output_to_operand_aliasing={{0}: (11, {}), {1}: (12, {}), {2}: (13, {}), {3}: (14, {}),... | custom-call | flops 8724152320 | bytes 25165824 | tf_op jit(solution)/shard_map/expert_pass/pallas_call | solution.py:664
  801.2 27.6 %expert_pass.14 = (f32[384,2560]{1,0:T(8,128)}, bf16[2048,2560]{1,0:T(8,128)(2,1)}, bf16[2048,2560]{1,0:T(8,128)(2,1)}, bf16[2048,768]{1,0:T(8,128)(2,1)}, bf16[...) custom-call(bf16[256,2560]{1,0:T(8,128)(2,1)} %collective-permute-do, ...), custom_call_target="tpu_custom_call", output_to_operand_aliasing={{0}: (11, {}), {1}: (12, {}), {2}: (13, {}), {3}: (14, {}),... | custom-call | flops 8724152320 | bytes 25165824 | tf_op jit(solution)/shard_map/expert_pass/pallas_call | solution.py:664
  829.4 27.4 %expert_pass.15 = (f32[384,2560]{1,0:T(8,128)}, bf16[2048,2560]{1,0:T(8,128)(2,1)}, bf16[2048,2560]{1,0:T(8,128)(2,1)}, bf16[2048,768]{1,0:T(8,128)(2,1)}, bf16[...) custom-call(bf16[256,2560]{1,0:T(8,128)(2,1)} %copy-done.66, ...), custom_call_target="tpu_custom_call", output_to_operand_aliasing={{0}: (11, {}), {1}: (12, {}), {2}: (13, {}), {3}: (14, {}),... | custom-call | flops 8724152320 | bytes 25165824 | tf_op jit(solution)/shard_map/expert_pass/pallas_call | solution.py:664
  946.4 43.0 %collective-permute-done.77 = bf16[256,2560]{1,0:T(8,128)(2,1)S(1)} collective-permute-done((bf16[256,2560]{1,0:T(8,128)(2,1)S(1)}, bf16[256,2560]{1,0:T(8,128)(2,1)S(1)}, u32[]{:S(2)}, u32[]{:S(2)}) %collective-permute-start.77) | collective-permute-done | bytes 1310752 | tf_op jit(solution)/shard_map/ppermute | solution.py:388
  1051.5 29.0 %collective-permute-done.78 = bf16[256,2560]{1,0:T(8,128)(2,1)} collective-permute-done((bf16[256,2560]{1,0:T(8,128)(2,1)}, bf16[256,2560]{1,0:T(8,128)(2,1)}, u32[]{:S(2)}, u32[]{:S(2)}) %collective-permute-start.78) | collective-permute-done | bytes 1310752 | tf_op jit(solution)/shard_map/ppermute | solution.py:388
  1090.7 24.5 %collective-permute-done.45 = bf16[256,2560]{1,0:T(8,128)(2,1)S(1)} collective-permute-done((bf16[256,2560]{1,0:T(8,128)(2,1)S(1)}, bf16[256,2560]{1,0:T(8,128)(2,1)S(1)}, u32[]{:S(2)}, u32[]{:S(2)}) %collective-permute-start.45) | collective-permute-done | bytes 1310752 | tf_op jit(solution)/shard_map/ppermute | solution.py:388
  1117.1 27.0 %collective-permute-done.57 = bf16[256,2560]{1,0:T(8,128)(2,1)S(1)} collective-permute-done((bf16[256,2560]{1,0:T(8,128)(2,1)S(1)}, bf16[256,2560]{1,0:T(8,128)(2,1)S(1)}, u32[]{:S(2)}, u32[]{:S(2)}) %collective-permute-start.57) | collective-permute-done | bytes 1310752 | tf_op jit(solution)/shard_map/ppermute | solution.py:388
  1161.7 30.6 %collective-permute-done.88 = bf16[128,2560]{1,0:T(8,128)(2,1)S(1)} collective-permute-done((bf16[128,2560]{1,0:T(8,128)(2,1)S(1)}, bf16[128,2560]{1,0:T(8,128)(2,1)S(1)}, u32[]{:S(2)}, u32[]{:S(2)}) %collective-permute-start.88) | collective-permute-done | bytes 655392 | tf_op jit(solution)/shard_map/ppermute | solution.py:388
  1283.9 22.7 %collective-permute-done.94 = bf16[320,1920]{1,0:T(8,128)(2,1)S(1)} collective-permute-done((bf16[320,1920]{1,0:T(8,128)(2,1)S(1)}, bf16[320,1920]{1,0:T(8,128)(2,1)S(1)}, u32[]{:S(2)}, u32[]{:S(2)}) %collective-permute-start.94) | collective-permute-done | bytes 1228832 | tf_op jit(solution)/shard_map/ppermute | solution.py:388
  1327.4 23.1 %collective-permute-done.93 = bf16[320,1920]{1,0:T(8,128)(2,1)S(1)} collective-permute-done((bf16[320,1920]{1,0:T(8,128)(2,1)S(1)}, bf16[320,1920]{1,0:T(8,128)(2,1)S(1)}, u32[]{:S(2)}, u32[]{:S(2)}) %collective-permute-start.93) | collective-permute-done | bytes 1228832 | tf_op jit(solution)/shard_map/ppermute | solution.py:388
  1353.3 22.4 %collective-permute-done.97 = bf16[320,1920]{1,0:T(8,128)(2,1)S(1)} collective-permute-done((bf16[320,1920]{1,0:T(8,128)(2,1)S(1)}, bf16[320,1920]{1,0:T(8,128)(2,1)S(1)}, u32[]{:S(2)}, u32[]{:S(2)}) %collective-permute-start.97) | collective-permute-done | bytes 1228832 | tf_op jit(solution)/shard_map/ppermute | solution.py:388
  1384.8 29.0 %collective-permute-done.105 = bf16[160,1280]{1,0:T(8,128)(2,1)S(1)} collective-permute-done((bf16[160,1280]{1,0:T(8,128)(2,1)S(1)}, bf16[160,1280]{1,0:T(8,128)(2,1)S(1)}, u32[]{:S(2)}, u32[]{:S(2)}) %collective-permute-start.105) | collective-permute-done | bytes 409632 | tf_op jit(solution)/shard_map/ppermute | solution.py:388
  1427.5 24.0 %collective-permute-done.96 = bf16[160,1920]{1,0:T(8,128)(2,1)S(1)} collective-permute-done((bf16[160,1920]{1,0:T(8,128)(2,1)S(1)}, bf16[160,1920]{1,0:T(8,128)(2,1)S(1)}, u32[]{:S(2)}, u32[]{:S(2)}) %collective-permute-start.96) | collective-permute-done | bytes 614432 | tf_op jit(solution)/shard_map/ppermute | solution.py:388
  (775 shorter events, 781.0 us)
Async XLA Ops:
  4.8 97.1 %collective-permute-start.1 = (bf16[160,1920]{1,0:T(8,128)(2,1)}, bf16[160,1920]{1,0:T(8,128)(2,1)S(1)}, u32[]{:S(2)}, u32[]{:S(2)}) collective-permute-start(bf16[160,1920]{1,0:T(8,128)(2,1)} %pad_maximum_fusion.18), channel_id=1, source_target_pairs={{0,16},{2,18},{4,20},{6,22},{8,24},{10,26},{12,28},{14,30},{16,0},... | collective-permute-start | bytes 1843208 | tf_op jit(solution)/shard_map/ppermute | solution.py:388
  7.4 93.1 %collective-permute-start.2 = (bf16[160,1920]{1,0:T(8,128)(2,1)}, bf16[160,1920]{1,0:T(8,128)(2,1)S(1)}, u32[]{:S(2)}, u32[]{:S(2)}) collective-permute-start(bf16[160,1920]{1,0:T(8,128)(2,1)} %pad_maximum_fusion.18), channel_id=1, source_target_pairs={{0,8},{2,10},{4,12},{6,14},{8,0},{10,2},{12,4},{14,6},{16,24},{18,... | collective-permute-start | bytes 1843208 | tf_op jit(solution)/shard_map/ppermute | solution.py:388
  7.9 120.7 %collective-permute-start.3 = (bf16[160,1920]{1,0:T(8,128)(2,1)}, bf16[160,1920]{1,0:T(8,128)(2,1)}, u32[]{:S(2)}, u32[]{:S(2)}) collective-permute-start(bf16[160,1920]{1,0:T(8,128)(2,1)} %pad_maximum_fusion.18), channel_id=1, source_target_pairs={{0,24},{2,26},{4,28},{6,30},{8,16},{10,18},{12,20},{14,22},{16,8},... | collective-permute-start | bytes 1843208 | tf_op jit(solution)/shard_map/ppermute | solution.py:388
  8.3 69.5 %collective-permute-start.10 = (bf16[160,1280]{1,0:T(8,128)(2,1)}, bf16[160,1280]{1,0:T(8,128)(2,1)S(1)}, u32[]{:S(2)}, u32[]{:S(2)}) collective-permute-start(bf16[160,1280]{1,0:T(8,128)(2,1)} %bitcast.161), channel_id=1, source_target_pairs={{0,16},{2,18},{4,20},{6,22},{8,24},{10,26},{12,28},{14,30},{16,0},... | collective-permute-start | bytes 1228808 | tf_op jit(solution)/shard_map/ppermute | solution.py:388
  11.8 67.8 %collective-permute-start.11 = (bf16[160,1280]{1,0:T(8,128)(2,1)}, bf16[160,1280]{1,0:T(8,128)(2,1)}, u32[]{:S(2)}, u32[]{:S(2)}) collective-permute-start(bf16[160,1280]{1,0:T(8,128)(2,1)} %bitcast.162), channel_id=1, source_target_pairs={{0,8},{2,10},{4,12},{6,14},{8,0},{10,2},{12,4},{14,6},{16,24},{18,... | collective-permute-start | bytes 1228808 | tf_op jit(solution)/shard_map/ppermute | solution.py:388
  161.1 165.7 %collective-permute-start.17 = (bf16[320,1280]{1,0:T(8,128)(2,1)}, bf16[320,1280]{1,0:T(8,128)(2,1)}, u32[]{:S(2)}, u32[]{:S(2)}) collective-permute-start(bf16[320,1280]{1,0:T(8,128)(2,1)} %collective-permute-done.13), channel_id=1, source_target_pairs={{0,2},{2,0},{4,6},{6,4},{8,10},{10,8},{12,14},{14,12},{16,18},{18,... | collective-permute-start | bytes 2457608 | tf_op jit(solution)/shard_map/ppermute | solution.py:388
  176.0 154.5 %collective-permute-start.18 = (bf16[320,1280]{1,0:T(8,128)(2,1)}, bf16[320,1280]{1,0:T(8,128)(2,1)}, u32[]{:S(2)}, u32[]{:S(2)}) collective-permute-start(bf16[320,1280]{1,0:T(8,128)(2,1)} %collective-permute-done.14), channel_id=1, source_target_pairs={{0,4},{2,6},{4,0},{6,2},{8,12},{10,14},{12,8},{14,10},{16,20},{18,... | collective-permute-start | bytes 2457608 | tf_op jit(solution)/shard_map/ppermute | solution.py:388
  431.0 67.5 %collective-permute-start.34 = (bf16[128,2560]{1,0:T(8,128)(2,1)S(1)}, bf16[128,2560]{1,0:T(8,128)(2,1)}, u32[]{:S(2)}, u32[]{:S(2)}) collective-permute-start(bf16[128,2560]{1,0:T(8,128)(2,1)S(1)} %copy-done.12), channel_id=1, source_target_pairs={{0,8},{2,10},{4,12},{6,14},{8,0},{10,2},{12,4},{14,6},{16,24},{18,... | collective-permute-start | bytes 1966088 | tf_op jit(solution)/shard_map/ppermute | solution.py:388
  432.9 67.6 %collective-permute-start.35 = (bf16[128,2560]{1,0:T(8,128)(2,1)S(1)}, bf16[128,2560]{1,0:T(8,128)(2,1)}, u32[]{:S(2)}, u32[]{:S(2)}) collective-permute-start(bf16[128,2560]{1,0:T(8,128)(2,1)S(1)} %copy-done.12), channel_id=1, source_target_pairs={{0,24},{2,26},{4,28},{6,30},{8,16},{10,18},{12,20},{14,22},{16,8},... | collective-permute-start | bytes 1966088 | tf_op jit(solution)/shard_map/ppermute | solution.py:388
  489.8 94.3 %all-to-all-start.1 = ((bf16[16,160,384]{2,1,0:T(8,128)(2,1)}), bf16[16,160,384]{2,1,0:T(8,128)(2,1)S(1)}, u32[]{:S(2)}, u32[]{:S(2)}) async-start(bf16[16,160,384]{2,1,0:T(8,128)(2,1)} %copy.513), calls=%async_computation.1 | async-start | bytes 3932160 | tf_op jit(solution)/shard_map/all_to_all | solution.py:746
  505.0 74.1 %collective-permute-start.28 = (bf16[256,2560]{1,0:T(8,128)(2,1)}, bf16[256,2560]{1,0:T(8,128)(2,1)}, u32[]{:S(2)}, u32[]{:S(2)}) collective-permute-start(bf16[256,2560]{1,0:T(8,128)(2,1)} %constant_dynamic-update-slice_fusion.4.refs_2_), channel_id=1, source_target_pairs={{0,2},{2,0},{4,6},{6,4},{8,10},{10,8},{12,14},{14,12},{16,18},{18,... | collective-permute-start | bytes 3932168 | tf_op jit(solution)/shard_map/ppermute | solution.py:388
  506.4 72.6 %collective-permute-start.53 = (bf16[256,2560]{1,0:T(8,128)(2,1)}, bf16[256,2560]{1,0:T(8,128)(2,1)}, u32[]{:S(2)}, u32[]{:S(2)}) collective-permute-start(bf16[256,2560]{1,0:T(8,128)(2,1)} %constant_dynamic-update-slice_fusion.8.refs_2_), channel_id=1, source_target_pairs={{0,4},{2,6},{4,0},{6,2},{8,12},{10,14},{12,8},{14,10},{16,20},{18,... | collective-permute-start | bytes 3932168 | tf_op jit(solution)/shard_map/ppermute | solution.py:388
  507.0 73.1 %collective-permute-start.20 = (bf16[128,2560]{1,0:T(8,128)(2,1)S(1)}, bf16[128,2560]{1,0:T(8,128)(2,1)S(1)}, u32[]{:S(2)}, u32[]{:S(2)}) collective-permute-start(bf16[128,2560]{1,0:T(8,128)(2,1)S(1)} %multiply_convert_fusion.1), channel_id=1, source_target_pairs={{0,16},{2,18},{4,20},{6,22},{8,24},{10,26},{12,28},{14,30},{16,0},... | collective-permute-start | bytes 1966088 | tf_op jit(solution)/shard_map/ppermute | solution.py:388
  604.0 79.7 %collective-permute-start.26 = (bf16[256,2560]{1,0:T(8,128)(2,1)}, bf16[256,2560]{1,0:T(8,128)(2,1)}, u32[]{:S(2)}, u32[]{:S(2)}) collective-permute-start(bf16[256,2560]{1,0:T(8,128)(2,1)} %pad_maximum_fusion.1.refs_0_), channel_id=1, source_target_pairs={{0,2},{2,0},{4,6},{6,4},{8,10},{10,8},{12,14},{14,12},{16,18},{18,... | collective-permute-start | bytes 3932168 | tf_op jit(solution)/shard_map/ppermute | solution.py:388
  771.2 256.6 %collective-permute-start.72 = (bf16[256,2560]{1,0:T(8,128)(2,1)}, bf16[256,2560]{1,0:T(8,128)(2,1)}, u32[]{:S(2)}, u32[]{:S(2)}) collective-permute-start(bf16[256,2560]{1,0:T(8,128)(2,1)} %get-tuple-element.164), channel_id=1, source_target_pairs={{0,1},{1,0},{2,3},{3,2},{4,5},{5,4},{6,7},{7,6},{8,9},{9,8},{10,11... | collective-permute-start | bytes 3932168 | tf_op jit(solution)/shard_map/ppermute | solution.py:392
  800.7 81.3 %collective-permute-start.73 = (bf16[256,2560]{1,0:T(8,128)(2,1)}, bf16[256,2560]{1,0:T(8,128)(2,1)}, u32[]{:S(2)}, u32[]{:S(2)}) collective-permute-start(bf16[256,2560]{1,0:T(8,128)(2,1)} %get-tuple-element.166), channel_id=1, source_target_pairs={{0,1},{1,0},{2,3},{3,2},{4,5},{5,4},{6,7},{7,6},{8,9},{9,8},{10,11... | collective-permute-start | bytes 3932168 | tf_op jit(solution)/shard_map/ppermute | solution.py:392
  801.0 144.4 %collective-permute-start.75 = (bf16[256,2560]{1,0:T(8,128)(2,1)}, bf16[256,2560]{1,0:T(8,128)(2,1)}, u32[]{:S(2)}, u32[]{:S(2)}) collective-permute-start(bf16[256,2560]{1,0:T(8,128)(2,1)} %get-tuple-element.168), channel_id=1, source_target_pairs={{0,1},{1,0},{2,3},{3,2},{4,5},{5,4},{6,7},{7,6},{8,9},{9,8},{10,11... | collective-permute-start | bytes 3932168 | tf_op jit(solution)/shard_map/ppermute | solution.py:392
  828.8 67.5 %collective-permute-start.81 = (bf16[256,2560]{1,0:T(8,128)(2,1)}, bf16[256,2560]{1,0:T(8,128)(2,1)S(1)}, u32[]{:S(2)}, u32[]{:S(2)}) collective-permute-start(bf16[256,2560]{1,0:T(8,128)(2,1)} %get-tuple-element.174), channel_id=1, source_target_pairs={{0,1},{1,0},{2,3},{3,2},{4,5},{5,4},{6,7},{7,6},{8,9},{9,8},{10,11... | collective-permute-start | bytes 3932168 | tf_op jit(solution)/shard_map/ppermute | solution.py:392
  829.2 163.8 %collective-permute-start.83 = (bf16[256,2560]{1,0:T(8,128)(2,1)}, bf16[256,2560]{1,0:T(8,128)(2,1)}, u32[]{:S(2)}, u32[]{:S(2)}) collective-permute-start(bf16[256,2560]{1,0:T(8,128)(2,1)} %get-tuple-element.176), channel_id=1, source_target_pairs={{0,1},{1,0},{2,3},{3,2},{4,5},{5,4},{6,7},{7,6},{8,9},{9,8},{10,11... | collective-permute-start | bytes 3932168 | tf_op jit(solution)/shard_map/ppermute | solution.py:392
  929.9 99.3 %all-to-all-start.3 = ((bf16[16,160,384]{2,1,0:T(8,128)(2,1)}), bf16[16,160,384]{2,1,0:T(8,128)(2,1)S(1)}, u32[]{:S(2)}, u32[]{:S(2)}) async-start(bf16[16,160,384]{2,1,0:T(8,128)(2,1)} %bitcast.54), calls=%async_computation.3 | async-start | bytes 3932160 | tf_op jit(solution)/shard_map/all_to_all | solution.py:857
  997.6 86.0 %collective-permute-start.80 = (bf16[256,2560]{1,0:T(8,128)(2,1)}, bf16[256,2560]{1,0:T(8,128)(2,1)}, u32[]{:S(2)}, u32[]{:S(2)}) collective-permute-start(bf16[256,2560]{1,0:T(8,128)(2,1)} %get-tuple-element.172), channel_id=1, source_target_pairs={{0,1},{1,0},{2,3},{3,2},{4,5},{5,4},{6,7},{7,6},{8,9},{9,8},{10,11... | collective-permute-start | bytes 3932168 | tf_op jit(solution)/shard_map/ppermute | solution.py:392
  1148.3 230.8 %collective-permute-start.58 = (bf16[128,2560]{1,0:T(8,128)(2,1)}, bf16[128,2560]{1,0:T(8,128)(2,1)}, u32[]{:S(2)}, u32[]{:S(2)}) collective-permute-start(bf16[128,2560]{1,0:T(8,128)(2,1)} %slice.350), channel_id=1, source_target_pairs={{0,16},{2,18},{4,20},{6,22},{8,24},{10,26},{12,28},{14,30},{16,0},... | collective-permute-start | bytes 1966088 | tf_op jit(solution)/shard_map/ppermute | solution.py:388
  1380.0 71.5 %collective-permute-start.96 = (bf16[160,1920]{1,0:T(8,128)(2,1)S(1)}, bf16[160,1920]{1,0:T(8,128)(2,1)S(1)}, u32[]{:S(2)}, u32[]{:S(2)}) collective-permute-start(bf16[160,1920]{1,0:T(8,128)(2,1)S(1)} %slice.367), channel_id=1, source_target_pairs={{0,16},{2,18},{4,20},{6,22},{8,24},{10,26},{12,28},{14,30},{16,0},... | collective-permute-start | bytes 1843208 | tf_op jit(solution)/shard_map/ppermute | solution.py:388
  1384.8 66.7 %collective-permute-start.100 = (bf16[160,1920]{1,0:T(8,128)(2,1)S(1)}, bf16[160,1920]{1,0:T(8,128)(2,1)S(1)}, u32[]{:S(2)}, u32[]{:S(2)}) collective-permute-start(bf16[160,1920]{1,0:T(8,128)(2,1)S(1)} %get-tuple-element.372), channel_id=1, source_target_pairs={{0,8},{2,10},{4,12},{6,14},{8,0},{10,2},{12,4},{14,6},{16,24},{18,... | collective-permute-start | bytes 1843208 | tf_op jit(solution)/shard_map/ppermute | solution.py:388
  (247 other events, 7646.8 us)

commit v2 on v0

--- a/solution.py
+++ b/solution.py
@@ -1,6 +1,9 @@
 import jax
 import jax.numpy as jnp
 from jax import lax
+from jax.experimental import pallas as pl
+from jax.experimental.layout import Layout, with_layout_constraint
+from jax.experimental.pallas import tpu as pltpu
 from jax.sharding import PartitionSpec as P
 
 QUERY_HEADS = 20
@@ -378,9 +381,1130 @@
     )
 
 
+PAIRS = ((4, 8), (0, 1), (9, 12), (14, 6), (15, 11), (13, 7), (5, 10), (2, 3))
+
+
+class Flight:
+    pass
+
+
+class Take:
+    def __init__(self, flight):
+        self.flight = flight
+
+    def __getattr__(self, name):
+        return vars(self.flight).pop(name)
+
+
+def hop(values, bit):
+    count = lax.axis_size("fsdp")
+    return lax.ppermute(values, "fsdp", [(i, i ^ bit) for i in range(count)])
+
+
+def swap(values):
+    return lax.ppermute(values, "tp", [(0, 1), (1, 0)])
+
+
+def route(values, rule):
+    pairs = []
+    for group in range(lax.axis_size("fsdp")):
+        for side in range(2):
+            target = rule(group, side)
+            if target is not None:
+                pairs.append((group * 2 + side, target[0] * 2 + target[1]))
+    return lax.ppermute(values, ("fsdp", "tp"), pairs)
+
+
+def is_home(group, side):
+    return (group // 4) % 2 == side
+
+
+def home_far(group, side):
+    return (group ^ 8, side) if is_home(group, side) else None
+
+
+def home_near(group, side):
+    return (group ^ 4, side) if is_home(group, side) else None
+
+
+def near_home(group, side):
+    return None if is_home(group, side) else (group ^ 4, side)
+
+
+def home_side(group, side):
+    return (group, 1 - side) if is_home(group, side) else None
+
+
+def pack_out_a(group, side):
+    return (group ^ 4, 1) if side == group // 8 else (group ^ 8, 0)
+
+
+def pack_out_b(group, side):
+    return (group, 0) if side == group // 8 else (group ^ 12, 1)
+
+
+def pack_back_a(group, side):
+    return (group ^ (8 if side == 0 else 4), group // 8)
+
+
+def pack_back_b(group, side):
+    return (group ^ (0 if side == 0 else 12), group // 8)
+
+
+def plane_one(group, side):
+    return (group ^ (1 if side == 0 else 2), side)
+
+
+def plane_two(group, side):
+    return (group ^ (2 if side == 0 else 1), side)
+
+
+def cot_first_route(group, side):
+    return (group ^ (8 if side == 0 else 4), side)
+
+
+def cot_second_route(group, side):
+    return (group ^ 4, 1) if side == 0 else None
+
+
+COT_CARRIED = ((0, 8, 1, 9, 2, 10, 3, 11), (4, 12, 6, 14, 5, 13, 7, 15))
+CARRIED = ((0, 8, 1, 9, 2, 10, 3, 11), (12, 4, 14, 6, 13, 5, 15, 7))
+
+
+def join(*parts):
+    return jnp.concatenate(parts, axis=0)
+
+
+def plus(left, right):
+    return (left.astype(jnp.float32) + right.astype(jnp.float32)).astype(jnp.bfloat16)
+
+
+def piece(view):
+    array, start, rows = view
+    return array if array.shape[0] == rows else array[start : start + rows]
+
+
+def whole_view(array):
+    return (array, 0, array.shape[0])
+
+
+def as_tuple(index):
+    return index if isinstance(index, tuple) else (index,)
+
+
+LINE = (0, 4, 8, 12)
+
+
+def exchange_plane(block_for):
+    parts = [jnp.stack([block_for(line + plane) for line in LINE]) for plane in range(4)]
+    parts = [parts[0]] + [hop(parts[plane], plane) for plane in (1, 2, 3)]
+    return {line: jnp.stack([part[i] for part in parts]) for i, line in enumerate(LINE)}
+
+
+def exchange_line(sent, lines):
+    return {line: hop(sent[line], line) if line else sent[line] for line in lines}
+
+
+def exchange_join(got, me):
+    rows, columns = got[0].shape[1:]
+    whole = jnp.zeros((16, rows, columns), got[0].dtype)
+    for line, blocks in got.items():
+        for plane in range(4):
+            whole = lax.dynamic_update_slice_in_dim(
+                whole, blocks[plane : plane + 1], me ^ (line + plane), 0
+            )
+    return whole
+
+
+def chosen_slots(place_ref, which, slots):
+    numbers = lax.broadcasted_iota(jnp.int32, (slots, place_ref.shape[2]), 0)
+    return numbers.astype(jnp.float32) == place_ref[0, which : which + 1, :]
+
+
+def expert_kernel(first, number, starts, *refs):
+    side_ref, tok_refs, cot_refs = refs[0], refs[1:5], refs[5:9]
+    w_gate_ref, w_up_ref, w_down_ref, in_ref, out_ref = refs[9:14]
+    refs = refs[14 if first else 21 :]
+    stores = refs[:7]
+    back_refs, note_ref = refs[7:10], refs[10]
+    (
+        toks,
+        cots,
+        rows,
+        cot_rows,
+        dys,
+        hids,
+        dboth,
+        shareds,
+        w_both,
+        w_down,
+        w_in,
+        w_out,
+        gate_terms,
+        sems,
+        store_sems,
+    ) = refs[11:]
+    part_rows = back_refs[0].shape[0]
+    starts, spots = starts
+    side = side_ref[0]
+    seq_rows = 2 * part_rows
+    hidden = w_down.shape[0]
+    tile = 256
+    slots = rows.shape[0] // 2
+
+    parts = [pl.ds(i * part_rows, part_rows) for i in range(4)]
+    pairs = [
+        (tok_refs[i].at[pl.ds(starts[i], part_rows)], toks.at[parts[i]]) for i in range(4)
+    ]
+    pairs += [(in_ref, w_in)]
+    pairs += [(None, cots.at[parts[i]]) for i in range(4)]
+    pairs += [(out_ref, w_out)]
+    for start in range(0, hidden, tile):
+        cut = pl.ds(start, tile)
+        pairs += [
+            (w_gate_ref.at[0, :, cut], w_both.at[:, cut]),
+            (w_up_ref.at[0, :, cut], w_both.at[:, pl.ds(hidden + start, tile)]),
+            (w_down_ref.at[0, cut], w_down.at[cut]),
+        ]
+    def cot_copy(which, half, source):
+        row = spots[which][0] * seq_rows + (side if half == 0 else 1 - side) * part_rows
+        index = 5 + 2 * which + half
+        return pltpu.make_async_copy(
+            source.at[pl.ds(pl.multiple_of(row, part_rows), part_rows)],
+            pairs[index][1],
+            sems.at[index],
+        )
+
+    loads = []
+    for index, (source, target) in enumerate(pairs):
+        if source is None:
+            which, half = divmod(index - 5, 2)
+            mine, other = cot_refs[2 * which], cot_refs[2 * which + 1]
+            is_mine = side == spots[which][1]
+
+            @pl.when(is_mine)
+            def start_mine(which=which, half=half, mine=mine):
+                cot_copy(which, half, mine).start()
+
+            @pl.when(jnp.logical_not(is_mine))
+            def start_other(which=which, half=half, other=other):
+                cot_copy(which, half, other).start()
+
+            loads.append(cot_copy(which, half, mine))
+        else:
+            loads.append(pltpu.make_async_copy(source, target, sems.at[index]))
+            loads[-1].start()
+
+    sent = []
+
+    def store(index, source):
+        target = stores[index].at[pl.ds(number * source.shape[0], source.shape[0])]
+        copy = pltpu.make_async_copy(source, target, store_sems.at[index])
+        copy.start()
+        sent.append(copy)
+
+    gate_loads = []
+    experts, term_width = gate_terms.shape[0] // 4, gate_terms.shape[1]
+    for i in range(4):
+        source = tok_refs[i].at[pl.ds(starts[i] + part_rows, experts), pl.ds(0, term_width)]
+        target = gate_terms.at[pl.ds(i * experts, experts)]
+        gate_loads.append(pltpu.make_async_copy(source, target, store_sems.at[7 + i]))
+        gate_loads[-1].start()
+    for load in gate_loads:
+        load.wait()
+    expert = side_ref[1]
+    numbers = lax.broadcasted_iota(jnp.int32, (experts, term_width), 0)
+    before = lax.broadcasted_iota(jnp.int32, (seq_rows, seq_rows), 0) < (
+        lax.broadcasted_iota(jnp.int32, (seq_rows, seq_rows), 1)
+    )
+    before = before.astype(jnp.float32).astype(jnp.bfloat16)
+    for which in range(2):
+        halves = []
+        for i in (2 * which, 2 * which + 1):
+            terms = gate_terms[i * experts : (i + 1) * experts, :].astype(jnp.float32)
+            row = jnp.sum(jnp.where(numbers == expert, terms, 0.0), axis=0, keepdims=True)
+            halves.append(
+                row[:, :part_rows]
+                + row[:, part_rows : 2 * part_rows]
+                + row[:, 2 * part_rows : 3 * part_rows]
+            )
+        gate_row = jnp.concatenate(halves, axis=1)
+        flags = jnp.where(gate_row >= 0.0, 1.0, 0.0)
+        ranks = product(
+            jnp.broadcast_to(flags, (8, seq_rows)).astype(jnp.bfloat16), before
+        )[:1]
+        note_ref[2 + which : 3 + which, :] = jnp.where(flags > 0.0, ranks, -1.0)
+        note_ref[4 + which : 5 + which, :] = gate_row
+    for load in loads[:4]:
+        load.wait()
+    slot_numbers = lax.broadcasted_iota(jnp.int32, (slots, seq_rows), 0).astype(jnp.float32)
+    chosen = [slot_numbers == note_ref[2 + which : 3 + which, :] for which in range(2)]
+    low = [c.astype(jnp.bfloat16) for c in chosen]
+    for which in range(2):
+        span = slice(which * slots, (which + 1) * slots)
+        seq = slice(which * seq_rows, (which + 1) * seq_rows)
+        rows[span, :] = product(low[which], toks[seq, :]).astype(jnp.bfloat16)
+    store(0, rows)
+    store(5, toks)
+    loads[4].wait()
+    shared_pre = product(toks[...], w_in[...])
+    for load in loads[5:9]:
+        load.wait()
+    gates = [
+        jnp.sum(
+            jnp.where(chosen[which], note_ref[4 + which : 5 + which, :], 0.0),
+            axis=1,
+            keepdims=True,
+        )
+        for which in range(2)
+    ]
+    for which in range(2):
+        span = slice(which * slots, (which + 1) * slots)
+        seq = slice(which * seq_rows, (which + 1) * seq_rows)
+        picked = product(low[which], cots[seq, :])
+        cot_rows[span, :] = picked.astype(jnp.bfloat16)
+        dys[span, :] = (gates[which] * picked).astype(jnp.bfloat16)
+    store(1, dys)
+    store(6, cots)
+    gates = jnp.concatenate(gates, axis=0)
+    loads[9].wait()
+    half = w_out.shape[0]
+    pre, up = shared_pre[:, :half], shared_pre[:, half:]
+    hid_grad = times_transposed(cots[...], w_out[...])
+    sigmoid = 1.0 / (1.0 + jnp.exp(-pre))
+    act = pre * sigmoid
+    shareds[:, :half] = (hid_grad * up * (sigmoid * (1.0 + pre * (1.0 - sigmoid)))).astype(
+        jnp.bfloat16
+    )
+    shareds[:, half : 2 * half] = (hid_grad * act).astype(jnp.bfloat16)
+    shareds[:, 2 * half :] = (act * up).astype(jnp.bfloat16)
+    store(4, shareds)
+
+    picks = jnp.zeros_like(gates)
+    for index, start in enumerate(range(0, hidden, tile)):
+        for load in loads[10 + 3 * index : 13 + 3 * index]:
+            load.wait()
+        cut = slice(start, start + tile)
+        cut_up = slice(hidden + start, hidden + start + tile)
+        gate_pre = product(rows[...], w_both[:, cut])
+        up_pre = product(rows[...], w_both[:, cut_up])
+        cot_hidden = times_transposed(cot_rows[...], w_down[cut, :])
+        sigmoid = 1.0 / (1.0 + jnp.exp(-gate_pre))
+        act = gate_pre * sigmoid
+        hid = (act * up_pre).astype(jnp.bfloat16)
+        grad = gates * cot_hidden
+        hids[:, cut] = hid
+        dboth[:, cut] = (grad * up_pre * (sigmoid * (1.0 + gate_pre * (1.0 - sigmoid)))).astype(
+            jnp.bfloat16
+        )
+        dboth[:, cut_up] = (grad * act).astype(jnp.bfloat16)
+        picks = picks + jnp.sum(hid.astype(jnp.float32) * cot_hidden, axis=1, keepdims=True)
+    store(2, hids)
+    store(3, dboth)
+    back_rows = times_transposed(dboth[...], w_both[...]).astype(jnp.bfloat16)
+    for which in range(2):
+        span = slice(which * slots, (which + 1) * slots)
+        seq = slice(which * seq_rows, (which + 1) * seq_rows)
+        back = transposed_times(low[which], back_rows[span, :]) + times_transposed(
+            shareds[seq, : 2 * half], w_in[...]
+        )
+        back_refs[which][...] = back[:part_rows, :].astype(jnp.bfloat16)
+        back_refs[2][which * part_rows : (which + 1) * part_rows, :] = back[
+            part_rows:, :
+        ].astype(jnp.bfloat16)
+        note_ref[which : which + 1, :] = jnp.sum(
+            jnp.where(chosen[which], picks[span, :], 0.0), axis=0, keepdims=True
+        )
+    for copy in sent:
+        copy.wait()
+
+
+def expert_call(number, position, tokens, cots, weights, kept):
+    w_gate, w_up, w_down, shared_in, shared_out = weights
+    experts, width = 16, tokens[0][0].shape[1]
+    part_rows = tokens[0][2] - experts
+    starts = (tuple(view[1] for view in tokens), tuple(cot[2:] for cot in cots))
+    slots = part_rows
+    hidden = w_gate.shape[2]
+    calls = len(PAIRS)
+    first = kept is None
+    low = jnp.bfloat16
+    some = pl.BlockSpec(memory_space=pl.ANY)
+    backs = [pl.BlockSpec((n * part_rows, width), lambda i: (0, 0)) for n in (1, 1, 2)]
+    note = pl.BlockSpec((6, 2 * part_rows), lambda i: (0, 0))
+    in_specs = [pl.BlockSpec(memory_space=pltpu.SMEM)] + [some] * 13
+    operands = [position, *(view[0] for view in tokens)]
+    operands += [array for cot in cots for array in cot[:2]]
+    operands += weights
+    aliases = {}
+    if not first:
+        aliases = {len(operands) + i: i for i in range(7)}
+        in_specs += [some] * 7
+        operands += list(kept)
+    shared_width = 3 * shared_out.shape[0]
+    kept_shapes = [(2 * slots, width)] * 2 + [(2 * slots, hidden), (2 * slots, 2 * hidden)]
+    kept_shapes += [(4 * part_rows, c) for c in (shared_width, width, width)]
+    out_shape = [jax.ShapeDtypeStruct((calls * r, c), low) for r, c in kept_shapes]
+    out_shape += [jax.ShapeDtypeStruct((n * part_rows, width), low) for n in (1, 1, 2)]
+    out_shape += [jax.ShapeDtypeStruct((6, 2 * part_rows), jnp.float32)]
+    results = pl.pallas_call(
+        lambda *refs: expert_kernel(first, number, starts, *refs),
+        grid=(1,),
+        in_specs=in_specs,
+        out_specs=[some] * 7 + backs + [note],
+        out_shape=out_shape,
+        scratch_shapes=[
+            pltpu.VMEM((4 * part_rows, width), low),
+            pltpu.VMEM((4 * part_rows, width), low),
+            pltpu.VMEM((2 * slots, width), low),
+            pltpu.VMEM((2 * slots, width), low),
+            pltpu.VMEM((2 * slots, width), low),
+            pltpu.VMEM((2 * slots, hidden), low),
+            pltpu.VMEM((2 * slots, 2 * hidden), low),
+            pltpu.VMEM((4 * part_rows, shared_width), low),
+            pltpu.VMEM((width, 2 * hidden), low),
+            pltpu.VMEM((hidden, width), low),
+            pltpu.VMEM(shared_in.shape, low),
+            pltpu.VMEM(shared_out.shape, low),
+            pltpu.VMEM((4 * experts, 3 * part_rows), low),
+            pltpu.SemaphoreType.DMA((10 + 3 * (hidden // 256),)),
+            pltpu.SemaphoreType.DMA((11,)),
+        ],
+        input_output_aliases=aliases,
+        compiler_params=pltpu.CompilerParams(vmem_limit_bytes=36 * 1024 * 1024),
+        cost_estimate=pl.CostEstimate(
+            flops=4 * slots * width * (5 * hidden + 10 * slots),
+            bytes_accessed=24 * 1024 * 1024,
+            transcendentals=slots * hidden,
+        ),
+        name="expert_pass",
+    )(*operands)
+    return results[:7], results[7:10], results[10]
+
+
+def output_kernel(
+    place_ref, gate_ref, hid_ref, shared_ref, w_down_ref, w_out_ref, own_ref, other_ref
+):
+    part_rows = own_ref.shape[0] // 2
+    seq_rows = 2 * part_rows
+    slots = hid_ref.shape[0] // 2
+    half = w_out_ref.shape[0]
+    result = product(hid_ref[...], w_down_ref[0])
+    for which in range(2):
+        chosen = chosen_slots(place_ref, which, slots)
+        gates = jnp.sum(
+            jnp.where(chosen, gate_ref[0, which : which + 1, :], 0.0), axis=1, keepdims=True
+        )
+        gated = (gates * result[which * slots : (which + 1) * slots, :]).astype(jnp.bfloat16)
+        seq = slice(which * seq_rows, (which + 1) * seq_rows)
+        out = transposed_times(chosen.astype(jnp.bfloat16), gated) + product(
+            shared_ref[seq, 2 * half :], w_out_ref[...]
+        )
+        rows = slice(which * part_rows, (which + 1) * part_rows)
+        own_ref[rows, :] = out[:part_rows, :].astype(jnp.bfloat16)
+        other_ref[rows, :] = out[part_rows:, :].astype(jnp.bfloat16)
+
+
+def output_call(places, gates, hids, shareds, w_down, shared_out):
+    calls = len(PAIRS)
+    slots, hidden = places.shape[2] // 2, hids.shape[1]
+    width = shared_out.shape[1]
+    tok_rows = shareds.shape[0] // calls
+    row = pl.BlockSpec((1, 2, places.shape[2]), lambda i: (i, 0, 0))
+    half = jax.ShapeDtypeStruct((calls * tok_rows // 2, width), jnp.bfloat16)
+    return pl.pallas_call(
+        output_kernel,
+        grid=(calls,),
+        in_specs=[
+            row,
+            row,
+            pl.BlockSpec((2 * slots, hidden), lambda i: (i, 0)),
+            pl.BlockSpec((tok_rows, shareds.shape[1]), lambda i: (i, 0)),
+            pl.BlockSpec(w_down.shape, lambda i: (0, 0, 0)),
+            pl.BlockSpec(shared_out.shape, lambda i: (0, 0)),
+        ],
+        out_specs=[pl.BlockSpec((tok_rows // 2, width), lambda i: (i, 0))] * 2,
+        out_shape=[half] * 2,
+        compiler_params=pltpu.CompilerParams(vmem_limit_bytes=48 * 1024 * 1024),
+        cost_estimate=pl.CostEstimate(
+            flops=4 * slots * width * (hidden + 4 * slots) * calls,
+            bytes_accessed=32 * 1024 * 1024,
+            transcendentals=0,
+        ),
+        name="expert_outputs",
+    )(places, gates, hids, shareds, w_down, shared_out)
+
+
+def gathered_shards(
+    tokens_in,
+    cotangent,
+    doc_ids,
+    routes,
+    gain_attn,
+    w_query,
+    w_key,
+    w_value,
+    w_out,
+    gain_ffn,
+    w_router,
+    w_shared_gate,
+    w_shared_up,
+    w_shared_down,
+    w_expert_gate,
+    w_expert_up,
+    w_expert_down,
+):
+    low = jnp.bfloat16
+    own_rows, width = tokens_in.shape
+    seq_rows = doc_ids.shape[0]
+    experts = w_router.shape[1]
+    sources = lax.axis_size("fsdp")
+    capacity = max(2, 4 * seq_rows * TOPK // (3 * experts))
+    me = lax.axis_index("fsdp")
+    side = lax.axis_index("tp")
+    relative = jnp.arange(sources, dtype=jnp.int32) ^ me
+    query_width, kv_width = w_query.shape[1], w_key.shape[1]
+    heads_local, kv_local = query_width // HEAD_SIZE, kv_width // HEAD_SIZE
+    per_kv = QUERY_HEADS // KEY_VALUE_HEADS
+
+    state = Flight()
+    take = Take(state)
+    state.expert_grads = {}
+
+    def barrier():
+        vars(state).update(lax.optimization_barrier(dict(vars(state))))
+
+    def launch(moves):
+        got = []
+        for name, parts in moves.items():
+            for starts, ends in parts:
+                starts, ends = as_tuple(starts), as_tuple(ends)
+                blocks = [vars(state)[name][index] for index in starts]
+                value = blocks[0] if len(blocks) == 1 else join(*blocks)
+                got.append((name, ends, hop(value, starts[0] ^ ends[0])))
+        return got
+
+    def meet(got, value):
+        blocks, value = lax.optimization_barrier(([block for *_, block in got], value))
+        return [(*key, block) for (*key, _), block in zip(got, blocks, strict=True)], value
+
+    def settle(got):
+        for name, ends, value in got:
+            rows = value.shape[0] // len(ends)
+            for place, end in enumerate(ends):
+                part = piece((value, place * rows, rows))
+                if name not in summed:
+                    vars(state)[name][end] = part
+                    views[end] = (value, place * rows, rows)
+                elif end in vars(state)[name]:
+                    vars(state)[name][end] = plus(vars(state)[name][end], part)
+                else:
+                    later[name, end] = part
+
+    def stage(moves, work=None):
+        barrier()
+        if work is not None:
+            work()
+        settle(launch(moves))
+
+    summed = ("back", "out")
+    later = {}
+    views = {}
+
+    small = jnp.concatenate([gain_attn[:, None], gain_ffn[:, None], w_router], axis=1)
+    small_width = small.shape[1]
+    small = jnp.pad(small, ((0, 0), (0, -small_width % 128)))
+    position = jnp.stack([side, me]).astype(jnp.int32)
+
+    layer = me // 4
+    here = side == layer // 2
+    home = layer % 2 == side
+    parity_b = jnp.where(here, layer, layer ^ 3) % 2
+    group_width = per_kv * HEAD_SIZE
+    pack_width = 2 * group_width + 2 * HEAD_SIZE
+    qkv_width = group_width + 2 * HEAD_SIZE
+    out_t = w_out.T
+    packs = [
+        jnp.concatenate(
+            [
+                w_query[:, j * group_width : (j + 1) * group_width],
+                w_key[:, j * HEAD_SIZE : (j + 1) * HEAD_SIZE],
+                w_value[:, j * HEAD_SIZE : (j + 1) * HEAD_SIZE],
+                out_t[:, j * group_width : (j + 1) * group_width],
+                small,
+            ],
+            axis=1,
+        )
+        for j in range(kv_local)
+    ]
+    state.packs = tuple(
+        jnp.where(parity_b == parity, packs[0], packs[1]) for parity in (1, 0)
+    )
+    state.tokens = tokens_in
+    state.cot = cotangent
+
+    def whole_of(own):
+        other = swap(own)
+        return jnp.where(side == 0, join(own, other), join(other, own))
+
+    def carried(number, mine):
+        zero, one = CARRIED[0][number], CARRIED[1][number]
+        return me ^ (jnp.where(side == 0, zero, one) if mine else jnp.where(side == 0, one, zero))
+
+    slice_width = w_shared_gate.shape[1] // sources
+    pad_width = -slice_width % 128
+    wide = slice_width + pad_width
+    state.shared_parts = (w_shared_gate, w_shared_up, w_shared_down)
+
+    def shard_for(index):
+        return lax.dynamic_index_in_dim(shards_in, me ^ index, 0, keepdims=False)
+
+    doc_rows = jnp.zeros((16, width), low).at[0, :seq_rows].set(doc_ids.astype(low))
+    barrier()
+    pack_a, pack_b = (
+        route(pack, rule)
+        for pack, rule in zip(take.packs, (pack_out_a, pack_out_b), strict=True)
+    )
+    state.base = join(pack_b, pack_a)
+    state.tokens = join(whole_of(take.tokens), doc_rows)
+    state.cot = whole_of(take.cot)
+    barrier()
+    base, whole_tokens = take.base, state.tokens
+    state.early = join(base, route(base, plane_one))
+    state.far = route(whole_tokens, home_far)
+    state.near = route(whole_tokens, home_near)
+    shared_parts = take.shared_parts
+    shards_in = jnp.concatenate(
+        [
+            jnp.pad(
+                part.reshape(part.shape[0], sources, slice_width),
+                ((0, 0), (0, 0), (0, pad_width)),
+            )
+            for part in (*shared_parts[:2], shared_parts[2].T)
+        ],
+        axis=2,
+    ).transpose(1, 0, 2)
+
+    state.shards = exchange_plane(shard_for)
+    barrier()
+    early, far = state.early, state.far
+    state.second = route(early, plane_two)
+    state.early_other = swap(early)
+    state.cross = route(far, home_near)
+    state.shards_got = exchange_line(state.shards, (0, 12))
+    barrier()
+    second, early, early_other = take.second, take.early, take.early_other
+    line_parts = [
+        jnp.where(home, one, two)
+        for one, two in ((take.tokens, take.near), (take.far, take.cross))
+    ]
+    token_rows = join(*(part[:seq_rows] for part in line_parts))
+    docs = jnp.stack([part[seq_rows, :seq_rows] for part in line_parts])
+    state.cot_one = route(state.cot, cot_first_route)
+    state.shards_got.update(exchange_line(state.shards, (8,)))
+    pack_rows = pack_a.shape[0]
+    full_weights = jnp.zeros((width, pack_a.shape[1]), low)
+    number = 0
+    for part, got in ((early, early_other), (second, swap(second))):
+        for place in range(part.shape[0] // pack_rows):
+            rows = slice(place * pack_rows, (place + 1) * pack_rows)
+            for block, mine in ((part[rows], True), (got[rows], False)):
+                full_weights = lax.dynamic_update_slice_in_dim(
+                    full_weights, block, carried(number, mine) * pack_rows, 0
+                )
+                full_weights = with_layout_constraint(
+                    full_weights, Layout(major_to_minor=(0, 1))
+                )
+            number += 1
+
+    rotary_cosine, rotary_sine = (
+        jnp.tile(table, (2, 1)) for table in rotary_tables(seq_rows)
+    )
+    order_ids = jnp.arange(seq_rows)
+    allowed = (docs[:, :, None] == docs[:, None, :]) & (
+        order_ids[:, None] >= order_ids[None, :]
+    )
+    small_all = full_weights[:, pack_width:]
+    gain_one = small_all[:, 0].astype(jnp.float32)
+    gain_two = small_all[:, 1].astype(jnp.float32)
+    full_router = small_all[:, 2:small_width]
+    scale = HEAD_SIZE ** (-0.5)
+
+    def attend():
+        rows = token_rows.astype(jnp.float32)
+        attn_input = (rows * rms_scale(rows) * gain_one).astype(low)
+        state.attn_input = attn_input
+        projected = product(attn_input, full_weights[:, :qkv_width])
+        query_rot = apply_rotary(
+            projected[:, :group_width].reshape(2 * seq_rows, per_kv, HEAD_SIZE),
+            rotary_cosine,
+            rotary_sine,
+        )
+        query_rot = query_rot.astype(low).reshape(2, seq_rows, per_kv, HEAD_SIZE)
+        rotated_key = apply_rotary(
+            projected[:, group_width : group_width + HEAD_SIZE][:, None, :],
+            rotary_cosine,
+            rotary_sine,
+        )
+        rotated_key = rotated_key.astype(low).reshape(2, seq_rows, HEAD_SIZE)
+        value_low = projected[:, group_width + HEAD_SIZE :].astype(low)
+        value_low = value_low.reshape(2, seq_rows, HEAD_SIZE)
+        scores = (
+            jnp.einsum("sqjd,skd->sjqk", query_rot, rotated_key, preferred_element_type=jnp.float32)
+            * scale
+        )
+        scores = jnp.where(allowed[:, None], scores, -1e30)
+        top_score = jnp.max(scores, axis=-1, keepdims=True)
+        weights = jnp.exp(scores - top_score)
+        attn_probs = weights / jnp.sum(weights, axis=-1, keepdims=True)
+        probs_low = attn_probs.astype(low)
+        heads_out = (
+            jnp.einsum("sjqk,skd->sqjd", probs_low, value_low, preferred_element_type=jnp.float32)
+            .astype(low)
+            .reshape(2 * seq_rows, group_width)
+        )
+        state.attention = (query_rot, rotated_key, value_low, attn_probs, probs_low)
+        state.heads_out = heads_out
+        state.branch = times_transposed(heads_out, full_weights[:, qkv_width:pack_width]).astype(low)
+
+    attend()
+    barrier()
+
+    own_routes = lax.dynamic_slice_in_dim(routes, side * own_rows, own_rows, 0)
+    routed = jnp.any(
+        own_routes[:, :, None] == jnp.arange(experts, dtype=jnp.int32)[None, None, :], axis=1
+    )
+
+    def near_sum(partial):
+        own_part, far_part = partial[:seq_rows], partial[seq_rows:]
+        state.far_part = plus(far_part, route(far_part, near_home))
+        state.own_part = own_part.astype(jnp.float32) + route(own_part, near_home).astype(
+            jnp.float32
+        )
+
+    def far_sum():
+        return take.own_part + route(take.far_part, home_far).astype(jnp.float32)
+
+    def own_of(own_sum):
+        mine = lax.dynamic_slice_in_dim(own_sum, side * own_rows, own_rows, 0)
+        other = lax.dynamic_slice_in_dim(own_sum, (1 - side) * own_rows, own_rows, 0)
+        return jnp.where(home, mine, route(other, home_side))
+
+    near_sum(take.branch)
+    cot_whole, cot_one = take.cot, take.cot_one
+    cot_two = route(cot_one, cot_second_route)
+    state.cot_base = jnp.where(side == 0, join(cot_whole, cot_one), join(cot_one, cot_two))
+    barrier()
+    cot_base = take.cot_base
+    state.cot_first = route(cot_base, plane_one)
+    cot_base_other = swap(cot_base)
+    state.shards_got.update(exchange_line(take.shards, (4,)))
+    state.own_sum = far_sum()
+    state.cot_base_other = cot_base_other
+    barrier()
+    own_sum, cot_base_other = take.own_sum, take.cot_base_other
+    middle = tokens_in.astype(jnp.float32) + own_of(own_sum)
+    state.middle = middle
+    state.scale_two = scale_two = rms_scale(middle)
+    normed_two = middle * scale_two
+    state.normed_two = normed_two
+    state.ffn = {0: (normed_two * gain_two).astype(low)}
+
+    def cot_view(index):
+        for core, order in enumerate(COT_CARRIED):
+            if index in order:
+                part, place = divmod(order.index(index), 2)
+                if part == 3:
+                    part, place = part + place, 0
+                return (*cot_parts[part], place, core)
+
+    logits = product(state.ffn[0], full_router)
+    top_pick = jnp.max(jnp.where(routed, logits, -jnp.inf), axis=-1, keepdims=True)
+    gate_exp = jnp.where(routed, jnp.exp(logits - top_pick), 0.0)
+    gate_values = gate_exp / jnp.sum(gate_exp, axis=-1, keepdims=True)
+    state.gate_values = gate_values
+    rest = jnp.where(routed, gate_values, -1.0).T
+    terms = []
+    for _ in range(3):
+        terms.append(rest.astype(low))
+        rest = rest - terms[-1].astype(jnp.float32)
+    gate_rows = jnp.concatenate(terms, axis=1)
+    gate_rows = jnp.pad(gate_rows, ((0, 0), (0, width - gate_rows.shape[1])))
+    ffn_own = state.ffn[0]
+    state.ffn[0] = join(ffn_own, gate_rows)
+    block_rows = own_rows + experts
+
+    views[0] = whole_view(state.ffn[0])
+    other_views = {}
+    swapping = []
+
+    def swap_tokens(indices):
+        blocks = [state.ffn[index] for index in indices]
+        others = swap(blocks[0] if len(blocks) == 1 else join(*blocks))
+        for place, index in enumerate(indices):
+            swapping.append((index, (others, place * block_rows, block_rows)))
+
+    def swapped():
+        other_views.update(dict(swapping))
+        swapping.clear()
+
+    barrier()
+    cot_first = take.cot_first
+    cot_parts = {0: (cot_base, cot_base_other)}
+    cot_third = route(cot_base, plane_two)
+    state.cot_third = cot_third
+    got = launch(dict(ffn=((0, 8), (0, 4), (0, 1), (0, 2))))
+    settle(got)
+    swapped()
+    shared_all = exchange_join(take.shards_got, me).reshape(width, 3 * wide)
+    state.shared_in = shared_all[:, : 2 * wide]
+    state.shared_out = shared_all[:, 2 * wide :].T
+
+    state.back, state.back_own, state.back_other, state.notes = {}, {}, {}, {}
+    kept = None
+
+    def experts_of(*numbers):
+        def work():
+            nonlocal kept
+            for number in numbers:
+                one, two = PAIRS[number]
+                kept, back, state.notes[number] = expert_call(
+                    number,
+                    position,
+                    (views[one], other_views[one], views[two], other_views[two]),
+                    (cot_view(one), cot_view(two)),
+                    (
+                        w_expert_gate,
+                        w_expert_up,
+                        w_expert_down,
+                        state.shared_in,
+                        state.shared_out,
+                    ),
+                    kept,
+                )
+                state.back_own[one], state.back_own[two] = back[:2]
+                state.back_other[one, two] = back[2]
+
+        return work
+
+    def swap_back():
+        ((indices, both_rows),) = state.back_other.items()
+        state.back_other.clear()
+        others = swap(both_rows)
+        return [
+            (index, others[place * own_rows : (place + 1) * own_rows])
+            for place, index in enumerate(indices)
+        ]
+
+    def merge_back(fresh):
+        for index, other in fresh:
+            total = plus(state.back_own.pop(index), other)
+            if ("back", index) in later:
+                total = plus(total, later.pop(("back", index)))
+            state.back[index] = total
+
+    def both(*works):
+        def work():
+            for one in works:
+                one()
+
+        return work
+
+    plan = (
+        ((4, 8, 0, 1), dict(ffn=((8, 12), (8, 9), (8, 10)))),
+        ((9, 12, 2), dict(ffn=((12, 14), (2, 6), (12, 13)))),
+        ((14, 6, 10), dict(ffn=((13, 15), (1, 5), (10, 11)))),
+        ((13, 15, 11), dict(ffn=((2, 3), (5, 7)))),
+        ((5, 3, 7), dict(back=((9, 8),))),
+        ((), dict(back=((14, 12), (6, 2)))),
+        ((), dict(back=((15, 13), (11, 10)))),
+        ((), dict(back=((13, 12), (7, 3)))),
+    )
+    fresh = []
+    for number, (arrived, moves) in enumerate(plan):
+        barrier()
+        if number in (1, 2):
+            cot_last = take.cot_last
+        if state.back_other:
+            fresh = swap_back()
+        if arrived:
+            swap_tokens(arrived)
+        if number == 0:
+            swapped()
+            cot_parts[1] = (cot_first, swap(cot_first))
+        if number == 1:
+            cot_third = take.cot_third
+            cot_parts[2] = (cot_third, swap(cot_third))
+        if number in (0, 1):
+            state.cot_last = route(
+                cot_first[number * seq_rows : (number + 1) * seq_rows], plane_two
+            )
+        if number in (1, 2):
+            cot_parts[number + 2] = (cot_last, swap(cot_last))
+        experts_of(number)()
+        got, state.notes[number] = meet(launch(moves), state.notes[number])
+        settle(got)
+        swapped()
+        merge_back(fresh)
+        fresh = []
+    barrier()
+    fresh = swap_back()
+    merge_back(fresh)
+    del state.ffn
+    state.kept = kept
+
+    def outputs():
+        hids, shareds = state.kept[2], state.kept[4]
+        notes = jnp.stack([state.notes[number] for number in range(len(PAIRS))])
+        state.out_own, state.out_other = output_call(
+            notes[:, 2:4],
+            notes[:, 4:],
+            hids,
+            shareds,
+            w_expert_down,
+            state.shared_out,
+        )
+
+    def return_picks():
+        picks = jnp.concatenate([state.notes[number][:2] for number in range(len(PAIRS))], axis=0)
+        picks = picks[:, :own_rows] + swap(picks[:, own_rows:])
+        picks = picks[jnp.argsort(jnp.asarray(PAIRS).reshape(-1))]
+        state.gate_grad = lax.all_to_all(
+            picks[relative], "fsdp", split_axis=0, concat_axis=0, tiled=True
+        ).T
+
+    def expert_grads(which):
+        def work():
+            slot_rows, slot_dy, hids, dboth = state.kept[:4]
+            hidden = hids.shape[1]
+            left, right = (
+                (hids, slot_dy),
+                (slot_rows, dboth[:, :hidden]),
+                (slot_rows, dboth[:, hidden:]),
+            )[which]
+            state.expert_grads[which] = transposed_times(left, right)[None]
+
+        return work
+
+    def shared_grads():
+        shareds, all_rows, all_cots = state.kept[4:]
+        both_grads = jnp.concatenate(
+            [
+                transposed_times(all_rows, shareds[:, : 2 * wide]),
+                transposed_times(all_cots, shareds[:, 2 * wide :]),
+            ],
+            axis=1,
+        )
+        state.shared_grads = both_grads.astype(low).reshape(
+            sources, width // sources, 3 * wide
+        )
+
+    def shared_grad_for(index):
+        return lax.dynamic_index_in_dim(state.shared_grads, me ^ index, 0, keepdims=False)
+
+    outputs()
+    got, state.out_own = meet(
+        launch(dict(back=((10, 8), ((5, 12), (1, 8))))), state.out_own
+    )
+    settle(got)
+    barrier()
+    return_picks()
+    shared_grads()
+    got, state.shared_grads = meet(
+        launch(dict(back=((8, 0), ((3, 1), (2, 0))))), state.shared_grads
+    )
+    settle(got)
+    out_own_rows, out_other_rows = take.out_own, swap(take.out_other)
+    state.out_other_rows = out_other_rows
+    barrier()
+    settle(launch(dict(back=((4, 0), (2, 0)))))
+    state.shards = exchange_plane(shared_grad_for)
+    out_other_rows = take.out_other_rows
+    state.out = {}
+    for number, index in enumerate(index for pair in PAIRS for index in pair):
+        rows = slice(number * own_rows, (number + 1) * own_rows)
+        state.out[index] = plus(out_own_rows[rows], out_other_rows[rows])
+    def middle_back():
+        gate_values, gate_grad = state.gate_values, state.gate_grad
+        normed_two, ffn_input = state.normed_two, ffn_own
+        pick_grad = gate_values * (
+            gate_grad - jnp.sum(gate_values * gate_grad, axis=-1, keepdims=True)
+        )
+        logit_low = jnp.where(routed, pick_grad, 0.0).astype(low)
+        input_grad = state.back.pop(0).astype(jnp.float32)
+        grad_router = transposed_times(ffn_input, logit_low)
+        input_grad = input_grad + times_transposed(logit_low, full_router)
+        grad_gain_ffn = jnp.sum(input_grad * normed_two, axis=0)
+        middle_grad = cotangent.astype(jnp.float32) + norm_back(
+            input_grad, normed_two, state.scale_two, gain_two
+        )
+        state.middle_grad = middle_grad
+        state.small_two = jnp.concatenate([grad_gain_ffn[:, None], grad_router], axis=1)
+        state.attn_grad = middle_grad.astype(low)
+
+    def attention_back():
+        attn_grad_low = take.attn_grad
+        full_qkv, full_out = full_weights[:, :qkv_width], full_weights[:, qkv_width:pack_width]
+        query_rot, rotated_key, value_low, attn_probs, probs_low = state.attention
+        heads_grad = (
+            product(attn_grad_low, full_out).astype(low).reshape(2, seq_rows, per_kv, HEAD_SIZE)
+        )
+        probs_grad = jnp.einsum(
+            "sqjd,skd->sjqk", heads_grad, value_low, preferred_element_type=jnp.float32
+        )
+        value_grad = (
+            jnp.einsum("sjqk,sqjd->skd", probs_low, heads_grad, preferred_element_type=jnp.float32)
+            .astype(low)
+            .reshape(2 * seq_rows, HEAD_SIZE)
+        )
+        score_low = (
+            attn_probs * (probs_grad - jnp.sum(attn_probs * probs_grad, axis=-1, keepdims=True))
+        ).astype(low)
+        query_grad = (
+            jnp.einsum("sjqk,skd->sqjd", score_low, rotated_key, preferred_element_type=jnp.float32)
+            * scale
+        )
+        key_grad = (
+            jnp.einsum("sjqk,sqjd->skd", score_low, query_rot, preferred_element_type=jnp.float32)
+            * scale
+        )
+        query_low = apply_rotary(
+            query_grad.reshape(2 * seq_rows, per_kv, HEAD_SIZE), rotary_cosine, -rotary_sine
+        )
+        key_low = apply_rotary(
+            key_grad.reshape(2 * seq_rows, 1, HEAD_SIZE), rotary_cosine, -rotary_sine
+        )
+        qkv_low = jnp.concatenate(
+            [
+                query_low.astype(low).reshape(2 * seq_rows, group_width),
+                key_low.astype(low).reshape(2 * seq_rows, HEAD_SIZE),
+                value_grad,
+            ],
+            axis=1,
+        )
+        attn_in_grad = times_transposed(qkv_low, full_qkv)
+        state.attn_in_grad = attn_in_grad.astype(low)
+        rows = token_rows.astype(jnp.float32)
+        grad_gain_attn = jnp.sum(attn_in_grad * (rows * rms_scale(rows)), axis=0)
+        small_grads = jnp.concatenate([grad_gain_attn[:, None], take.small_two], axis=1)
+        grads = jnp.concatenate(
+            [
+                transposed_times(state.attn_input, qkv_low).astype(low),
+                transposed_times(attn_grad_low, state.heads_out).astype(low),
+                jnp.pad(small_grads.astype(low), ((0, 0), (0, -small_width % 128))),
+            ],
+            axis=1,
+        )
+        state.grads = with_layout_constraint(grads, Layout(major_to_minor=(0, 1)))
+
+    def split_grads():
+        grads = take.grads
+        return tuple(
+            join(
+                *(
+                    lax.dynamic_slice_in_dim(grads, carried(n, mine) * pack_rows, pack_rows, 0)
+                    for n in range(len(CARRIED[0]))
+                )
+            )
+            for mine in (True, False)
+        )
+
+    barrier()
+    middle_back()
+    state.whole = whole_of(take.attn_grad)
+    barrier()
+    whole_grad = state.whole
+    state.far = route(whole_grad, home_far)
+    state.near = route(whole_grad, home_near)
+    expert_grads(0)()
+    got, state.expert_grads[0] = meet(
+        launch(dict(out=(((3, 1), (2, 0)), ((15, 14), (13, 12))))), state.expert_grads[0]
+    )
+    settle(got)
+    barrier()
+    state.cross = route(state.far, home_near)
+    expert_grads(1)()
+    got, state.expert_grads[1] = meet(
+        launch(dict(out=(((11, 13), (10, 12)), ((7, 2), (5, 0))))), state.expert_grads[1]
+    )
+    settle(got)
+    state.shards_got = exchange_line(state.shards, (0, 4, 12))
+    barrier()
+    state.attn_grad = jnp.where(
+        home,
+        join(take.whole, take.far),
+        join(take.near, take.cross),
+    )
+    attention_back()
+    barrier()
+    kept_part, sent_part = split_grads()
+    state.total = plus(kept_part, swap(sent_part))
+    near_sum(take.attn_in_grad)
+    state.shards_got.update(exchange_line(take.shards, (8,)))
+    settle(launch(dict(out=(((9, 5), (8, 4)), ((10, 6), (8, 4))))))
+    expert_grads(2)()
+    barrier()
+    rows = state.total.shape[0] // 2
+    state.total = plus(state.total[:rows], route(state.total[rows:], plane_two))
+    state.own_sum = far_sum()
+    settle(launch(dict(out=((12, 8),))))
+    barrier()
+    settle(launch(dict(out=((8, 0), (4, 0)))))
+    shared_back = exchange_join(take.shards_got, me)
+    shared_back = shared_back.transpose(1, 0, 2).astype(jnp.float32)
+    state.shared_sums = [
+        shared_back[:, :, i * wide : i * wide + slice_width].reshape(width // sources, -1)
+        for i in range(3)
+    ]
+    rows = state.total.shape[0] // 2
+    state.total = plus(state.total[:rows], route(state.total[rows:], plane_one))
+    attn_in_grad = own_of(take.own_sum)
+    tokens_float = tokens_in.astype(jnp.float32)
+    scale_one = rms_scale(tokens_float)
+    normed_own = tokens_float * scale_one
+    state.grad_tokens = take.middle_grad + norm_back(
+        attn_in_grad, normed_own, scale_one, gain_one
+    )
+    barrier()
+    part_b = route(state.total[:pack_rows], pack_back_b).astype(jnp.float32)
+    part_a = route(state.total[pack_rows:], pack_back_a).astype(jnp.float32)
+    packs_back = (
+        jnp.where(parity_b == 0, part_b, part_a),
+        jnp.where(parity_b == 0, part_a, part_b),
+    )
+
+    grad_shared_gate, grad_shared_up, grad_shared_down = state.shared_sums
+    small_sum = sum(part[:, pack_width : pack_width + small_width] for part in packs_back)
+    small_sum = small_sum + swap(small_sum)
+    block_out = (state.middle + state.out[0].astype(jnp.float32)).astype(low)
+    cuts = (0, group_width, group_width + HEAD_SIZE, qkv_width, pack_width)
+    grad_query, grad_key, grad_value, grad_out_t = (
+        jnp.concatenate([part[:, start:stop] for part in packs_back], axis=1)
+        for start, stop in zip(cuts[:-1], cuts[1:], strict=True)
+    )
+    return (
+        block_out,
+        state.grad_tokens,
+        small_sum[:, 0],
+        grad_query,
+        grad_key,
+        grad_value,
+        grad_out_t.T,
+        small_sum[:, 1],
+        small_sum[:, 2:],
+        grad_shared_gate,
+        grad_shared_up,
+        grad_shared_down.T,
+        state.expert_grads[1],
+        state.expert_grads[2],
+        state.expert_grads[0],
+    )
+
+
 def solution(mesh):
+    wide = mesh.shape["fsdp"] == 16 and mesh.shape["tp"] == 2
     return jax.shard_map(
-        shards,
+        gathered_shards if wide else shards,
         mesh=mesh,
         in_specs=(
             P(("fsdp", "tp"), None),

time: 3390 us -> 972 us (0.29)
  waiting for transfers between devices: 2440 us -> 306 us
  blocking collectives: 402 us -> 0 us
  Pallas kernels: 0 us -> 173 us
  matrix products: 254 us -> 93.3 us
  starting transfers between devices: 24.1 us -> 150 us
  local copies, waits for them, and re-layouts: 163 us -> 114 us
  other arithmetic: 76.1 us -> 121 us
    reduce_scatter x8 -> x0, waiting for transfers between devices: 1370 us -> none  [the longest x1 285 us: shards(): lax.psum_scatter(grad_out, 'fsdp', scatter_dimension=1, tiled=True)]
    all_to_all x3 -> x1, waiting for transfers between devices: 573 us -> 1.52 us  [return_picks(): lax.all_to_all(picks[relative], 'fsdp', split_axis=0, concat_axis=0, tile...]
    all_gather x9 -> x0, waiting for transfers between devices: 496 us -> none  [the longest x1 260 us: shards(): lax.all_gather(w_shared_down, 'fsdp', axis=1, tiled=True)]
    ppermute x0 -> x104, waiting for transfers between devices: none -> 304 us  [the longest x49 199 us: hop(): return lax.ppermute(values, 'fsdp', [(i, i ^ bit) for i in range(count)])]
    all_to_all x1 -> x0, blocking collectives: 232 us -> none  [shards(): lax.all_to_all(send_rows, 'fsdp', split_axis=0, concat_axis=0, tiled=True)]
    pallas_call x0 -> x9, Pallas kernels: none -> 173 us  [the longest x8 148 us: expert_call(): pl.pallas_call(lambda *refs: expert_kernel(first, number, starts, *refs),...]
    ppermute x0 -> x104, starting transfers between devices: none -> 144 us  [the longest x49 83.9 us: hop(): return lax.ppermute(values, 'fsdp', [(i, i ^ bit) for i in range(count)])]
    unnamed x2 -> x0, blocking collectives: 136 us -> none
  transfers between devices with their start and end apart: 24 -> 105, of which waited for: 13 -> 34; matrix products, arithmetic and copies ran while one was open for 13% -> 24% of each run, Pallas kernels for 0% -> 18%
where the time goes in v2:
time: 972 us; the launch traced here: 961 us
  waiting for transfers between devices  306 us (31%)
  Pallas kernels  173 us (18%)
  starting transfers between devices  150 us (15%)
  other arithmetic  121 us (12%)
  local copies, waits for them, and re-layouts  114 us (12%)
  matrix products  93.3 us (10%)
    ppermute x49, waiting for transfers between devices, hop(): return lax.ppermute(values, 'fsdp', [(i, i ^ bit) for i in range(count)])  199 us
    pallas_call x8, Pallas kernels, expert_call(): pl.pallas_call(lambda *refs: expert_kernel(first, number, starts, *refs),...  148 us
    ppermute x28, waiting for transfers between devices, route(): return lax.ppermute(values, ('fsdp', 'tp'), pairs)  104 us
    ppermute x49, starting transfers between devices, hop(): return lax.ppermute(values, 'fsdp', [(i, i ^ bit) for i in range(count)])  83.9 us
    dot_general x8, matrix products, transposed_times(): lax.dot_general(left_mat, right_mat, (((0,), (0,)), ((), ())), preferred_...  63.6 us
    ppermute x28, starting transfers between devices, route(): return lax.ppermute(values, ('fsdp', 'tp'), pairs)  48.8 us
    convert_element_type x26, other arithmetic, plus(): (left.astype(jnp.float32) + right.astype(jnp.float32)).astype(jnp.bfloat16)  44.5 us
    unnamed x379, local copies, waits for them, and re-layouts  41.4 us
  transfers between devices with their start and end apart: 105, of which 34 were waited for; matrix products, arithmetic and copies ran while one was open for 24% of the time, Pallas kernels for 18%

profile of v2, /device:TPU:10, one launch (start us, length us, event | category | flops | bytes accessed | tf_op | source)
XLA Modules:
  0.0 961.3 jit_solution(3573856630530474925)
XLA Ops:
  63.8 18.4 %collective-permute-done.4 = bf16[320,1664]{1,0:T(8,128)(2,1)S(1)} collective-permute-done((bf16[320,1664]{1,0:T(8,128)(2,1)S(1)}, bf16[320,1664]{1,0:T(8,128)(2,1)S(1)}, u32[]{:S(2)}, u32[]{:S(2)}) %collective-permute-start.4) | collective-permute-done | bytes 1064992 | tf_op jit(solution)/shard_map/ppermute | solution.py:415
  99.5 18.2 %collective-permute-done.13 = bf16[4,160,384]{2,1,0:T(8,128)(2,1)} collective-permute-done((bf16[4,160,384]{2,1,0:T(8,128)(2,1)}, bf16[4,160,384]{2,1,0:T(8,128)(2,1)}, u32[]{:S(2)}, u32[]{:S(2)}) %collective-permute-start.13) | collective-permute-done | bytes 491552 | tf_op jit(solution)/shard_map/ppermute | solution.py:401
  161.8 16.5 %collective-permute-done.16 = bf16[4,160,384]{2,1,0:T(8,128)(2,1)} collective-permute-done((bf16[4,160,384]{2,1,0:T(8,128)(2,1)}, bf16[4,160,384]{2,1,0:T(8,128)(2,1)}, u32[]{:S(2)}, u32[]{:S(2)}) %collective-permute-start.16) | collective-permute-done | bytes 491552 | tf_op jit(solution)/shard_map/ppermute | solution.py:401
  209.0 14.0 %collective-permute-done.18 = bf16[256,2560]{1,0:T(8,128)(2,1)S(1)} collective-permute-done((bf16[256,2560]{1,0:T(8,128)(2,1)S(1)}, bf16[256,2560]{1,0:T(8,128)(2,1)S(1)}, u32[]{:S(2)}, u32[]{:S(2)}) %collective-permute-start.18) | collective-permute-done | bytes 1310752 | tf_op jit(solution)/shard_map/ppermute | solution.py:415
  237.0 22.8 %collective-permute-done.23 = bf16[4,160,384]{2,1,0:T(8,128)(2,1)S(1)} collective-permute-done((bf16[4,160,384]{2,1,0:T(8,128)(2,1)}, bf16[4,160,384]{2,1,0:T(8,128)(2,1)S(1)}, u32[]{:S(2)}, u32[]{:S(2)}) %collective-permute-start.23) | collective-permute-done | bytes 491552 | tf_op jit(solution)/shard_map/ppermute | solution.py:401
  325.7 20.7 %expert_pass.8 = (bf16[2048,2560]{1,0:T(8,128)(2,1)}, bf16[2048,2560]{1,0:T(8,128)(2,1)}, bf16[2048,768]{1,0:T(8,128)(2,1)S(1)}, bf16[2048,1536]{1,0:T(8,128)(2,...) custom-call(s32[2]{0:T(128)S(1)} %pad_add_fusion.refs_0_, ...), custom_call_target="tpu_custom_call" | custom-call | flops 6710886400 | bytes 25165824 | tf_op jit(solution)/shard_map/expert_pass/pallas_call | solution.py:750
  373.9 20.3 %expert_pass.9 = (bf16[2048,2560]{1,0:T(8,128)(2,1)}, bf16[2048,2560]{1,0:T(8,128)(2,1)}, bf16[2048,768]{1,0:T(8,128)(2,1)}, bf16[2048,1536]{1,0:T(8,128)(2,1)},...) custom-call(s32[2]{0:T(128)S(1)} %pad_add_fusion.refs_0_, ...), custom_call_target="tpu_custom_call", output_to_operand_aliasing={{0}: (14, {}), {1}: (15, {}), {2}: (16, {}), {3}: (17, {}),... | custom-call | flops 6710886400 | bytes 25165824 | tf_op jit(solution)/shard_map/expert_pass/pallas_call | solution.py:750
  404.3 20.8 %expert_pass.10 = (bf16[2048,2560]{1,0:T(8,128)(2,1)}, bf16[2048,2560]{1,0:T(8,128)(2,1)}, bf16[2048,768]{1,0:T(8,128)(2,1)}, bf16[2048,1536]{1,0:T(8,128)(2,1)}...) custom-call(s32[2]{0:T(128)S(1)} %pad_add_fusion.refs_0_, ...), custom_call_target="tpu_custom_call", output_to_operand_aliasing={{0}: (14, {}), {1}: (15, {}), {2}: (16, {}), {3}: (17, {}),... | custom-call | flops 6710886400 | bytes 25165824 | tf_op jit(solution)/shard_map/expert_pass/pallas_call | solution.py:750
  435.7 17.5 %expert_pass.11 = (bf16[2048,2560]{1,0:T(8,128)(2,1)}, bf16[2048,2560]{1,0:T(8,128)(2,1)}, bf16[2048,768]{1,0:T(8,128)(2,1)S(1)}, bf16[2048,1536]{1,0:T(8,128)(2...) custom-call(s32[2]{0:T(128)S(1)} %pad_add_fusion.refs_0_, ...), custom_call_target="tpu_custom_call", output_to_operand_aliasing={{0}: (14, {}), {1}: (15, {}), {2}: (16, {}), {3}: (17, {}),... | custom-call | flops 6710886400 | bytes 25165824 | tf_op jit(solution)/shard_map/expert_pass/pallas_call | solution.py:750
  460.8 17.2 %expert_pass.12 = (bf16[2048,2560]{1,0:T(8,128)(2,1)}, bf16[2048,2560]{1,0:T(8,128)(2,1)}, bf16[2048,768]{1,0:T(8,128)(2,1)S(1)}, bf16[2048,1536]{1,0:T(8,128)(2...) custom-call(s32[2]{0:T(128)S(1)} %pad_add_fusion.refs_0_, ...), custom_call_target="tpu_custom_call", output_to_operand_aliasing={{0}: (14, {}), {1}: (15, {}), {2}: (16, {}), {3}: (17, {}),... | custom-call | flops 6710886400 | bytes 25165824 | tf_op jit(solution)/shard_map/expert_pass/pallas_call | solution.py:750
  488.8 16.0 %expert_pass.13 = (bf16[2048,2560]{1,0:T(8,128)(2,1)}, bf16[2048,2560]{1,0:T(8,128)(2,1)}, bf16[2048,768]{1,0:T(8,128)(2,1)}, bf16[2048,1536]{1,0:T(8,128)(2,1)}...) custom-call(s32[2]{0:T(128)S(1)} %pad_add_fusion.refs_0_, ...), custom_call_target="tpu_custom_call", output_to_operand_aliasing={{0}: (14, {}), {1}: (15, {}), {2}: (16, {}), {3}: (17, {}),... | custom-call | flops 6710886400 | bytes 25165824 | tf_op jit(solution)/shard_map/expert_pass/pallas_call | solution.py:750
  508.5 19.6 %expert_pass.14 = (bf16[2048,2560]{1,0:T(8,128)(2,1)}, bf16[2048,2560]{1,0:T(8,128)(2,1)}, bf16[2048,768]{1,0:T(8,128)(2,1)}, bf16[2048,1536]{1,0:T(8,128)(2,1)}...) custom-call(s32[2]{0:T(128)S(1)} %pad_add_fusion.refs_0_, ...), custom_call_target="tpu_custom_call", output_to_operand_aliasing={{0}: (14, {}), {1}: (15, {}), {2}: (16, {}), {3}: (17, {}),... | custom-call | flops 6710886400 | bytes 25165824 | tf_op jit(solution)/shard_map/expert_pass/pallas_call | solution.py:750
  531.8 15.8 %expert_pass.15 = (bf16[2048,2560]{1,0:T(8,128)(2,1)}, bf16[2048,2560]{1,0:T(8,128)(2,1)}, bf16[2048,768]{1,0:T(8,128)(2,1)}, bf16[2048,1536]{1,0:T(8,128)(2,1)}...) custom-call(s32[2]{0:T(128)S(1)} %pad_add_fusion.refs_0_, ...), custom_call_target="tpu_custom_call", output_to_operand_aliasing={{0}: (14, {}), {1}: (15, {}), {2}: (16, {}), {3}: (17, {}),... | custom-call | flops 6710886400 | bytes 25165824 | tf_op jit(solution)/shard_map/expert_pass/pallas_call | solution.py:750
  551.0 24.7 %expert_outputs.1 = (bf16[2048,2560]{1,0:T(8,128)(2,1)}, bf16[2048,2560]{1,0:T(8,128)(2,1)}) custom-call(f32[8,2,256]{2,1,0:T(2,128)S(1)} %get-tuple-element.1713.place_ref, f32[8,2,256]{2,1,0:T(2,128)S(1)} %get-tuple-element.1712.gate_ref, bf16[2048,768]{1,0:T(8,128)(2,1)S(1)} %copy-done.5, bf16[4096,384]{1,0:T(8,128)(2,1)} %get-tuple-element.1209.shared_ref, ...), custom_call_target="tpu_custom_call" | custom-call | flops 13421772800 | bytes 33554432 | tf_op jit(solution)/shard_map/expert_outputs/pallas_call | solution.py:815
  586.8 11.1 %convolution_convert_fusion.3 = bf16[2560,256]{1,0:T(8,128)(2,1)} fusion(bf16[4096,2560]{1,0:T(8,128)(2,1)} %get-tuple-element.1208, bf16[4096,384]{1,0:T(8,128)(2,1)S(1)} %copy-done.8), kind=kOutput, calls=%fused_computation.34 | convolution fusion | flops 5369364480 | bytes 24379392 | tf_op jit(solution)/shard_map/dot_general | solution.py:70
  597.8 10.8 %convolution_convert_fusion.4 = bf16[2560,128]{1,0:T(8,128)(2,1)} fusion(bf16[4096,2560]{1,0:T(8,128)(2,1)} %get-tuple-element.1210, bf16[4096,384]{1,0:T(8,128)(2,1)S(1)} %copy-done.8), kind=kOutput, calls=%fused_computation.36 | convolution fusion | flops 2684682240 | bytes 22675456 | tf_op jit(solution)/shard_map/dot_general | solution.py:70
  676.9 10.9 %convolution_bitcast_fusion.2 = f32[1,768,2560]{2,1,0:T(8,128)} fusion(bf16[2048,768]{1,0:T(8,128)(2,1)S(1)} %copy-done.5, bf16[2048,2560]{1,0:T(8,128)(2,1)S(1)} %bitcast.251), kind=kOutput, calls=%fused_computation.15 | convolution fusion | flops 8053063680 | bytes 21495808 | tf_op jit(solution)/shard_map/dot_general | solution.py:70
  687.8 14.5 %collective-permute-done.79 = bf16[256,2560]{1,0:T(8,128)(2,1)} collective-permute-done((bf16[256,2560]{1,0:T(8,128)(2,1)S(1)}, bf16[256,2560]{1,0:T(8,128)(2,1)}, u32[]{:S(2)}, u32[]{:S(2)}) %collective-permute-start.79) | collective-permute-done | bytes 1310752 | tf_op jit(solution)/shard_map/ppermute | solution.py:401
  715.9 11.3 %convolution_bitcast_fusion.1 = f32[1,2560,768]{2,1,0:T(8,128)} fusion(bf16[2048,2560]{1,0:T(8,128)(2,1)S(1)} %bitcast.247, bf16[2048,1536]{1,0:T(8,128)(2,1)S(1)} %bitcast.253), kind=kOutput, calls=%fused_computation.14 | convolution fusion | flops 8053063680 | bytes 21495808 | tf_op jit(solution)/shard_map/dot_general | solution.py:70
  727.2 12.1 %collective-permute-done.84 = bf16[256,2560]{1,0:T(8,128)(2,1)S(1)} collective-permute-done((bf16[256,2560]{1,0:T(8,128)(2,1)S(1)}, bf16[256,2560]{1,0:T(8,128)(2,1)S(1)}, u32[]{:S(2)}, u32[]{:S(2)}) %collective-permute-start.84) | collective-permute-done | bytes 1310752 | tf_op jit(solution)/shard_map/ppermute | solution.py:401
  804.6 10.9 %convolution_bitcast_fusion = f32[1,2560,768]{2,1,0:T(8,128)} fusion(bf16[2048,2560]{1,0:T(8,128)(2,1)S(1)} %bitcast.249, bf16[2048,1536]{1,0:T(8,128)(2,1)S(1)} %bitcast.255), kind=kOutput, calls=%fused_computation.13 | convolution fusion | flops 8053063680 | bytes 21495808 | tf_op jit(solution)/shard_map/dot_general | solution.py:70
  815.5 17.3 %collective-permute-done.90 = bf16[256,2560]{1,0:T(8,128)(2,1)} collective-permute-done((bf16[256,2560]{1,0:T(8,128)(2,1)}, bf16[256,2560]{1,0:T(8,128)(2,1)}, u32[]{:S(2)}, u32[]{:S(2)}) %collective-permute-start.90) | collective-permute-done | bytes 1310752 | tf_op jit(solution)/shard_map/ppermute | solution.py:401
  858.8 19.0 %collective-permute-done.94 = bf16[128,2560]{1,0:T(8,128)(2,1)S(1)} collective-permute-done((bf16[128,2560]{1,0:T(8,128)(2,1)S(1)}, bf16[128,2560]{1,0:T(8,128)(2,1)S(1)}, u32[]{:S(2)}, u32[]{:S(2)}) %collective-permute-start.94) | collective-permute-done | bytes 655392 | tf_op jit(solution)/shard_map/ppermute | solution.py:401
  936.9 18.9 %collective-permute-done.102 = bf16[160,1664]{1,0:T(8,128)(2,1)S(1)} collective-permute-done((bf16[160,1664]{1,0:T(8,128)(2,1)S(1)}, bf16[160,1664]{1,0:T(8,128)(2,1)S(1)}, u32[]{:S(2)}, u32[]{:S(2)}) %collective-permute-start.102) | collective-permute-done | bytes 532512 | tf_op jit(solution)/shard_map/ppermute | solution.py:415
  (855 shorter events, 557.6 us)
Async XLA Ops:
  29.6 52.8 %collective-permute-start.5 = (bf16[272,2560]{1,0:T(8,128)(2,1)}, bf16[272,2560]{1,0:T(8,128)(2,1)}, u32[]{:S(2)}, u32[]{:S(2)}) collective-permute-start(bf16[272,2560]{1,0:T(8,128)(2,1)} %fusion.32), channel_id=1, source_target_pairs={{0,16},{2,18},{4,20},{6,22},{9,25},{11,27},{13,29},{15,31},{16,0},... | collective-permute-start | bytes 4177928 | tf_op jit(solution)/shard_map/ppermute | solution.py:415
  31.3 51.1 %collective-permute-start.6 = (bf16[272,2560]{1,0:T(8,128)(2,1)}, bf16[272,2560]{1,0:T(8,128)(2,1)}, u32[]{:S(2)}, u32[]{:S(2)}) collective-permute-start(bf16[272,2560]{1,0:T(8,128)(2,1)} %fusion.32), channel_id=1, source_target_pairs={{0,8},{2,10},{4,12},{6,14},{9,1},{11,3},{13,5},{15,7},{16,24},{18,... | collective-permute-start | bytes 4177928 | tf_op jit(solution)/shard_map/ppermute | solution.py:415
  82.4 35.3 %collective-permute-start.11 = (bf16[640,1664]{1,0:T(8,128)(2,1)S(1)}, bf16[640,1664]{1,0:T(8,128)(2,1)}, u32[]{:S(2)}, u32[]{:S(2)}) collective-permute-start(bf16[640,1664]{1,0:T(8,128)(2,1)S(1)} %pad_maximum_fusion.6), channel_id=1, source_target_pairs={{0,1},{1,0},{2,3},{3,2},{4,5},{5,4},{6,7},{7,6},{8,9},{9,8},{10,11... | collective-permute-start | bytes 6389768 | tf_op jit(solution)/shard_map/ppermute | solution.py:405
  121.6 56.8 %collective-permute-start.15 = (bf16[256,2560]{1,0:T(8,128)(2,1)}, bf16[256,2560]{1,0:T(8,128)(2,1)}, u32[]{:S(2)}, u32[]{:S(2)}) collective-permute-start(bf16[256,2560]{1,0:T(8,128)(2,1)} %maximum_select_fusion.2), channel_id=1, source_target_pairs={{0,16},{1,9},{2,18},{3,11},{4,20},{5,13},{6,22},{7,15},{8,24},{9,1... | collective-permute-start | bytes 3932168 | tf_op jit(solution)/shard_map/ppermute | solution.py:415
  128.5 49.9 %collective-permute-start.16 = (bf16[4,160,384]{2,1,0:T(8,128)(2,1)}, bf16[4,160,384]{2,1,0:T(8,128)(2,1)}, u32[]{:S(2)}, u32[]{:S(2)}) collective-permute-start(bf16[4,160,384]{2,1,0:T(8,128)(2,1)} %pad_maximum_fusion.27), channel_id=1, source_target_pairs={{0,16},{2,18},{4,20},{6,22},{8,24},{10,26},{12,28},{14,30},{16,0},... | collective-permute-start | bytes 1474568 | tf_op jit(solution)/shard_map/ppermute | solution.py:401
  184.2 38.9 %collective-permute-start.18 = (bf16[256,2560]{1,0:T(8,128)(2,1)S(1)}, bf16[256,2560]{1,0:T(8,128)(2,1)S(1)}, u32[]{:S(2)}, u32[]{:S(2)}) collective-permute-start(bf16[256,2560]{1,0:T(8,128)(2,1)S(1)} %get-tuple-element.1594), channel_id=1, source_target_pairs={{1,9},{3,11},{5,13},{7,15},{8,0},{10,2},{12,4},{14,6},{17,25},{19,... | collective-permute-start | bytes 3932168 | tf_op jit(solution)/shard_map/ppermute | solution.py:415
  225.6 34.2 %collective-permute-start.20 = (bf16[512,2560]{1,0:T(8,128)(2,1)}, bf16[512,2560]{1,0:T(8,128)(2,1)}, u32[]{:S(2)}, u32[]{:S(2)}) collective-permute-start(bf16[512,2560]{1,0:T(8,128)(2,1)} %maximum_select_fusion.refs_5_.refs_7_), channel_id=1, source_target_pairs={{0,1},{1,0},{2,3},{3,2},{4,5},{5,4},{6,7},{7,6},{8,9},{9,8},{10,11... | collective-permute-start | bytes 7864328 | tf_op jit(solution)/shard_map/ppermute | solution.py:405
  225.6 34.2 %collective-permute-start.21 = (bf16[512,2560]{1,0:T(8,128)(2,1)}, bf16[512,2560]{1,0:T(8,128)(2,1)S(1)}, u32[]{:S(2)}, u32[]{:S(2)}) collective-permute-start(bf16[512,2560]{1,0:T(8,128)(2,1)} %maximum_select_fusion.refs_5_.refs_7_), channel_id=1, source_target_pairs={{0,2},{1,5},{2,0},{3,7},{4,6},{5,1},{6,4},{7,3},{8,10},{9,13},{10,... | collective-permute-start | bytes 7864328 | tf_op jit(solution)/shard_map/ppermute | solution.py:415
  262.5 39.9 %collective-permute-start.25 = (bf16[512,2560]{1,0:T(8,128)(2,1)}, bf16[512,2560]{1,0:T(8,128)(2,1)}, u32[]{:S(2)}, u32[]{:S(2)}) collective-permute-start(bf16[512,2560]{1,0:T(8,128)(2,1)} %maximum_select_fusion.refs_5_.refs_7_), channel_id=1, source_target_pairs={{0,4},{1,3},{2,6},{3,1},{4,0},{5,7},{6,2},{7,5},{8,12},{9,11},{10,... | collective-permute-start | bytes 7864328 | tf_op jit(solution)/shard_map/ppermute | solution.py:415
  317.8 43.6 %collective-permute-start.36 = (bf16[512,2560]{1,0:T(8,128)(2,1)S(1)}, bf16[512,2560]{1,0:T(8,128)(2,1)S(1)}, u32[]{:S(2)}, u32[]{:S(2)}) collective-permute-start(bf16[512,2560]{1,0:T(8,128)(2,1)S(1)} %copy-done.12), channel_id=1, source_target_pairs={{0,1},{1,0},{2,3},{3,2},{4,5},{5,4},{6,7},{7,6},{8,9},{9,8},{10,11... | collective-permute-start | bytes 7864328 | tf_op jit(solution)/shard_map/ppermute | solution.py:405
  319.9 33.6 %collective-permute-start.31 = (bf16[256,2560]{1,0:T(8,128)(2,1)}, bf16[256,2560]{1,0:T(8,128)(2,1)S(1)}, u32[]{:S(2)}, u32[]{:S(2)}) collective-permute-start(bf16[256,2560]{1,0:T(8,128)(2,1)} %get-tuple-element.1590), channel_id=1, source_target_pairs={{0,4},{1,3},{2,6},{3,1},{4,0},{5,7},{6,2},{7,5},{8,12},{9,11},{10,... | collective-permute-start | bytes 3932168 | tf_op jit(solution)/shard_map/ppermute | solution.py:415
  354.2 40.0 %collective-permute-start.35 = (bf16[256,2560]{1,0:T(8,128)(2,1)}, bf16[256,2560]{1,0:T(8,128)(2,1)}, u32[]{:S(2)}, u32[]{:S(2)}) collective-permute-start(bf16[256,2560]{1,0:T(8,128)(2,1)} %get-tuple-element.869), channel_id=1, source_target_pairs={{0,1},{1,0},{2,3},{3,2},{4,5},{5,4},{6,7},{7,6},{8,9},{9,8},{10,11... | collective-permute-start | bytes 3932168 | tf_op jit(solution)/shard_map/ppermute | solution.py:405
  358.1 46.1 %collective-permute-start.42 = (bf16[432,2560]{1,0:T(8,128)(2,1)}, bf16[432,2560]{1,0:T(8,128)(2,1)S(1)}, u32[]{:S(2)}, u32[]{:S(2)}) collective-permute-start(bf16[432,2560]{1,0:T(8,128)(2,1)} %pad_maximum_fusion.2), channel_id=1, source_target_pairs={{0,1},{1,0},{2,3},{3,2},{4,5},{5,4},{6,7},{7,6},{8,9},{9,8},{10,11... | collective-permute-start | bytes 6635528 | tf_op jit(solution)/shard_map/ppermute | solution.py:405
  358.2 36.0 %collective-permute-start.39 = (bf16[144,2560]{1,0:T(8,128)(2,1)S(1)}, bf16[144,2560]{1,0:T(8,128)(2,1)S(1)}, u32[]{:S(2)}, u32[]{:S(2)}) collective-permute-start(bf16[144,2560]{1,0:T(8,128)(2,1)S(1)} %collective-permute-done.27.refs_1_), channel_id=1, source_target_pairs={{0,8},{2,10},{4,12},{6,14},{8,0},{10,2},{12,4},{14,6},{16,24},{18,... | collective-permute-start | bytes 2211848 | tf_op jit(solution)/shard_map/ppermute | solution.py:401
  584.0 41.3 %collective-permute-start.72 = (bf16[2048,2560]{1,0:T(8,128)(2,1)}, bf16[2048,2560]{1,0:T(8,128)(2,1)}, u32[]{:S(2)}, u32[]{:S(2)}) collective-permute-start(bf16[2048,2560]{1,0:T(8,128)(2,1)} %get-tuple-element.1232), channel_id=1, source_target_pairs={{0,1},{1,0},{2,3},{3,2},{4,5},{5,4},{6,7},{7,6},{8,9},{9,8},{10,11... | collective-permute-start | bytes 31457288 | tf_op jit(solution)/shard_map/ppermute | solution.py:405
  584.1 36.4 %collective-permute-start.69 = (bf16[128,2560]{1,0:T(8,128)(2,1)}, bf16[128,2560]{1,0:T(8,128)(2,1)}, u32[]{:S(2)}, u32[]{:S(2)}) collective-permute-start(bf16[128,2560]{1,0:T(8,128)(2,1)} %get-tuple-element.1205), channel_id=1, source_target_pairs={{0,16},{2,18},{4,20},{6,22},{8,24},{10,26},{12,28},{14,30},{16,0},... | collective-permute-start | bytes 1966088 | tf_op jit(solution)/shard_map/ppermute | solution.py:401
  585.3 35.2 %collective-permute-start.70 = (bf16[256,2560]{1,0:T(8,128)(2,1)}, bf16[256,2560]{1,0:T(8,128)(2,1)}, u32[]{:S(2)}, u32[]{:S(2)}) collective-permute-start(bf16[256,2560]{1,0:T(8,128)(2,1)} %pad_maximum_fusion.9), channel_id=1, source_target_pairs={{0,2},{2,0},{4,6},{6,4},{8,10},{10,8},{12,14},{14,12},{16,18},{18,... | collective-permute-start | bytes 3932168 | tf_op jit(solution)/shard_map/ppermute | solution.py:401
  673.6 33.4 %collective-permute-start.81 = (bf16[256,2560]{1,0:T(8,128)(2,1)S(1)}, bf16[256,2560]{1,0:T(8,128)(2,1)}, u32[]{:S(2)}, u32[]{:S(2)}) collective-permute-start(bf16[256,2560]{1,0:T(8,128)(2,1)S(1)} %maximum_select_fusion.4), channel_id=1, source_target_pairs={{0,16},{2,18},{4,20},{6,22},{9,25},{11,27},{13,29},{15,31},{16,0},... | collective-permute-start | bytes 3932168 | tf_op jit(solution)/shard_map/ppermute | solution.py:415
  707.8 36.7 %collective-permute-start.83 = (bf16[256,2560]{1,0:T(8,128)(2,1)}, bf16[256,2560]{1,0:T(8,128)(2,1)}, u32[]{:S(2)}, u32[]{:S(2)}) collective-permute-start(bf16[256,2560]{1,0:T(8,128)(2,1)} %collective-permute-done.81), channel_id=1, source_target_pairs={{0,8},{2,10},{4,12},{6,14},{9,1},{11,3},{13,5},{15,7},{16,24},{18,... | collective-permute-start | bytes 3932168 | tf_op jit(solution)/shard_map/ppermute | solution.py:415
  783.7 54.4 %collective-permute-start.91 = (bf16[256,2560]{1,0:T(8,128)(2,1)}, bf16[256,2560]{1,0:T(8,128)(2,1)}, u32[]{:S(2)}, u32[]{:S(2)}) collective-permute-start(bf16[256,2560]{1,0:T(8,128)(2,1)} %get-tuple-element.1585), channel_id=1, source_target_pairs={{1,9},{3,11},{5,13},{7,15},{8,0},{10,2},{12,4},{14,6},{17,25},{19,... | collective-permute-start | bytes 3932168 | tf_op jit(solution)/shard_map/ppermute | solution.py:415
  790.4 47.7 %collective-permute-start.88 = (bf16[256,2560]{1,0:T(8,128)(2,1)}, bf16[256,2560]{1,0:T(8,128)(2,1)}, u32[]{:S(2)}, u32[]{:S(2)}) collective-permute-start(bf16[256,2560]{1,0:T(8,128)(2,1)} %get-tuple-element.1586), channel_id=1, source_target_pairs={{1,9},{3,11},{5,13},{7,15},{8,0},{10,2},{12,4},{14,6},{17,25},{19,... | collective-permute-start | bytes 3932168 | tf_op jit(solution)/shard_map/ppermute | solution.py:415
  800.2 41.3 %collective-permute-start.93 = (bf16[1280,1664]{1,0:T(8,128)(2,1)}, bf16[1280,1664]{1,0:T(8,128)(2,1)S(1)}, u32[]{:S(2)}, u32[]{:S(2)}) collective-permute-start(bf16[1280,1664]{1,0:T(8,128)(2,1)} %get-tuple-element.1563), channel_id=1, source_target_pairs={{0,1},{1,0},{2,3},{3,2},{4,5},{5,4},{6,7},{7,6},{8,9},{9,8},{10,11... | collective-permute-start | bytes 12779528 | tf_op jit(solution)/shard_map/ppermute | solution.py:405
  885.9 41.8 %collective-permute-start.97 = (f32[128,2560]{1,0:T(8,128)}, f32[128,2560]{1,0:T(8,128)}, u32[]{:S(2)}, u32[]{:S(2)}) collective-permute-start(f32[128,2560]{1,0:T(8,128)} %constant_dynamic-slice_fusion), channel_id=1, source_target_pairs={{0,1},{2,3},{4,5},{6,7},{9,8},{11,10},{13,12},{15,14},{16,17},{18,... | collective-permute-start | bytes 3932168 | tf_op jit(solution)/shard_map/ppermute | solution.py:415
  887.3 33.4 %collective-permute-start.99 = (bf16[128,2560]{1,0:T(8,128)(2,1)}, bf16[128,2560]{1,0:T(8,128)(2,1)}, u32[]{:S(2)}, u32[]{:S(2)}) collective-permute-start(bf16[128,2560]{1,0:T(8,128)(2,1)} %get-tuple-element.1441), channel_id=1, source_target_pairs={{0,8},{2,10},{4,12},{6,14},{8,0},{10,2},{12,4},{14,6},{16,24},{18,... | collective-permute-start | bytes 1966088 | tf_op jit(solution)/shard_map/ppermute | solution.py:401
  (255 other events, 3947.4 us)

commit v3 on v2

--- a/solution.py
+++ b/solution.py
@@ -771,7 +771,7 @@
             pltpu.SemaphoreType.DMA((11,)),
         ],
         input_output_aliases=aliases,
-        compiler_params=pltpu.CompilerParams(vmem_limit_bytes=36 * 1024 * 1024),
+        compiler_params=pltpu.CompilerParams(vmem_limit_bytes=40 * 1024 * 1024),
         cost_estimate=pl.CostEstimate(
             flops=4 * slots * width * (5 * hidden + 10 * slots),
             bytes_accessed=24 * 1024 * 1024,
@@ -1221,10 +1221,9 @@
         ((), dict(back=((13, 12), (7, 3)))),
     )
     fresh = []
+    state.cot_lasts = {}
     for number, (arrived, moves) in enumerate(plan):
         barrier()
-        if number in (1, 2):
-            cot_last = take.cot_last
         if state.back_other:
             fresh = swap_back()
         if arrived:
@@ -1232,15 +1231,16 @@
         if number == 0:
             swapped()
             cot_parts[1] = (cot_first, swap(cot_first))
-        if number == 1:
+        if number == 4:
             cot_third = take.cot_third
             cot_parts[2] = (cot_third, swap(cot_third))
         if number in (0, 1):
-            state.cot_last = route(
+            state.cot_lasts[number] = route(
                 cot_first[number * seq_rows : (number + 1) * seq_rows], plane_two
             )
-        if number in (1, 2):
-            cot_parts[number + 2] = (cot_last, swap(cot_last))
+        if number in (2, 3):
+            cot_last = state.cot_lasts.pop(3 - number)
+            cot_parts[6 - number] = (cot_last, swap(cot_last))
         experts_of(number)()
         got, state.notes[number] = meet(launch(moves), state.notes[number])
         settle(got)

time: 972 us -> 965 us (level)
  waiting for transfers between devices: 306 us -> 293 us
    ppermute x49, waiting for transfers between devices: 199 us -> 185 us  [hop(): return lax.ppermute(values, 'fsdp', [(i, i ^ bit) for i in range(count)])]
    dynamic_update_slice x16, local copies, waits for them, and re-layouts: 9.32 us -> 21.8 us  [gathered_shards(): lax.dynamic_update_slice_in_dim(full_weights, block, carried(number, mine...]
    unnamed x379 -> x355, local copies, waits for them, and re-layouts: 41.4 us -> 33 us
  transfers between devices with their start and end apart: 105 -> 105, of which waited for: 34 -> 36; matrix products, arithmetic and copies ran while one was open for 24% -> 27% of each run, Pallas kernels for 18% -> 17%
where the time goes in v3:
time: 965 us; the launch traced here: 954 us
  waiting for transfers between devices  293 us (30%)
  Pallas kernels  164 us (17%)
  starting transfers between devices  151 us (16%)
  other arithmetic  127 us (13%)
  local copies, waits for them, and re-layouts  122 us (13%)
  matrix products  94.4 us (10%)
    ppermute x49, waiting for transfers between devices, hop(): return lax.ppermute(values, 'fsdp', [(i, i ^ bit) for i in range(count)])  185 us
    pallas_call x8, Pallas kernels, expert_call(): pl.pallas_call(lambda *refs: expert_kernel(first, number, starts, *refs),...  139 us
    ppermute x28, waiting for transfers between devices, route(): return lax.ppermute(values, ('fsdp', 'tp'), pairs)  105 us
    ppermute x49, starting transfers between devices, hop(): return lax.ppermute(values, 'fsdp', [(i, i ^ bit) for i in range(count)])  82.8 us
    dot_general x8, matrix products, transposed_times(): lax.dot_general(left_mat, right_mat, (((0,), (0,)), ((), ())), preferred_...  61.6 us
    ppermute x28, starting transfers between devices, route(): return lax.ppermute(values, ('fsdp', 'tp'), pairs)  49.3 us
    convert_element_type x26, other arithmetic, plus(): (left.astype(jnp.float32) + right.astype(jnp.float32)).astype(jnp.bfloat16)  48.3 us
    unnamed x355, local copies, waits for them, and re-layouts  33 us
  transfers between devices with their start and end apart: 105, of which 36 were waited for; matrix products, arithmetic and copies ran while one was open for 27% of the time, Pallas kernels for 17%

profile of v3, /device:TPU:10, one launch (start us, length us, event | category | flops | bytes accessed | tf_op | source)
XLA Modules:
  0.0 954.4 jit_solution(3837932180541129404)
XLA Ops:
  63.8 18.4 %collective-permute-done.4 = bf16[320,1664]{1,0:T(8,128)(2,1)S(1)} collective-permute-done((bf16[320,1664]{1,0:T(8,128)(2,1)S(1)}, bf16[320,1664]{1,0:T(8,128)(2,1)S(1)}, u32[]{:S(2)}, u32[]{:S(2)}) %collective-permute-start.4) | collective-permute-done | bytes 1064992 | tf_op jit(solution)/shard_map/ppermute | solution.py:415
  99.4 18.3 %collective-permute-done.13 = bf16[4,160,384]{2,1,0:T(8,128)(2,1)} collective-permute-done((bf16[4,160,384]{2,1,0:T(8,128)(2,1)}, bf16[4,160,384]{2,1,0:T(8,128)(2,1)}, u32[]{:S(2)}, u32[]{:S(2)}) %collective-permute-start.13) | collective-permute-done | bytes 491552 | tf_op jit(solution)/shard_map/ppermute | solution.py:401
  187.9 11.5 %collective-permute-done.17 = bf16[256,2560]{1,0:T(8,128)(2,1)S(1)} collective-permute-done((bf16[256,2560]{1,0:T(8,128)(2,1)}, bf16[256,2560]{1,0:T(8,128)(2,1)S(1)}, u32[]{:S(2)}, u32[]{:S(2)}) %collective-permute-start.17) | collective-permute-done | bytes 1310752 | tf_op jit(solution)/shard_map/ppermute | solution.py:415
  213.3 14.0 %collective-permute-done.18 = bf16[256,2560]{1,0:T(8,128)(2,1)S(1)} collective-permute-done((bf16[256,2560]{1,0:T(8,128)(2,1)S(1)}, bf16[256,2560]{1,0:T(8,128)(2,1)S(1)}, u32[]{:S(2)}, u32[]{:S(2)}) %collective-permute-start.18) | collective-permute-done | bytes 1310752 | tf_op jit(solution)/shard_map/ppermute | solution.py:415
  238.7 22.8 %collective-permute-done.23 = bf16[4,160,384]{2,1,0:T(8,128)(2,1)S(1)} collective-permute-done((bf16[4,160,384]{2,1,0:T(8,128)(2,1)}, bf16[4,160,384]{2,1,0:T(8,128)(2,1)S(1)}, u32[]{:S(2)}, u32[]{:S(2)}) %collective-permute-start.23) | collective-permute-done | bytes 491552 | tf_op jit(solution)/shard_map/ppermute | solution.py:401
  329.6 19.1 %expert_pass.8 = (bf16[2048,2560]{1,0:T(8,128)(2,1)}, bf16[2048,2560]{1,0:T(8,128)(2,1)}, bf16[2048,768]{1,0:T(8,128)(2,1)}, bf16[2048,1536]{1,0:T(8,128)(2,1)},...) custom-call(s32[2]{0:T(128)S(1)} %pad_add_fusion.refs_0_, ...), custom_call_target="tpu_custom_call" | custom-call | flops 6710886400 | bytes 25165824 | tf_op jit(solution)/shard_map/expert_pass/pallas_call | solution.py:750
  374.2 19.0 %expert_pass.9 = (bf16[2048,2560]{1,0:T(8,128)(2,1)}, bf16[2048,2560]{1,0:T(8,128)(2,1)}, bf16[2048,768]{1,0:T(8,128)(2,1)}, bf16[2048,1536]{1,0:T(8,128)(2,1)},...) custom-call(s32[2]{0:T(128)S(1)} %pad_add_fusion.refs_0_, ...), custom_call_target="tpu_custom_call", output_to_operand_aliasing={{0}: (14, {}), {1}: (15, {}), {2}: (16, {}), {3}: (17, {}),... | custom-call | flops 6710886400 | bytes 25165824 | tf_op jit(solution)/shard_map/expert_pass/pallas_call | solution.py:750
  406.1 16.8 %expert_pass.10 = (bf16[2048,2560]{1,0:T(8,128)(2,1)}, bf16[2048,2560]{1,0:T(8,128)(2,1)}, bf16[2048,768]{1,0:T(8,128)(2,1)}, bf16[2048,1536]{1,0:T(8,128)(2,1)}...) custom-call(s32[2]{0:T(128)S(1)} %pad_add_fusion.refs_0_, ...), custom_call_target="tpu_custom_call", output_to_operand_aliasing={{0}: (14, {}), {1}: (15, {}), {2}: (16, {}), {3}: (17, {}),... | custom-call | flops 6710886400 | bytes 25165824 | tf_op jit(solution)/shard_map/expert_pass/pallas_call | solution.py:750
  430.8 16.4 %expert_pass.11 = (bf16[2048,2560]{1,0:T(8,128)(2,1)}, bf16[2048,2560]{1,0:T(8,128)(2,1)}, bf16[2048,768]{1,0:T(8,128)(2,1)}, bf16[2048,1536]{1,0:T(8,128)(2,1)}...) custom-call(s32[2]{0:T(128)S(1)} %pad_add_fusion.refs_0_, ...), custom_call_target="tpu_custom_call", output_to_operand_aliasing={{0}: (14, {}), {1}: (15, {}), {2}: (16, {}), {3}: (17, {}),... | custom-call | flops 6710886400 | bytes 25165824 | tf_op jit(solution)/shard_map/expert_pass/pallas_call | solution.py:750
  456.0 17.2 %expert_pass.12 = (bf16[2048,2560]{1,0:T(8,128)(2,1)}, bf16[2048,2560]{1,0:T(8,128)(2,1)}, bf16[2048,768]{1,0:T(8,128)(2,1)S(1)}, bf16[2048,1536]{1,0:T(8,128)(2...) custom-call(s32[2]{0:T(128)S(1)} %pad_add_fusion.refs_0_, ...), custom_call_target="tpu_custom_call", output_to_operand_aliasing={{0}: (14, {}), {1}: (15, {}), {2}: (16, {}), {3}: (17, {}),... | custom-call | flops 6710886400 | bytes 25165824 | tf_op jit(solution)/shard_map/expert_pass/pallas_call | solution.py:750
  484.2 15.7 %expert_pass.13 = (bf16[2048,2560]{1,0:T(8,128)(2,1)}, bf16[2048,2560]{1,0:T(8,128)(2,1)}, bf16[2048,768]{1,0:T(8,128)(2,1)}, bf16[2048,1536]{1,0:T(8,128)(2,1)}...) custom-call(s32[2]{0:T(128)S(1)} %pad_add_fusion.refs_0_, ...), custom_call_target="tpu_custom_call", output_to_operand_aliasing={{0}: (14, {}), {1}: (15, {}), {2}: (16, {}), {3}: (17, {}),... | custom-call | flops 6710886400 | bytes 25165824 | tf_op jit(solution)/shard_map/expert_pass/pallas_call | solution.py:750
  504.2 19.5 %expert_pass.14 = (bf16[2048,2560]{1,0:T(8,128)(2,1)}, bf16[2048,2560]{1,0:T(8,128)(2,1)}, bf16[2048,768]{1,0:T(8,128)(2,1)}, bf16[2048,1536]{1,0:T(8,128)(2,1)}...) custom-call(s32[2]{0:T(128)S(1)} %pad_add_fusion.refs_0_, ...), custom_call_target="tpu_custom_call", output_to_operand_aliasing={{0}: (14, {}), {1}: (15, {}), {2}: (16, {}), {3}: (17, {}),... | custom-call | flops 6710886400 | bytes 25165824 | tf_op jit(solution)/shard_map/expert_pass/pallas_call | solution.py:750
  526.8 15.5 %expert_pass.15 = (bf16[2048,2560]{1,0:T(8,128)(2,1)}, bf16[2048,2560]{1,0:T(8,128)(2,1)}, bf16[2048,768]{1,0:T(8,128)(2,1)}, bf16[2048,1536]{1,0:T(8,128)(2,1)}...) custom-call(s32[2]{0:T(128)S(1)} %pad_add_fusion.refs_0_, ...), custom_call_target="tpu_custom_call", output_to_operand_aliasing={{0}: (14, {}), {1}: (15, {}), {2}: (16, {}), {3}: (17, {}),... | custom-call | flops 6710886400 | bytes 25165824 | tf_op jit(solution)/shard_map/expert_pass/pallas_call | solution.py:750
  544.7 24.7 %expert_outputs.1 = (bf16[2048,2560]{1,0:T(8,128)(2,1)}, bf16[2048,2560]{1,0:T(8,128)(2,1)}) custom-call(f32[8,2,256]{2,1,0:T(2,128)S(1)} %get-tuple-element.1723.place_ref, f32[8,2,256]{2,1,0:T(2,128)S(1)} %get-tuple-element.1722.gate_ref, bf16[2048,768]{1,0:T(8,128)(2,1)S(1)} %copy-done.4, bf16[4096,384]{1,0:T(8,128)(2,1)} %get-tuple-element.1219.shared_ref, ...), custom_call_target="tpu_custom_call" | custom-call | flops 13421772800 | bytes 33554432 | tf_op jit(solution)/shard_map/expert_outputs/pallas_call | solution.py:815
  580.1 12.1 %convolution_convert_fusion.3 = bf16[2560,256]{1,0:T(8,128)(2,1)} fusion(bf16[4096,2560]{1,0:T(8,128)(2,1)} %get-tuple-element.1218, bf16[4096,384]{1,0:T(8,128)(2,1)} %get-tuple-element.1219.shared_ref), kind=kOutput, calls=%fused_computation.34 | convolution fusion | flops 5369364480 | bytes 24379392 | tf_op jit(solution)/shard_map/dot_general | solution.py:70
  670.1 10.9 %convolution_bitcast_fusion.2 = f32[1,768,2560]{2,1,0:T(8,128)} fusion(bf16[2048,768]{1,0:T(8,128)(2,1)S(1)} %copy-done.4, bf16[2048,2560]{1,0:T(8,128)(2,1)S(1)} %bitcast.253), kind=kOutput, calls=%fused_computation.15 | convolution fusion | flops 8053063680 | bytes 21495808 | tf_op jit(solution)/shard_map/dot_general | solution.py:70
  681.0 14.3 %collective-permute-done.79 = bf16[256,2560]{1,0:T(8,128)(2,1)} collective-permute-done((bf16[256,2560]{1,0:T(8,128)(2,1)S(1)}, bf16[256,2560]{1,0:T(8,128)(2,1)}, u32[]{:S(2)}, u32[]{:S(2)}) %collective-permute-start.79) | collective-permute-done | bytes 1310752 | tf_op jit(solution)/shard_map/ppermute | solution.py:401
  707.9 11.3 %convolution_bitcast_fusion.1 = f32[1,2560,768]{2,1,0:T(8,128)} fusion(bf16[2048,2560]{1,0:T(8,128)(2,1)S(1)} %bitcast.249, bf16[2048,1536]{1,0:T(8,128)(2,1)S(1)} %bitcast.255), kind=kOutput, calls=%fused_computation.14 | convolution fusion | flops 8053063680 | bytes 21495808 | tf_op jit(solution)/shard_map/dot_general | solution.py:70
  719.2 14.3 %collective-permute-done.84 = bf16[256,2560]{1,0:T(8,128)(2,1)S(1)} collective-permute-done((bf16[256,2560]{1,0:T(8,128)(2,1)S(1)}, bf16[256,2560]{1,0:T(8,128)(2,1)S(1)}, u32[]{:S(2)}, u32[]{:S(2)}) %collective-permute-start.84) | collective-permute-done | bytes 1310752 | tf_op jit(solution)/shard_map/ppermute | solution.py:401
  798.3 10.9 %convolution_bitcast_fusion = f32[1,2560,768]{2,1,0:T(8,128)} fusion(bf16[2048,2560]{1,0:T(8,128)(2,1)S(1)} %bitcast.251, bf16[2048,1536]{1,0:T(8,128)(2,1)S(1)} %bitcast.257), kind=kOutput, calls=%fused_computation.13 | convolution fusion | flops 8053063680 | bytes 21495808 | tf_op jit(solution)/shard_map/dot_general | solution.py:70
  809.2 17.3 %collective-permute-done.90 = bf16[256,2560]{1,0:T(8,128)(2,1)} collective-permute-done((bf16[256,2560]{1,0:T(8,128)(2,1)}, bf16[256,2560]{1,0:T(8,128)(2,1)}, u32[]{:S(2)}, u32[]{:S(2)}) %collective-permute-start.90) | collective-permute-done | bytes 1310752 | tf_op jit(solution)/shard_map/ppermute | solution.py:401
  836.2 10.6 %collective-permute-done.92 = bf16[4,160,384]{2,1,0:T(8,128)(2,1)S(1)} collective-permute-done((bf16[4,160,384]{2,1,0:T(8,128)(2,1)}, bf16[4,160,384]{2,1,0:T(8,128)(2,1)S(1)}, u32[]{:S(2)}, u32[]{:S(2)}) %collective-permute-start.92) | collective-permute-done | bytes 491552 | tf_op jit(solution)/shard_map/ppermute | solution.py:401
  852.6 19.7 %collective-permute-done.94 = bf16[128,2560]{1,0:T(8,128)(2,1)S(1)} collective-permute-done((bf16[128,2560]{1,0:T(8,128)(2,1)S(1)}, bf16[128,2560]{1,0:T(8,128)(2,1)S(1)}, u32[]{:S(2)}, u32[]{:S(2)}) %collective-permute-start.94) | collective-permute-done | bytes 655392 | tf_op jit(solution)/shard_map/ppermute | solution.py:401
  930.0 18.9 %collective-permute-done.102 = bf16[160,1664]{1,0:T(8,128)(2,1)S(1)} collective-permute-done((bf16[160,1664]{1,0:T(8,128)(2,1)S(1)}, bf16[160,1664]{1,0:T(8,128)(2,1)S(1)}, u32[]{:S(2)}, u32[]{:S(2)}) %collective-permute-start.102) | collective-permute-done | bytes 532512 | tf_op jit(solution)/shard_map/ppermute | solution.py:415
  (832 shorter events, 561.0 us)
Async XLA Ops:
  29.6 52.8 %collective-permute-start.5 = (bf16[272,2560]{1,0:T(8,128)(2,1)}, bf16[272,2560]{1,0:T(8,128)(2,1)}, u32[]{:S(2)}, u32[]{:S(2)}) collective-permute-start(bf16[272,2560]{1,0:T(8,128)(2,1)} %fusion.32), channel_id=1, source_target_pairs={{0,16},{2,18},{4,20},{6,22},{9,25},{11,27},{13,29},{15,31},{16,0},... | collective-permute-start | bytes 4177928 | tf_op jit(solution)/shard_map/ppermute | solution.py:415
  31.4 51.1 %collective-permute-start.6 = (bf16[272,2560]{1,0:T(8,128)(2,1)}, bf16[272,2560]{1,0:T(8,128)(2,1)}, u32[]{:S(2)}, u32[]{:S(2)}) collective-permute-start(bf16[272,2560]{1,0:T(8,128)(2,1)} %fusion.32), channel_id=1, source_target_pairs={{0,8},{2,10},{4,12},{6,14},{9,1},{11,3},{13,5},{15,7},{16,24},{18,... | collective-permute-start | bytes 4177928 | tf_op jit(solution)/shard_map/ppermute | solution.py:415
  82.4 35.2 %collective-permute-start.11 = (bf16[640,1664]{1,0:T(8,128)(2,1)S(1)}, bf16[640,1664]{1,0:T(8,128)(2,1)}, u32[]{:S(2)}, u32[]{:S(2)}) collective-permute-start(bf16[640,1664]{1,0:T(8,128)(2,1)S(1)} %pad_maximum_fusion.6), channel_id=1, source_target_pairs={{0,1},{1,0},{2,3},{3,2},{4,5},{5,4},{6,7},{7,6},{8,9},{9,8},{10,11... | collective-permute-start | bytes 6389768 | tf_op jit(solution)/shard_map/ppermute | solution.py:405
  121.5 59.1 %collective-permute-start.15 = (bf16[256,2560]{1,0:T(8,128)(2,1)}, bf16[256,2560]{1,0:T(8,128)(2,1)}, u32[]{:S(2)}, u32[]{:S(2)}) collective-permute-start(bf16[256,2560]{1,0:T(8,128)(2,1)} %maximum_select_fusion.2), channel_id=1, source_target_pairs={{0,16},{1,9},{2,18},{3,11},{4,20},{5,13},{6,22},{7,15},{8,24},{9,1... | collective-permute-start | bytes 3932168 | tf_op jit(solution)/shard_map/ppermute | solution.py:415
  128.5 52.1 %collective-permute-start.16 = (bf16[4,160,384]{2,1,0:T(8,128)(2,1)}, bf16[4,160,384]{2,1,0:T(8,128)(2,1)}, u32[]{:S(2)}, u32[]{:S(2)}) collective-permute-start(bf16[4,160,384]{2,1,0:T(8,128)(2,1)} %pad_maximum_fusion.27), channel_id=1, source_target_pairs={{0,16},{2,18},{4,20},{6,22},{8,24},{10,26},{12,28},{14,30},{16,0},... | collective-permute-start | bytes 1474568 | tf_op jit(solution)/shard_map/ppermute | solution.py:401
  186.5 40.9 %collective-permute-start.18 = (bf16[256,2560]{1,0:T(8,128)(2,1)S(1)}, bf16[256,2560]{1,0:T(8,128)(2,1)S(1)}, u32[]{:S(2)}, u32[]{:S(2)}) collective-permute-start(bf16[256,2560]{1,0:T(8,128)(2,1)S(1)} %get-tuple-element.1604), channel_id=1, source_target_pairs={{1,9},{3,11},{5,13},{7,15},{8,0},{10,2},{12,4},{14,6},{17,25},{19,... | collective-permute-start | bytes 3932168 | tf_op jit(solution)/shard_map/ppermute | solution.py:415
  264.9 39.9 %collective-permute-start.25 = (bf16[512,2560]{1,0:T(8,128)(2,1)}, bf16[512,2560]{1,0:T(8,128)(2,1)}, u32[]{:S(2)}, u32[]{:S(2)}) collective-permute-start(bf16[512,2560]{1,0:T(8,128)(2,1)} %maximum_select_fusion.refs_5_.refs_7_), channel_id=1, source_target_pairs={{0,4},{1,3},{2,6},{3,1},{4,0},{5,7},{6,2},{7,5},{8,12},{9,11},{10,... | collective-permute-start | bytes 7864328 | tf_op jit(solution)/shard_map/ppermute | solution.py:415
  281.3 33.7 %collective-permute-start.28 = (bf16[144,2560]{1,0:T(8,128)(2,1)S(1)}, bf16[144,2560]{1,0:T(8,128)(2,1)}, u32[]{:S(2)}, u32[]{:S(2)}) collective-permute-start(bf16[144,2560]{1,0:T(8,128)(2,1)S(1)} %pad_maximum_fusion.19.refs_1_), channel_id=1, source_target_pairs={{0,8},{2,10},{4,12},{6,14},{8,0},{10,2},{12,4},{14,6},{16,24},{18,... | collective-permute-start | bytes 2211848 | tf_op jit(solution)/shard_map/ppermute | solution.py:401
  319.8 43.5 %collective-permute-start.36 = (bf16[512,2560]{1,0:T(8,128)(2,1)S(1)}, bf16[512,2560]{1,0:T(8,128)(2,1)S(1)}, u32[]{:S(2)}, u32[]{:S(2)}) collective-permute-start(bf16[512,2560]{1,0:T(8,128)(2,1)S(1)} %copy-done.8), channel_id=1, source_target_pairs={{0,1},{1,0},{2,3},{3,2},{4,5},{5,4},{6,7},{7,6},{8,9},{9,8},{10,11... | collective-permute-start | bytes 7864328 | tf_op jit(solution)/shard_map/ppermute | solution.py:405
  321.6 33.7 %collective-permute-start.31 = (bf16[256,2560]{1,0:T(8,128)(2,1)}, bf16[256,2560]{1,0:T(8,128)(2,1)S(1)}, u32[]{:S(2)}, u32[]{:S(2)}) collective-permute-start(bf16[256,2560]{1,0:T(8,128)(2,1)} %get-tuple-element.1600), channel_id=1, source_target_pairs={{0,4},{1,3},{2,6},{3,1},{4,0},{5,7},{6,2},{7,5},{8,12},{9,11},{10,... | collective-permute-start | bytes 3932168 | tf_op jit(solution)/shard_map/ppermute | solution.py:415
  356.2 37.1 %collective-permute-start.35 = (bf16[256,2560]{1,0:T(8,128)(2,1)S(1)}, bf16[256,2560]{1,0:T(8,128)(2,1)}, u32[]{:S(2)}, u32[]{:S(2)}) collective-permute-start(bf16[256,2560]{1,0:T(8,128)(2,1)S(1)} %get-tuple-element.874), channel_id=1, source_target_pairs={{0,1},{1,0},{2,3},{3,2},{4,5},{5,4},{6,7},{7,6},{8,9},{9,8},{10,11... | collective-permute-start | bytes 3932168 | tf_op jit(solution)/shard_map/ppermute | solution.py:405
  357.7 48.3 %collective-permute-start.42 = (bf16[432,2560]{1,0:T(8,128)(2,1)}, bf16[432,2560]{1,0:T(8,128)(2,1)S(1)}, u32[]{:S(2)}, u32[]{:S(2)}) collective-permute-start(bf16[432,2560]{1,0:T(8,128)(2,1)} %pad_maximum_fusion.2), channel_id=1, source_target_pairs={{0,1},{1,0},{2,3},{3,2},{4,5},{5,4},{6,7},{7,6},{8,9},{9,8},{10,11... | collective-permute-start | bytes 6635528 | tf_op jit(solution)/shard_map/ppermute | solution.py:405
  358.2 35.0 %collective-permute-start.39 = (bf16[144,2560]{1,0:T(8,128)(2,1)S(1)}, bf16[144,2560]{1,0:T(8,128)(2,1)S(1)}, u32[]{:S(2)}, u32[]{:S(2)}) collective-permute-start(bf16[144,2560]{1,0:T(8,128)(2,1)S(1)} %collective-permute-done.27.refs_1_), channel_id=1, source_target_pairs={{0,8},{2,10},{4,12},{6,14},{8,0},{10,2},{12,4},{14,6},{16,24},{18,... | collective-permute-start | bytes 2211848 | tf_op jit(solution)/shard_map/ppermute | solution.py:401
  577.7 39.7 %collective-permute-start.72 = (bf16[2048,2560]{1,0:T(8,128)(2,1)}, bf16[2048,2560]{1,0:T(8,128)(2,1)}, u32[]{:S(2)}, u32[]{:S(2)}) collective-permute-start(bf16[2048,2560]{1,0:T(8,128)(2,1)} %get-tuple-element.1242), channel_id=1, source_target_pairs={{0,1},{1,0},{2,3},{3,2},{4,5},{5,4},{6,7},{7,6},{8,9},{9,8},{10,11... | collective-permute-start | bytes 31457288 | tf_op jit(solution)/shard_map/ppermute | solution.py:405
  577.8 34.8 %collective-permute-start.69 = (bf16[128,2560]{1,0:T(8,128)(2,1)}, bf16[128,2560]{1,0:T(8,128)(2,1)}, u32[]{:S(2)}, u32[]{:S(2)}) collective-permute-start(bf16[128,2560]{1,0:T(8,128)(2,1)} %get-tuple-element.1215), channel_id=1, source_target_pairs={{0,16},{2,18},{4,20},{6,22},{8,24},{10,26},{12,28},{14,30},{16,0},... | collective-permute-start | bytes 1966088 | tf_op jit(solution)/shard_map/ppermute | solution.py:401
  579.0 33.5 %collective-permute-start.70 = (bf16[256,2560]{1,0:T(8,128)(2,1)}, bf16[256,2560]{1,0:T(8,128)(2,1)}, u32[]{:S(2)}, u32[]{:S(2)}) collective-permute-start(bf16[256,2560]{1,0:T(8,128)(2,1)} %pad_maximum_fusion.9), channel_id=1, source_target_pairs={{0,2},{2,0},{4,6},{6,4},{8,10},{10,8},{12,14},{14,12},{16,18},{18,... | collective-permute-start | bytes 3932168 | tf_op jit(solution)/shard_map/ppermute | solution.py:401
  666.7 33.4 %collective-permute-start.81 = (bf16[256,2560]{1,0:T(8,128)(2,1)}, bf16[256,2560]{1,0:T(8,128)(2,1)}, u32[]{:S(2)}, u32[]{:S(2)}) collective-permute-start(bf16[256,2560]{1,0:T(8,128)(2,1)} %maximum_select_fusion.4), channel_id=1, source_target_pairs={{0,16},{2,18},{4,20},{6,22},{9,25},{11,27},{13,29},{15,31},{16,0},... | collective-permute-start | bytes 3932168 | tf_op jit(solution)/shard_map/ppermute | solution.py:415
  701.2 37.4 %collective-permute-start.83 = (bf16[256,2560]{1,0:T(8,128)(2,1)}, bf16[256,2560]{1,0:T(8,128)(2,1)S(1)}, u32[]{:S(2)}, u32[]{:S(2)}) collective-permute-start(bf16[256,2560]{1,0:T(8,128)(2,1)} %collective-permute-done.81), channel_id=1, source_target_pairs={{0,8},{2,10},{4,12},{6,14},{9,1},{11,3},{13,5},{15,7},{16,24},{18,... | collective-permute-start | bytes 3932168 | tf_op jit(solution)/shard_map/ppermute | solution.py:415
  704.8 33.7 %collective-permute-start.86 = (bf16[4,160,384]{2,1,0:T(8,128)(2,1)}, bf16[4,160,384]{2,1,0:T(8,128)(2,1)S(1)}, u32[]{:S(2)}, u32[]{:S(2)}) collective-permute-start(bf16[4,160,384]{2,1,0:T(8,128)(2,1)} %pad_maximum_fusion.33), channel_id=1, source_target_pairs={{0,8},{2,10},{4,12},{6,14},{8,0},{10,2},{12,4},{14,6},{16,24},{18,... | collective-permute-start | bytes 1474568 | tf_op jit(solution)/shard_map/ppermute | solution.py:401
  778.2 53.5 %collective-permute-start.91 = (bf16[256,2560]{1,0:T(8,128)(2,1)}, bf16[256,2560]{1,0:T(8,128)(2,1)}, u32[]{:S(2)}, u32[]{:S(2)}) collective-permute-start(bf16[256,2560]{1,0:T(8,128)(2,1)} %get-tuple-element.1595), channel_id=1, source_target_pairs={{1,9},{3,11},{5,13},{7,15},{8,0},{10,2},{12,4},{14,6},{17,25},{19,... | collective-permute-start | bytes 3932168 | tf_op jit(solution)/shard_map/ppermute | solution.py:415
  784.1 47.5 %collective-permute-start.88 = (bf16[256,2560]{1,0:T(8,128)(2,1)}, bf16[256,2560]{1,0:T(8,128)(2,1)}, u32[]{:S(2)}, u32[]{:S(2)}) collective-permute-start(bf16[256,2560]{1,0:T(8,128)(2,1)} %get-tuple-element.1596), channel_id=1, source_target_pairs={{1,9},{3,11},{5,13},{7,15},{8,0},{10,2},{12,4},{14,6},{17,25},{19,... | collective-permute-start | bytes 3932168 | tf_op jit(solution)/shard_map/ppermute | solution.py:415
  793.9 41.1 %collective-permute-start.93 = (bf16[1280,1664]{1,0:T(8,128)(2,1)}, bf16[1280,1664]{1,0:T(8,128)(2,1)S(1)}, u32[]{:S(2)}, u32[]{:S(2)}) collective-permute-start(bf16[1280,1664]{1,0:T(8,128)(2,1)} %get-tuple-element.1573), channel_id=1, source_target_pairs={{0,1},{1,0},{2,3},{3,2},{4,5},{5,4},{6,7},{7,6},{8,9},{9,8},{10,11... | collective-permute-start | bytes 12779528 | tf_op jit(solution)/shard_map/ppermute | solution.py:405
  879.7 41.1 %collective-permute-start.97 = (f32[128,2560]{1,0:T(8,128)}, f32[128,2560]{1,0:T(8,128)}, u32[]{:S(2)}, u32[]{:S(2)}) collective-permute-start(f32[128,2560]{1,0:T(8,128)} %constant_dynamic-slice_fusion), channel_id=1, source_target_pairs={{0,1},{2,3},{4,5},{6,7},{9,8},{11,10},{13,12},{15,14},{16,17},{18,... | collective-permute-start | bytes 3932168 | tf_op jit(solution)/shard_map/ppermute | solution.py:415
  881.1 32.7 %collective-permute-start.99 = (bf16[128,2560]{1,0:T(8,128)(2,1)}, bf16[128,2560]{1,0:T(8,128)(2,1)}, u32[]{:S(2)}, u32[]{:S(2)}) collective-permute-start(bf16[128,2560]{1,0:T(8,128)(2,1)} %get-tuple-element.1451), channel_id=1, source_target_pairs={{0,8},{2,10},{4,12},{6,14},{8,0},{10,2},{12,4},{14,6},{16,24},{18,... | collective-permute-start | bytes 1966088 | tf_op jit(solution)/shard_map/ppermute | solution.py:401
  (243 other events, 3996.9 us)
